TPU v7x, 256 devices: a whole 4x4x8 slice. The times are simulated.
256 devices in a mesh: mem: 8 (over z), dom: 32 (over y, x, core).
Axes of the slice: x: 4, y: 4, z: 8, core: 2. Of those that a mesh axis runs over, the one named last changes fastest.
Arguments:
- ensemble: float32 [80, 131072], P('mem', 'dom'), may hold values from -6 to 6
- obs_index: int32 [4, 4, 1024], replicated, may hold values from 0 to 131071
- obs_weight: float32 [4, 4, 1024], replicated, may hold values from 0.1 to 0.6
- obs_value: float32 [4, 1024], replicated, may hold values from -6 to 6
- obs_error_var: float32 [4, 1024], replicated, may hold values from 0.25 to 4
- loc_class: int32 [1024, 32], P(('dom', 'mem')), may hold values from 0 to 4
Outputs:
- posterior: float32 [80, 131072], P(None, ('dom', 'mem'))
All inputs are finite; a program needn't handle non-finite values.
Results may differ from a plain program's by a relative error of at most 0.0085.
Values may be sent and summed in bfloat16 or wider, within the bound.
No kernel may reach another device: no remote copies, remote signals or barrier semaphores. Data moves between devices by JAX's collectives and lax.ppermute only.
A program may use at most 64 MiB of HBM per device.

v0:
```python
import jax
import jax.numpy as jnp
from jax import lax
from jax.sharding import PartitionSpec as P

EPS = 1e-05
LOC_TABLE = (1.0, 0.6848958, 0.2083333, 0.0164931, 0.0)
span_width = 512


def class_weights(classes):
    weights = jnp.zeros(classes.shape, jnp.float32)
    for level, value in enumerate(LOC_TABLE):
        weights = weights + jnp.where(classes == level, jnp.float32(value), jnp.float32(0.0))
    return weights


def adjust(prior, value, errvar):
    count = prior.shape[0]
    mean = jnp.mean(prior, axis=0)
    anom = prior - mean
    var = jnp.sum(anom * anom, axis=0) / (count - 1)
    inverse = 1.0 / (var + EPS)
    post_var = 1.0 / (inverse + 1.0 / errvar)
    post_mean = post_var * (mean * inverse + value / errvar)
    shrink = jnp.sqrt(errvar / (errvar + var))
    incr = post_mean - mean + (shrink - 1.0) * anom
    return (anom, incr, inverse)


def update_block(block, classes, anom_b, incr_b, inverse):
    count = block.shape[0]
    centered = (block - jnp.mean(block, axis=0)).astype(jnp.bfloat16)
    cov = lax.dot_general(
        centered, anom_b, (((0,), (0,)), ((), ())), preferred_element_type=jnp.float32
    ) / (count - 1)
    weights = class_weights(classes)
    row_blocks, col_blocks = classes.shape
    scaled = (cov * inverse).reshape(
        row_blocks, cov.shape[0] // row_blocks, col_blocks, cov.shape[1] // col_blocks
    )
    gain = (scaled * weights[:, None, :, None]).reshape(cov.shape).astype(jnp.bfloat16)
    delta = lax.dot_general(
        incr_b, gain, (((1,), (1,)), ((), ())), preferred_element_type=jnp.float32
    )
    return block + delta


def local_prior(states, first, index, weight):
    width = states.shape[1]
    total = jnp.zeros((states.shape[0], index.shape[1]), jnp.float32)
    for point in range(index.shape[0]):
        local = index[point] - first
        valid = (local >= 0) & (local < width)
        safe = jnp.where(valid, local, 0)
        picked = states[:, safe]
        total = total + jnp.where(valid[None], picked * weight[point][None], jnp.float32(0.0))
    return total


def per_device(ensemble, obs_index, obs_weight, obs_value, obs_error_var, loc_class):
    batches = obs_index.shape[0]
    ready = 0
    early = None
    states = lax.all_to_all(ensemble, "mem", split_axis=1, concat_axis=0, tiled=True)
    members, width = states.shape
    start = (lax.axis_index("dom") * lax.axis_size("mem") + lax.axis_index("mem")) * width
    blocks = states.reshape(members, width // span_width, span_width).transpose(1, 0, 2)
    obs_blocks = loc_class.shape[1] // batches
    rows_each = span_width // (width // loc_class.shape[0])
    for batch in range(batches):
        current = blocks.transpose(1, 0, 2).reshape(members, width)
        partial_value = local_prior(current, start, obs_index[batch], obs_weight[batch])
        prior = lax.psum(partial_value, ("mem", "dom"))
        anom, incr, inverse = adjust(prior, obs_value[batch], obs_error_var[batch])
        anom_b = anom.astype(jnp.bfloat16)
        incr_b = incr.astype(jnp.bfloat16)
        classes = loc_class[:, batch * obs_blocks : (batch + 1) * obs_blocks]
        classes = classes.reshape(width // span_width, rows_each, obs_blocks)

        def step(pair):
            return update_block(pair[0], pair[1], anom_b, incr_b, inverse)

        blocks = lax.map(step, (blocks, classes))
    return blocks.transpose(1, 0, 2).reshape(members, width)


def solution(mesh):
    in_specs = (P("mem", "dom"), P(), P(), P(), P(), P(("dom", "mem"), None))
    out_specs = P(None, ("dom", "mem"))
    return jax.shard_map(
        per_device, mesh=mesh, in_specs=in_specs, out_specs=out_specs, check_vma=False
    )
```

profile of v0, /device:TPU:1, one launch (start us, length us, event | category | flops | bytes accessed | tf_op | source)
XLA Modules:
  0.0 1109.5 jit_solution(13231728230315594404)
XLA Ops:
  8.5 9.0 all-to-all-start
  20.2 7.7 all-to-all-done
  28.0 2.8 gather_fusion
  30.9 2.8 gather_fusion.1
  33.7 2.8 gather_fusion.2
  36.5 2.8 gather_fusion.3
  39.3 2.4 add_bitcast_fusion.3
  41.9 248.7 %all-reduce.5.cloned.1.call-done = f32[80,1024]{0,1:T(8,128)} async-done(((f32[80,1024]{0,1:T(8,128)}), f32[80,1024]{0,1:T(8,128)}) %all-reduce.5.cloned.1.call-update) | async-done | bytes 327696 | tf_op jit(solution)/shard_map/psum | solution.py:74
  291.8 1.4 multiply_reduce_fusion.3
  295.1 2.8 gather_fusion.4
  297.9 2.8 gather_fusion.5
  300.7 2.8 gather_fusion.6
  303.5 2.8 gather_fusion.7
  306.3 2.4 add_bitcast_fusion.2
  308.8 250.9 %all-reduce.7.cloned.1.call-done = f32[80,1024]{0,1:T(8,128)} async-done(((f32[80,1024]{0,1:T(8,128)}), f32[80,1024]{0,1:T(8,128)}) %all-reduce.7.cloned.1.call-update) | async-done | bytes 327696 | tf_op jit(solution)/shard_map/psum | solution.py:74
  561.1 1.4 multiply_reduce_fusion.2
  562.8 1.4 fusion.46
  564.3 2.8 gather_fusion.10
  567.1 2.8 gather_fusion.11
  569.9 2.8 gather_fusion.8
  572.7 2.8 gather_fusion.9
  575.5 2.4 add_bitcast_fusion.1
  578.2 250.5 %all-reduce.9.cloned.1.call-done = f32[80,1024]{0,1:T(8,128)} async-done(((f32[80,1024]{0,1:T(8,128)}), f32[80,1024]{0,1:T(8,128)}) %all-reduce.9.cloned.1.call-update) | async-done | bytes 327696 | tf_op jit(solution)/shard_map/psum | solution.py:74
  830.0 1.4 multiply_reduce_fusion.1
  833.3 2.8 gather_fusion.12
  836.1 2.8 gather_fusion.13
  838.9 2.8 gather_fusion.14
  841.7 2.8 gather_fusion.15
  844.5 2.4 add_bitcast_fusion
  847.0 250.9 %all-reduce.11.cloned.1.call-done = f32[80,1024]{0,1:T(8,128)} async-done(((f32[80,1024]{0,1:T(8,128)}), f32[80,1024]{0,1:T(8,128)}) %all-reduce.11.cloned.1.call-update) | async-done | bytes 327696 | tf_op jit(solution)/shard_map/psum | solution.py:74
  1099.2 1.4 multiply_reduce_fusion
  1100.9 2.0 fusion.8
  (79 shorter events, 14.5 us)
Async XLA Ops:
  6.5 13.3 %copy-start.4 = (s32[4,4,1024]{2,1,0:T(4,128)S(1)}, s32[4,4,1024]{2,1,0:T(4,128)}, u32[]{:S(2)}) copy-start(s32[4,4,1024]{2,1,0:T(4,128)} %param.7) | copy-start | bytes 196612
  6.5 13.6 %copy-start.5 = (f32[4,4,1024]{2,1,0:T(4,128)S(1)}, f32[4,4,1024]{2,1,0:T(4,128)}, u32[]{:S(2)}) copy-start(f32[4,4,1024]{2,1,0:T(4,128)} %param.8) | copy-start | bytes 196612
  8.5 19.4 %all-to-all-start = ((f32[10,8,512]{2,0,1:T(8,128)}), f32[10,8,512]{2,0,1:T(8,128)S(1)}, u32[]{:S(2)}, u32[]{:S(2)}) async-start(f32[10,8,512]{2,0,1:T(8,128)} %copy.24), calls=%async_computation | async-start | bytes 524288 | tf_op jit(solution)/shard_map/all_to_all | solution.py:65
  17.5 273.0 %all-reduce.5.cloned.1.call-start = ((), (), s32[]{:S(2)}) async-start(), calls=%async_computation.1 | async-start | bytes 1048576 | tf_op jit(solution)/shard_map/psum | solution.py:74
  39.3 254.0 %copy-start.6 = (f32[4,1024]{1,0:T(4,128)S(1)}, f32[4,1024]{1,0:T(4,128)}, u32[]{:S(2)}) copy-start(f32[4,1024]{1,0:T(4,128)} %param.9) | copy-start | bytes 49156
  39.3 254.0 %copy-start.7 = (f32[4,1024]{1,0:T(4,128)S(1)}, f32[4,1024]{1,0:T(4,128)}, u32[]{:S(2)}) copy-start(f32[4,1024]{1,0:T(4,128)} %param.10) | copy-start | bytes 49156
  41.8 518.0 %all-reduce.7.cloned.1.call-start = ((), (), s32[]{:S(2)}) async-start(), calls=%async_computation.2 | async-start | bytes 1048576 | tf_op jit(solution)/shard_map/psum | solution.py:74
  290.5 3.0 copy-start
  308.8 519.9 %all-reduce.9.cloned.1.call-start = ((), (), s32[]{:S(2)}) async-start(), calls=%async_computation.3 | async-start | bytes 1048576 | tf_op jit(solution)/shard_map/psum | solution.py:74
  559.7 3.0 copy-start.1
  578.0 519.9 %all-reduce.11.cloned.1.call-start = ((), (), s32[]{:S(2)}) async-start(), calls=%async_computation.4 | async-start | bytes 1048576 | tf_op jit(solution)/shard_map/psum | solution.py:74
  828.7 3.0 copy-start.2
  1097.9 3.0 copy-start.3
Sparse Core Ops, SparseCore 0:
  41.9 248.5 all-reduce.4
  308.9 250.7 all-reduce.6
  578.1 250.5 all-reduce.8
  847.1 250.7 all-reduce.10
where the time goes:
time: 1110 us
  waiting for transfers between devices  1010 us (91%)
  local copies, waits for them, and re-layouts  48.3 us (4%)
  other arithmetic  23.2 us (2%)
  between operations  13.7 us (1%)
    psum x4, waiting for transfers between devices, per_device(): prior = lax.psum(partial_value, ('mem', 'dom'))  1000 us
    gather x16, local copies, waits for them, and re-layouts, local_prior(): picked = states[:, safe]  44.9 us
  transfers between devices with their start and end apart: 5, of which 5 were waited for; matrix products, arithmetic and copies ran while one was open for 0% of the time, Pallas kernels for 0%

commit v1 on v0

v1 whole, which is shorter than its diff:
```python
import jax
import jax.numpy as jnp
from jax import lax
from jax.experimental import pallas as pl
from jax.experimental.pallas import tpu as pltpu
from jax.sharding import Mesh, PartitionSpec as P

EPS = 1e-05
LOC_TABLE = (1.0, 0.6848958, 0.2083333, 0.0164931, 0.0)
F32 = jnp.float32
BF16 = jnp.bfloat16
VMEM = pl.BlockSpec(memory_space=pltpu.VMEM)
SMEM = pl.BlockSpec(memory_space=pltpu.SMEM)

CHUNK = 168
PACK = 192


def call(body, shapes, args, scalars, scratch=(), flops=0, name=None):
    outs = [jax.ShapeDtypeStruct(s, d) for s, d in shapes]
    moved = sum(a.size * a.dtype.itemsize for a in args) + sum(o.size * o.dtype.itemsize for o in outs)
    made = pl.pallas_call(
        body,
        out_shape=outs,
        in_specs=[SMEM] * len(scalars) + [VMEM] * len(args),
        out_specs=[VMEM] * len(outs),
        scratch_shapes=list(scratch),
        compiler_params=pltpu.CompilerParams(vmem_limit_bytes=40 * 2**20),
        cost_estimate=pl.CostEstimate(flops=flops, bytes_accessed=moved, transcendentals=0),
        name=name,
    )(*scalars, *args)
    return list(made)


def lanes(info_ref):
    return pl.ds(pl.multiple_of(info_ref[1] * 128, 128), 128)


def pick(info_ref, shifts, core, index_ref, ext_ref, tile, start_ref, out_refs):
    first = info_ref[0]

    def group(n, carry):
        by = shifts + n
        block = lax.rem(info_ref[3] + by, 4) * 2 + core
        here = pl.ds(pl.multiple_of(block * 128, 128), 128)
        for k in range(4):
            local = [index_ref[b, k : k + 1, here] - first for b in range(4)]
            tail = jnp.concatenate([jnp.broadcast_to(v, (2, 128)) for v in local], axis=0)
            wide = [jnp.broadcast_to(v, (8, 128)) for v in local] + [tail]
            for b in range(5):
                low = wide[b] & 127
                high = wide[b] >> 7
                top = 0 if b < 4 else 8
                rows = slice(40 * k + 8 * b, 40 * k + 8 * b + 8)
                acc = jnp.zeros((8, 128), F32) if start_ref is None else start_ref[lax.rem(by, 4), rows, :]
                for part in range(32):
                    source = ext_ref[top : top + 8, part * 128 : (part + 1) * 128]
                    got = jnp.take_along_axis(source, low, axis=1)
                    acc = jnp.where(high == part, got, acc)
                out_refs[n, rows, :] = acc
        rest = tile if start_ref is None else tile + start_ref[lax.rem(by, 4), 160:168, :]
        out_refs[n, 160:168, :] = rest
        return carry

    lax.fori_loop(0, out_refs.shape[0], group, 0)


def collect_other(info_ref, index_ref, ens_ref, class_ref, out_ref, ext_ref, tile_ref, row_ref):
    ext_ref[0:8, :] = ens_ref[0:8, :]
    for r in range(4):
        ext_ref[8 + 2 * r : 10 + 2 * r, :] = ens_ref[8:10, :]
    even = lax.broadcasted_iota(jnp.int32, (32, 16), 0) == 2 * lax.broadcasted_iota(jnp.int32, (32, 16), 1)
    odd = lax.broadcasted_iota(jnp.int32, (32, 16), 0) == 2 * lax.broadcasted_iota(jnp.int32, (32, 16), 1) + 1
    mix = jnp.where(even, 1.0, jnp.where(odd, 8.0, 0.0)).astype(BF16)
    pairs = jnp.dot(class_ref[...].astype(F32).astype(BF16), mix, preferred_element_type=F32)
    for half in range(2):
        for i in range(4):
            row_ref[0:1, 64 * half + 16 * i : 64 * half + 16 * i + 16] = pairs[i : i + 1, :]
    row = lax.broadcasted_iota(jnp.int32, (8, 128), 0) == (info_ref[2] & 1) * 4 + info_ref[3]
    lane = (lax.broadcasted_iota(jnp.int32, (8, 128), 1) >> 6) == info_ref[4]
    tile = jnp.where(row & lane, jnp.broadcast_to(row_ref[...], (8, 128)), 0.0)
    tile_ref[...] = tile
    pick(info_ref, 0, 1 - info_ref[4], index_ref, ext_ref, tile, None, out_ref)


def collect_own(info_ref, index_ref, ext_ref, tile_ref, out_ref):
    pick(info_ref, 1, info_ref[4], index_ref, ext_ref, tile_ref[...], None, out_ref)


def collect_rest(info_ref, index_ref, ext_ref, tile_ref, start_ref, p0_ref, p3_ref, work_ref):
    pick(info_ref, 3, info_ref[4], index_ref, ext_ref, tile_ref[...], start_ref, work_ref)
    p3_ref[...] = work_ref[0]
    p0_ref[...] = work_ref[1]


def add_cores(own_ref, other_ref, p1_ref, p2_ref):
    p1_ref[...] = own_ref[0] + other_ref[1]
    p2_ref[...] = own_ref[1] + other_ref[2]


def add_columns(p0_ref, p1_ref, p2_ref, p3_ref, out_ref):
    out_ref[...] = (p0_ref[...] + p1_ref[...]) + (p2_ref[...] + p3_ref[...])


def add_rows(info_ref, weight_ref, ext_ref, p0_ref, p1_ref, p2_ref, p3_ref, out_ref, sum_ref):
    parts = [p0_ref, p1_ref, p2_ref, p3_ref]
    sum_ref[...] = (p0_ref[0:160, :] + p1_ref[0:160, :]) + (p2_ref[0:160, :] + p3_ref[0:160, :])
    here = lanes(info_ref)
    head = jnp.zeros((8, 128), F32)
    tail = jnp.zeros((2, 128), F32)
    for k in range(4):
        weight = weight_ref[0, k : k + 1, here]
        head = head + sum_ref[40 * k : 40 * k + 8, :] * weight
        tail = tail + sum_ref[40 * k + 32 : 40 * k + 34, :] * weight
    classes = [jnp.zeros((8, 128), F32)] * 2
    for s in range(4):
        upper = lax.rem(info_ref[2] - s + 4, 4) >> 1
        for t in range(2):
            classes[t] = classes[t] + jnp.where(upper == t, parts[s][160:168, :], 0.0)
    pair = lax.broadcasted_iota(jnp.int32, (8, 128), 0) >> 1
    for z in range(8):
        for k in range(4):
            out_ref[z, 24 * k : 24 * k + 24, :] = sum_ref[40 * k + 8 : 40 * k + 32, :]
            out_ref[z, 104 + 6 * k : 110 + 6 * k, :] = sum_ref[40 * k + 34 : 40 * k + 40, :]
        out_ref[z, 96:104, :] = head
        out_ref[z, 128:136, :] = jnp.zeros((8, 128), F32)
        out_ref[z, 128:130, :] = tail
        last = jnp.zeros((8, 128), F32)
        for i in range(4):
            at = slice(512 * z + 128 * i, 512 * z + 128 * i + 128)
            out_ref[z, 136 + 8 * i : 144 + 8 * i, :] = ext_ref[0:8, at]
            last = jnp.where(pair == i, ext_ref[8:16, at], last)
        out_ref[z, 168:176, :] = last
        for t in range(2):
            out_ref[z, 176 + 8 * t : 184 + 8 * t, :] = classes[t]


def increments(prior, value, errvar, out_ref, wide_ref):
    mean = jnp.mean(prior, axis=0, keepdims=True)
    anom = prior - mean
    var = jnp.sum(anom * anom, axis=0, keepdims=True) / 79.0
    inverse = 1.0 / (var + EPS)
    post_var = 1.0 / (inverse + 1.0 / errvar)
    post_mean = post_var * (mean * inverse + value / errvar)
    shrink = jnp.sqrt(errvar / (errvar + var))
    incr = post_mean - mean + (shrink - 1.0) * anom
    rest = inverse / 79.0
    wide_ref[0:80, :] = anom.astype(BF16).astype(F32)
    wide_ref[80:128, :] = jnp.zeros((48, 128), F32)
    for row in (80, 81, 82):
        part = rest.astype(BF16).astype(F32)
        wide_ref[row : row + 1, :] = part
        rest = rest - part
    out_ref[0:128, :] = jnp.transpose(wide_ref[...]).astype(BF16)
    out_ref[128:208, :] = incr.astype(BF16)


def first_batch(info_ref, pack_ref, value_ref, errvar_ref, out_ref, prior_ref, wide_ref):
    for z in range(8):
        prior_ref[8 * z : 8 * z + 8, :] = pack_ref[z, 96:104, :]
        prior_ref[64 + 2 * z : 66 + 2 * z, :] = pack_ref[z, 128:130, :]
    here = lanes(info_ref)
    increments(prior_ref[...], value_ref[0:1, here], errvar_ref[0:1, here], out_ref, wide_ref)


def center(x, out_ref):
    out_ref[0:80, :] = (x - jnp.mean(x, axis=0, keepdims=True)).astype(BF16)
    out_ref[80:128, :] = jnp.zeros((48, x.shape[1]), BF16)


def unpack(info_ref, pack_ref, index_ref, *refs):
    outs, centered, loc_ref = refs[:4], refs[4:8], refs[8]
    here = lanes(info_ref)
    table = pack_ref[:, 176:192, :].reshape(128, 128).astype(BF16)
    for b in range(4):
        for k in range(4):
            at = slice(128 * k, 128 * k + 128)
            for z in range(8):
                if b < 3:
                    outs[b][8 * z : 8 * z + 8, at] = pack_ref[z, 24 * k + 8 * b : 24 * k + 8 * b + 8, :]
                    outs[b][64 + 2 * z : 66 + 2 * z, at] = pack_ref[z, 104 + 6 * k + 2 * b : 106 + 6 * k + 2 * b, :]
                else:
                    outs[b][8 * z : 8 * z + 8, at] = pack_ref[z, 136 + 8 * k : 144 + 8 * k, :]
                    outs[b][64 + 2 * z : 66 + 2 * z, at] = pack_ref[z, 168 + 2 * k : 170 + 2 * k, :]
            if b < 3:
                block = index_ref[b + 1, k : k + 1, here] >> 7
            else:
                block = jnp.full((1, 128), info_ref[5] + k, jnp.int32)
            holder = ((block >> 2) & 7) * 16 + (block >> 6)
            own = (lax.broadcasted_iota(jnp.int32, (128, 128), 0) == holder).astype(F32).astype(BF16)
            found = lax.dot_general(table, own, (((0,), (0,)), ((), ())), preferred_element_type=F32)
            which = ((block >> 5) & 1) * 4 + (block & 3)
            pairs = jnp.zeros((16, 128), F32)
            for i in range(8):
                pairs = pairs + jnp.where(which == i, found[16 * i : 16 * i + 16, :], 0.0)
            odd = jnp.floor(pairs * 0.125)
            for top, level in ((0, pairs - 8.0 * odd), (16, odd)):
                weights = jnp.zeros((16, 128), F32)
                for n, w in enumerate(LOC_TABLE):
                    weights = weights + jnp.where(level == n, w, 0.0)
                loc_ref[b, top : top + 16, at] = weights
    for x_ref, c_ref in zip(outs, centered):
        center(x_ref[...], c_ref)


def slots(info_ref):
    here, core = info_ref[3], info_ref[4]
    straight = [lax.rem(here - s + 4, 4) * 2 + core for s in range(4)]
    return straight + [lax.rem(here - s + 4, 4) * 2 + 1 - core for s in range(4)]


def stack(info_ref, refs, anom_ref, incr_ref, inverse_ref):
    for slot, ref in zip(slots(info_ref), refs):
        at = pl.ds(pl.multiple_of(slot * 128, 128), 128)
        rows = ref[0:128, :]
        anom_ref[at, :] = rows
        incr_ref[:, at] = ref[128:208, :]
        wide = rows.astype(F32)
        inverse_ref[at, :] = jnp.broadcast_to((wide[:, 80:81] + wide[:, 81:82]) + wide[:, 82:83], (128, 128))


def moved(x_ref, centered_ref, loc_ref, at, batch, anom_ref, incr_ref, inverse_ref, cov_ref, gain_ref):
    cov_ref[...] = jnp.dot(anom_ref[...], centered_ref[...], preferred_element_type=F32)
    for ob in range(8):
        row = 16 * (ob % 2) + 4 * batch + ob // 2
        rows = slice(128 * ob, 128 * ob + 128)
        for k in range(4):
            cols = slice(128 * k, 128 * k + 128)
            gain = (cov_ref[rows, cols] * inverse_ref[rows, :]) * loc_ref[at, row : row + 1, cols]
            gain_ref[rows, cols] = gain.astype(BF16)
    return x_ref[...] + jnp.dot(incr_ref[...], gain_ref[...], preferred_element_type=F32)


def next_batch(batch):
    def body(info_ref, *refs):
        x_ref, c_ref, loc_ref, weight_ref, value_ref, errvar_ref = refs[8:14]
        out_ref, anom_ref, incr_ref, inverse_ref, cov_ref, gain_ref, wide_ref = refs[14:]
        stack(info_ref, refs[:8], anom_ref, incr_ref, inverse_ref)
        x = moved(x_ref, c_ref, loc_ref, batch - 1, batch - 1, anom_ref, incr_ref, inverse_ref, cov_ref, gain_ref)
        here = lanes(info_ref)
        prior = x[:, 0:128] * weight_ref[batch, 0:1, here]
        for k in range(1, 4):
            prior = prior + x[:, 128 * k : 128 * k + 128] * weight_ref[batch, k : k + 1, here]
        increments(prior, value_ref[batch : batch + 1, here], errvar_ref[batch : batch + 1, here], out_ref, wide_ref)

    return body


def advance(at, batch):
    def body(anom_ref, incr_ref, inverse_ref, x_ref, c_ref, loc_ref, out_ref, c_out_ref, cov_ref, gain_ref):
        x = moved(x_ref, c_ref, loc_ref, at, batch, anom_ref, incr_ref, inverse_ref, cov_ref, gain_ref)
        out_ref[...] = x
        center(x, c_out_ref)

    return body


def finish(info_ref, *refs):
    x_ref, c_ref, loc_ref, out_ref, anom_ref, incr_ref, inverse_ref, cov_ref, gain_ref, work_ref = refs[8:]
    stack(info_ref, refs[:8], anom_ref, incr_ref, inverse_ref)
    work_ref[...] = moved(x_ref, c_ref, loc_ref, 3, 3, anom_ref, incr_ref, inverse_ref, cov_ref, gain_ref)
    for z in range(8):
        out_ref[10 * z : 10 * z + 8, :] = work_ref[8 * z : 8 * z + 8, :]
        out_ref[10 * z + 8 : 10 * z + 10, :] = work_ref[64 + 2 * z : 66 + 2 * z, :]


def shift(a, axis, by, size):
    return lax.ppermute(a, axis, [(i, (i + by) % size) for i in range(size)])


def spread(g):
    own = [g] + [shift(g, "x", s, 4) for s in (1, 2, 3)]
    return own + [shift(v, "c", 1, 2) for v in own]


def per_device(ensemble, obs_index, obs_weight, obs_value, obs_error_var, loc_class):
    z, y, x, c = [lax.axis_index(n) for n in ("z", "y", "x", "c")]
    block = x * 2 + c
    info = jnp.stack([(y * 8 + block) * 4096, block, y, x, c, (y * 8 + block) * 32 + z * 4]).astype(jnp.int32)

    rows = [((CHUNK, 128), F32)]
    other, ext, tile = call(
        collect_other,
        [((4, CHUNK, 128), F32), ((16, 4096), F32), ((8, 128), F32)],
        [obs_index, ensemble, loc_class],
        [info],
        [pltpu.VMEM((1, 128), F32)],
        name="collect_other",
    )
    other = shift(other, "c", 1, 2)
    (own,) = call(collect_own, [((2, CHUNK, 128), F32)], [obs_index, ext, tile], [info], flops=10**9, name="collect_own")
    p1, p2 = call(add_cores, rows * 2, [own, other], [], name="add_cores")
    p1, p2 = shift(p1, "x", 1, 4), shift(p2, "x", 2, 4)
    p0, p3 = call(
        collect_rest,
        rows * 2,
        [obs_index, ext, tile, other],
        [info],
        [pltpu.VMEM((2, CHUNK, 128), F32)],
        flops=10**9,
        name="collect_rest",
    )
    sums = [p0, p1, p2, shift(p3, "x", 3, 4)]
    (part,) = call(add_columns, rows, sums, [], name="add_columns")
    parts = [part] + [shift(part, "y", s, 4) for s in (1, 2, 3)]
    (pack,) = call(
        add_rows,
        [((8, PACK, 128), F32)],
        [obs_weight, ext] + parts,
        [info],
        [pltpu.VMEM((160, 128), F32)],
        name="add_rows",
    )
    pack = lax.all_to_all(pack, "z", 0, 0, tiled=True)

    tall, centered, sent = ((80, 512), F32), ((128, 512), BF16), ((208, 128), BF16)
    blocks = [((1024, 128), BF16), ((80, 1024), BF16), ((1024, 128), F32)]
    wide = pltpu.VMEM((128, 128), F32)
    work = [pltpu.VMEM((1024, 512), F32), pltpu.VMEM((1024, 512), BF16)]
    flops = 2 * 2 * 1024 * 128 * 512
    (g,) = call(
        first_batch,
        [sent],
        [pack, obs_value, obs_error_var],
        [info],
        [pltpu.VMEM((80, 128), F32), wide],
        name="first_batch",
    )
    *both, loc = call(
        unpack,
        [tall] * 4 + [centered] * 4 + [((4, 32, 512), F32)],
        [pack, obs_index],
        [info],
        flops=2 * 128 * 128 * 2048,
        name="unpack",
    )
    held = dict(enumerate(zip(both[:4], both[4:])))
    for batch in range(3):
        g, *stacked = call(
            next_batch(batch + 1),
            [sent] + blocks,
            spread(g) + [*held[batch], loc, obs_weight, obs_value, obs_error_var],
            [info],
            work + [wide],
            flops=flops,
            name="next_batch",
        )
        for at in range(batch + 1, 4):
            held[at] = call(
                advance(at, batch),
                [tall, centered],
                stacked + [*held[at], loc],
                [],
                work,
                flops=flops,
                name="advance",
            )
    (state,) = call(
        finish,
        [tall],
        spread(g) + [*held[3], loc],
        [info],
        [pltpu.VMEM(s, d) for s, d in blocks] + work + [pltpu.VMEM((80, 512), F32)],
        flops=flops,
        name="finish",
    )
    return state


def solution(mesh):
    fine = Mesh(mesh.devices.reshape(8, 4, 4, 2), ("z", "y", "x", "c"))
    tiles = ("y", "x", "c")
    in_specs = (P("z", tiles), P(), P(), P(), P(), P(tiles + ("z",), None))
    out_specs = P(None, tiles + ("z",))
    return jax.shard_map(per_device, mesh=fine, in_specs=in_specs, out_specs=out_specs, check_vma=False)
```

time: 1110 us -> 108 us (0.10)
  waiting for transfers between devices: 1010 us -> 9.85 us
  local copies, waits for them, and re-layouts: 48.3 us -> 2.49 us
  starting transfers between devices: 9.36 us -> 45.5 us
  blocking collectives: 0 us -> 26.6 us
  other arithmetic: 23.2 us -> 0 us
  Pallas kernels: 0 us -> 22.9 us
  between operations: 13.7 us -> 0.31 us
    psum x4 -> x0, waiting for transfers between devices: 1000 us -> none  [per_device(): prior = lax.psum(partial_value, ('mem', 'dom'))]
    ppermute x0 -> x35, starting transfers between devices: none -> 45.5 us  [shift(): return lax.ppermute(a, axis, [(i, (i + by) % size) for i in range(size)])]
    gather x16 -> x0, local copies, waits for them, and re-layouts: 44.9 us -> none  [local_prior(): picked = states[:, safe]]
    all_to_all x0 -> x1, blocking collectives: none -> 26.6 us  [per_device(): pack = lax.all_to_all(pack, 'z', 0, 0, tiled=True)]
    pallas_call x0 -> x18, Pallas kernels: none -> 22.9 us  [call(): pl.pallas_call(body, out_shape=outs, in_specs=[SMEM] * len(scalars) + [VM...]
  transfers between devices with their start and end apart: 5 -> 35, of which waited for: 5 -> 11; matrix products, arithmetic and copies ran while one was open for 0% -> 0% of each run, Pallas kernels for 0% -> 9%
where the time goes in v1:
time: 108 us
  starting transfers between devices  45.5 us (42%)
  blocking collectives  26.6 us (25%)
  Pallas kernels  22.9 us (21%)
  waiting for transfers between devices  9.85 us (9%)
  local copies, waits for them, and re-layouts  2.49 us (2%)
    ppermute x35, starting transfers between devices, shift(): return lax.ppermute(a, axis, [(i, (i + by) % size) for i in range(size)])  45.5 us
    all_to_all x1, blocking collectives, per_device(): pack = lax.all_to_all(pack, 'z', 0, 0, tiled=True)  26.6 us
    pallas_call x18, Pallas kernels, call(): pl.pallas_call(body, out_shape=outs, in_specs=[SMEM] * len(scalars) + [VM...  22.9 us
    ppermute x35, waiting for transfers between devices, shift(): return lax.ppermute(a, axis, [(i, (i + by) % size) for i in range(size)])  9.85 us
    unnamed x14, local copies, waits for them, and re-layouts  2.41 us
  transfers between devices with their start and end apart: 35, of which 11 were waited for; matrix products, arithmetic and copies ran while one was open for 0% of the time, Pallas kernels for 9%

profile of v1, /device:TPU:1, one launch (start us, length us, event | category | flops | bytes accessed | tf_op | source)
XLA Modules:
  0.0 107.8 jit_solution(4795619776677111432)
XLA Ops:
  1.5 0.9 copy-done.5
  2.5 4.0 %collect_other.1 = (f32[4,168,128]{2,1,0:T(8,128)S(1)}, f32[16,4096]{1,0:T(8,128)S(1)}, f32[8,128]{1,0:T(8,128)S(1)}) custom-call(s32[6]{0:T(128)S(1)} %stack.27.info_ref, s32[4,4,1024]{2,1,0:T(4,128)S(1)} %copy-done.3, f32[10,4096]{1,0:T(8,128)S(1)} %copy-done.5, s32[4,32]{1,0:T(4,128)S(1)} %copy-done.6), custom_call_target="tpu_custom_call" | custom-call | bytes 840192 | tf_op jit(solution)/shard_map/collect_other/pallas_call | solution.py:22
  6.5 3.3 %collective-permute-start = (f32[4,168,128]{2,1,0:T(8,128)S(1)}, f32[4,168,128]{2,1,0:T(8,128)S(1)}, u32[]{:S(2)}, u32[]{:S(2)}) collective-permute-start(f32[4,168,128]{2,1,0:T(8,128)S(1)} %get-tuple-element.47), channel_id=1, source_target_pairs={{0,1},{1,0},{2,3},{3,2},{4,5},{5,4},{6,7},{7,6},{8,9},{9,8},{10,11... | collective-permute-start | bytes 1032200 | tf_op jit(solution)/shard_map/ppermute | solution.py:268
  9.8 2.2 %collect_own.1.own_ref = f32[2,168,128]{2,1,0:T(8,128)S(1)} custom-call(s32[6]{0:T(128)S(1)} %stack.27.info_ref, s32[4,4,1024]{2,1,0:T(4,128)S(1)} %copy-done.3, f32[16,4096]{1,0:T(8,128)S(1)} %get-tuple-element.45.ext_ref, f32[8,128]{1,0:T(8,128)S(1)} %get-tuple-element.46.tile_ref), custom_call_target="tpu_custom_call" | custom-call | flops 1000000000 | bytes 503808 | tf_op jit(solution)/shard_map/collect_own/pallas_call | solution.py:22
  12.1 1.9 %collective-permute-start.2 = (f32[168,128]{1,0:T(8,128)S(1)}, f32[168,128]{1,0:T(8,128)S(1)}, u32[]{:S(2)}, u32[]{:S(2)}) collective-permute-start(f32[168,128]{1,0:T(8,128)S(1)} %get-tuple-element.50), channel_id=1, source_target_pairs={{0,4},{2,6},{4,0},{6,2},{1,5},{3,7},{5,1},{7,3},{8,12},{10,14},{12... | collective-permute-start | bytes 258056 | tf_op jit(solution)/shard_map/ppermute | solution.py:268
  14.0 2.2 %collect_rest.1 = (f32[168,128]{1,0:T(8,128)S(1)}, f32[168,128]{1,0:T(8,128)S(1)}) custom-call(s32[6]{0:T(128)S(1)} %stack.27.info_ref, s32[4,4,1024]{2,1,0:T(4,128)S(1)} %copy-done.3, f32[16,4096]{1,0:T(8,128)S(1)} %get-tuple-element.45.ext_ref, f32[8,128]{1,0:T(8,128)S(1)} %get-tuple-element.46.tile_ref, ...), custom_call_target="tpu_custom_call" | custom-call | flops 1000000000 | bytes 847872 | tf_op jit(solution)/shard_map/collect_rest/pallas_call | solution.py:22
  16.2 1.2 %collective-permute-start.3 = (f32[168,128]{1,0:T(8,128)S(1)}, f32[168,128]{1,0:T(8,128)S(1)}, u32[]{:S(2)}, u32[]{:S(2)}) collective-permute-start(f32[168,128]{1,0:T(8,128)S(1)} %get-tuple-element.51), channel_id=1, source_target_pairs={{0,6},{2,0},{4,2},{6,4},{1,7},{3,1},{5,3},{7,5},{8,14},{10,8},{12,... | collective-permute-start | bytes 258056 | tf_op jit(solution)/shard_map/ppermute | solution.py:268
  17.5 1.9 %collective-permute-done.1.p1_ref = f32[168,128]{1,0:T(8,128)S(1)} collective-permute-done((f32[168,128]{1,0:T(8,128)S(1)}, f32[168,128]{1,0:T(8,128)S(1)}, u32[]{:S(2)}, u32[]{:S(2)}) %collective-permute-start.1) | collective-permute-done | bytes 86048 | tf_op jit(solution)/shard_map/ppermute | solution.py:268
  19.7 2.7 %collective-permute-start.6 = (f32[168,128]{1,0:T(8,128)S(1)}, f32[168,128]{1,0:T(8,128)S(1)}, u32[]{:S(2)}, u32[]{:S(2)}) collective-permute-start(f32[168,128]{1,0:T(8,128)S(1)} %add_columns.1.p0_ref), channel_id=1, source_target_pairs={{0,24},{8,0},{16,8},{24,16},{1,25},{9,1},{17,9},{25,17},{2,26},{10... | collective-permute-start | bytes 258056 | tf_op jit(solution)/shard_map/ppermute | solution.py:268
  24.0 3.4 %collective-permute-done.5.p2_ref = f32[168,128]{1,0:T(8,128)S(1)} collective-permute-done((f32[168,128]{1,0:T(8,128)S(1)}, f32[168,128]{1,0:T(8,128)S(1)}, u32[]{:S(2)}, u32[]{:S(2)}) %collective-permute-start.5) | collective-permute-done | bytes 86048 | tf_op jit(solution)/shard_map/ppermute | solution.py:268
  28.9 26.6 %all_to_all.5.pack_ref = f32[8,192,128]{2,1,0:T(8,128)S(1)} all-to-all(f32[8,192,128]{2,1,0:T(8,128)S(1)} %add_rows.1), channel_id=1, replica_groups=mesh['z'=8,'y'=4,'x'=4,'c'=2] {'z'}, dimensions={0} | all-to-all | bytes 1572864 | tf_op jit(solution)/shard_map/all_to_all | solution.py:314
  56.2 2.4 %collective-permute-start.9 = (bf16[208,128]{1,0:T(8,128)(2,1)S(1)}, bf16[208,128]{1,0:T(8,128)(2,1)S(1)}, u32[]{:S(2)}, u32[]{:S(2)}) collective-permute-start(bf16[208,128]{1,0:T(8,128)(2,1)S(1)} %first_batch.1.refs_0_), channel_id=1, source_target_pairs={{0,6},{2,0},{4,2},{6,4},{1,7},{3,1},{5,3},{7,5},{8,14},{10,8},{12,... | collective-permute-start | bytes 159752 | tf_op jit(solution)/shard_map/ppermute | solution.py:268
  59.7 5.6 %collective-permute-start.10 = (bf16[208,128]{1,0:T(8,128)(2,1)S(1)}, bf16[208,128]{1,0:T(8,128)(2,1)S(1)}, u32[]{:S(2)}, u32[]{:S(2)}) collective-permute-start(bf16[208,128]{1,0:T(8,128)(2,1)S(1)} %first_batch.1.refs_0_), channel_id=1, source_target_pairs={{0,1},{1,0},{2,3},{3,2},{4,5},{5,4},{6,7},{7,6},{8,9},{9,8},{10,11... | collective-permute-start | bytes 159752 | tf_op jit(solution)/shard_map/ppermute | solution.py:268
  66.2 3.9 %collective-permute-start.12 = (bf16[208,128]{1,0:T(8,128)(2,1)S(1)}, bf16[208,128]{1,0:T(8,128)(2,1)S(1)}, u32[]{:S(2)}, u32[]{:S(2)}) collective-permute-start(bf16[208,128]{1,0:T(8,128)(2,1)S(1)} %collective-permute-done.8.refs_2_), channel_id=1, source_target_pairs={{0,1},{1,0},{2,3},{3,2},{4,5},{5,4},{6,7},{7,6},{8,9},{9,8},{10,11... | collective-permute-start | bytes 159752 | tf_op jit(solution)/shard_map/ppermute | solution.py:268
  70.3 1.1 %unpack.1 = (f32[80,512]{1,0:T(8,128)S(1)}, f32[80,512]{1,0:T(8,128)S(1)}, f32[80,512]{1,0:T(8,128)S(1)}, f32[80,512]{1,0:T(8,128)S(1)}, bf16[128,512]{1,0:T(8,1...) custom-call(s32[6]{0:T(128)S(1)} %stack.27.info_ref, ...), custom_call_target="tpu_custom_call" | custom-call | flops 67108864 | bytes 2293760 | tf_op jit(solution)/shard_map/unpack/pallas_call | solution.py:22
  71.4 1.9 %next_batch.3 = (bf16[208,128]{1,0:T(8,128)(2,1)S(1)}, bf16[1024,128]{1,0:T(8,128)(2,1)S(1)}, bf16[80,1024]{1,0:T(8,128)(2,1)S(1)}, f32[1024,128]{1,0:T(8,128)S(1)}) custom-call(s32[6]{0:T(128)S(1)} %stack.27.info_ref, bf16[208,128]{1,0:T(8,128)(2,1)S(1)} %first_batch.1.refs_0_, bf16[208,128]{1,0:T(8,128)(2,1)S(1)} %collective-permute-done.7.refs_1_, ...), custom_call_target="tpu_custom_call" | custom-call | flops 268435456 | bytes 2084864 | tf_op jit(solution)/shard_map/next_batch/pallas_call | solution.py:22
  74.0 1.0 collective-permute-start.15
  75.8 0.9 collective-permute-start.17
  76.7 1.7 %collective-permute-start.20 = (bf16[208,128]{1,0:T(8,128)(2,1)S(1)}, bf16[208,128]{1,0:T(8,128)(2,1)S(1)}, u32[]{:S(2)}, u32[]{:S(2)}) collective-permute-start(bf16[208,128]{1,0:T(8,128)(2,1)S(1)} %collective-permute-done.16.refs_3_), channel_id=1, source_target_pairs={{0,1},{1,0},{2,3},{3,2},{4,5},{5,4},{6,7},{7,6},{8,9},{9,8},{10,11... | collective-permute-start | bytes 159752 | tf_op jit(solution)/shard_map/ppermute | solution.py:268
  78.5 1.6 %collective-permute-start.19 = (bf16[208,128]{1,0:T(8,128)(2,1)S(1)}, bf16[208,128]{1,0:T(8,128)(2,1)S(1)}, u32[]{:S(2)}, u32[]{:S(2)}) collective-permute-start(bf16[208,128]{1,0:T(8,128)(2,1)S(1)} %collective-permute-done.15.refs_2_), channel_id=1, source_target_pairs={{0,1},{1,0},{2,3},{3,2},{4,5},{5,4},{6,7},{7,6},{8,9},{9,8},{10,11... | collective-permute-start | bytes 159752 | tf_op jit(solution)/shard_map/ppermute | solution.py:268
  81.9 1.9 %next_batch.4 = (bf16[208,128]{1,0:T(8,128)(2,1)S(1)}, bf16[1024,128]{1,0:T(8,128)(2,1)S(1)}, bf16[80,1024]{1,0:T(8,128)(2,1)S(1)}, f32[1024,128]{1,0:T(8,128)S(1)}) custom-call(s32[6]{0:T(128)S(1)} %stack.27.info_ref, bf16[208,128]{1,0:T(8,128)(2,1)S(1)} %get-tuple-element.55.refs_0_, bf16[208,128]{1,0:T(8,128)(2,1)S(1)} %collective-permute-done.14.refs_1_, ...), custom_call_target="tpu_custom_call" | custom-call | flops 268435456 | bytes 2084864 | tf_op jit(solution)/shard_map/next_batch/pallas_call | solution.py:22
  83.8 1.4 %collective-permute-start.23 = (bf16[208,128]{1,0:T(8,128)(2,1)S(1)}, bf16[208,128]{1,0:T(8,128)(2,1)S(1)}, u32[]{:S(2)}, u32[]{:S(2)}) collective-permute-start(bf16[208,128]{1,0:T(8,128)(2,1)S(1)} %get-tuple-element.63.refs_0_), channel_id=1, source_target_pairs={{0,6},{2,0},{4,2},{6,4},{1,7},{3,1},{5,3},{7,5},{8,14},{10,8},{12,... | collective-permute-start | bytes 159752 | tf_op jit(solution)/shard_map/ppermute | solution.py:268
  85.2 1.0 collective-permute-start.22
  86.9 1.8 %collective-permute-start.27 = (bf16[208,128]{1,0:T(8,128)(2,1)S(1)}, bf16[208,128]{1,0:T(8,128)(2,1)S(1)}, u32[]{:S(2)}, u32[]{:S(2)}) collective-permute-start(bf16[208,128]{1,0:T(8,128)(2,1)S(1)} %collective-permute-done.23.refs_3_), channel_id=1, source_target_pairs={{0,1},{1,0},{2,3},{3,2},{4,5},{5,4},{6,7},{7,6},{8,9},{9,8},{10,11... | collective-permute-start | bytes 159752 | tf_op jit(solution)/shard_map/ppermute | solution.py:268
  88.7 1.0 collective-permute-done.22.refs_2_
  89.7 2.0 %collective-permute-start.26 = (bf16[208,128]{1,0:T(8,128)(2,1)S(1)}, bf16[208,128]{1,0:T(8,128)(2,1)S(1)}, u32[]{:S(2)}, u32[]{:S(2)}) collective-permute-start(bf16[208,128]{1,0:T(8,128)(2,1)S(1)} %collective-permute-done.22.refs_2_), channel_id=1, source_target_pairs={{0,1},{1,0},{2,3},{3,2},{4,5},{5,4},{6,7},{7,6},{8,9},{9,8},{10,11... | collective-permute-start | bytes 159752 | tf_op jit(solution)/shard_map/ppermute | solution.py:268
  93.7 1.9 %next_batch.5 = (bf16[208,128]{1,0:T(8,128)(2,1)S(1)}, bf16[1024,128]{1,0:T(8,128)(2,1)S(1)}, bf16[80,1024]{1,0:T(8,128)(2,1)S(1)}, f32[1024,128]{1,0:T(8,128)S(1)}) custom-call(s32[6]{0:T(128)S(1)} %stack.27.info_ref, bf16[208,128]{1,0:T(8,128)(2,1)S(1)} %get-tuple-element.63.refs_0_, bf16[208,128]{1,0:T(8,128)(2,1)S(1)} %collective-permute-done.21.refs_1_, ...), custom_call_target="tpu_custom_call" | custom-call | flops 268435456 | bytes 2084864 | tf_op jit(solution)/shard_map/next_batch/pallas_call | solution.py:22
  97.5 0.8 collective-permute-start.31
  99.1 1.2 %collective-permute-start.34 = (bf16[208,128]{1,0:T(8,128)(2,1)S(1)}, bf16[208,128]{1,0:T(8,128)(2,1)S(1)}, u32[]{:S(2)}, u32[]{:S(2)}) collective-permute-start(bf16[208,128]{1,0:T(8,128)(2,1)S(1)} %collective-permute-done.30.refs_3_), channel_id=1, source_target_pairs={{0,1},{1,0},{2,3},{3,2},{4,5},{5,4},{6,7},{7,6},{8,9},{9,8},{10,11... | collective-permute-start | bytes 159752 | tf_op jit(solution)/shard_map/ppermute | solution.py:268
  100.7 1.5 %collective-permute-start.33 = (bf16[208,128]{1,0:T(8,128)(2,1)S(1)}, bf16[208,128]{1,0:T(8,128)(2,1)S(1)}, u32[]{:S(2)}, u32[]{:S(2)}) collective-permute-start(bf16[208,128]{1,0:T(8,128)(2,1)S(1)} %collective-permute-done.29.refs_2_), channel_id=1, source_target_pairs={{0,1},{1,0},{2,3},{3,2},{4,5},{5,4},{6,7},{7,6},{8,9},{9,8},{10,11... | collective-permute-start | bytes 159752 | tf_op jit(solution)/shard_map/ppermute | solution.py:268
  102.2 1.0 collective-permute-start.32
  105.2 2.6 %finish.1 = f32[80,512]{1,0:T(8,128)} custom-call(s32[6]{0:T(128)S(1)} %stack.27.info_ref, bf16[208,128]{1,0:T(8,128)(2,1)S(1)} %get-tuple-element.73.refs_0_, bf16[208,128]{1,0:T(8,128)(2,1)S(1)} %collective-permute-done.28.refs_1_, bf16[208,128]{1,0:T(8,128)(2,1)S(1)} %collective-permute-done.29.refs_2_, ...), custom_call_target="tpu_custom_call" | custom-call | flops 268435456 | bytes 1146880 | tf_op jit(solution)/shard_map/finish/pallas_call | solution.py:22
  (72 shorter events, 18.8 us)
Async XLA Ops:
  6.5 5.5 %collective-permute-start = (f32[4,168,128]{2,1,0:T(8,128)S(1)}, f32[4,168,128]{2,1,0:T(8,128)S(1)}, u32[]{:S(2)}, u32[]{:S(2)}) collective-permute-start(f32[4,168,128]{2,1,0:T(8,128)S(1)} %get-tuple-element.47), channel_id=1, source_target_pairs={{0,1},{1,0},{2,3},{3,2},{4,5},{5,4},{6,7},{7,6},{8,9},{9,8},{10,11... | collective-permute-start | bytes 1032200 | tf_op jit(solution)/shard_map/ppermute | solution.py:268
  12.0 7.3 %collective-permute-start.1 = (f32[168,128]{1,0:T(8,128)S(1)}, f32[168,128]{1,0:T(8,128)S(1)}, u32[]{:S(2)}, u32[]{:S(2)}) collective-permute-start(f32[168,128]{1,0:T(8,128)S(1)} %get-tuple-element.49), channel_id=1, source_target_pairs={{0,2},{2,4},{4,6},{6,0},{1,3},{3,5},{5,7},{7,1},{8,10},{10,12},{12... | collective-permute-start | bytes 258056 | tf_op jit(solution)/shard_map/ppermute | solution.py:268
  12.1 7.2 %collective-permute-start.2 = (f32[168,128]{1,0:T(8,128)S(1)}, f32[168,128]{1,0:T(8,128)S(1)}, u32[]{:S(2)}, u32[]{:S(2)}) collective-permute-start(f32[168,128]{1,0:T(8,128)S(1)} %get-tuple-element.50), channel_id=1, source_target_pairs={{0,4},{2,6},{4,0},{6,2},{1,5},{3,7},{5,1},{7,3},{8,12},{10,14},{12... | collective-permute-start | bytes 258056 | tf_op jit(solution)/shard_map/ppermute | solution.py:268
  16.2 3.5 %collective-permute-start.3 = (f32[168,128]{1,0:T(8,128)S(1)}, f32[168,128]{1,0:T(8,128)S(1)}, u32[]{:S(2)}, u32[]{:S(2)}) collective-permute-start(f32[168,128]{1,0:T(8,128)S(1)} %get-tuple-element.51), channel_id=1, source_target_pairs={{0,6},{2,0},{4,2},{6,4},{1,7},{3,1},{5,3},{7,5},{8,14},{10,8},{12,... | collective-permute-start | bytes 258056 | tf_op jit(solution)/shard_map/ppermute | solution.py:268
  19.7 4.3 %collective-permute-start.6 = (f32[168,128]{1,0:T(8,128)S(1)}, f32[168,128]{1,0:T(8,128)S(1)}, u32[]{:S(2)}, u32[]{:S(2)}) collective-permute-start(f32[168,128]{1,0:T(8,128)S(1)} %add_columns.1.p0_ref), channel_id=1, source_target_pairs={{0,24},{8,0},{16,8},{24,16},{1,25},{9,1},{17,9},{25,17},{2,26},{10... | collective-permute-start | bytes 258056 | tf_op jit(solution)/shard_map/ppermute | solution.py:268
  22.5 4.9 %collective-permute-start.5 = (f32[168,128]{1,0:T(8,128)S(1)}, f32[168,128]{1,0:T(8,128)S(1)}, u32[]{:S(2)}, u32[]{:S(2)}) collective-permute-start(f32[168,128]{1,0:T(8,128)S(1)} %add_columns.1.p0_ref), channel_id=1, source_target_pairs={{0,16},{8,24},{16,0},{24,8},{1,17},{9,25},{17,1},{25,9},{2,18},{10... | collective-permute-start | bytes 258056 | tf_op jit(solution)/shard_map/ppermute | solution.py:268
  22.8 5.4 %collective-permute-start.4 = (f32[168,128]{1,0:T(8,128)S(1)}, f32[168,128]{1,0:T(8,128)S(1)}, u32[]{:S(2)}, u32[]{:S(2)}) collective-permute-start(f32[168,128]{1,0:T(8,128)S(1)} %add_columns.1.p0_ref), channel_id=1, source_target_pairs={{0,8},{8,16},{16,24},{24,0},{1,9},{9,17},{17,25},{25,1},{2,10},{10... | collective-permute-start | bytes 258056 | tf_op jit(solution)/shard_map/ppermute | solution.py:268
  56.2 9.1 %collective-permute-start.9 = (bf16[208,128]{1,0:T(8,128)(2,1)S(1)}, bf16[208,128]{1,0:T(8,128)(2,1)S(1)}, u32[]{:S(2)}, u32[]{:S(2)}) collective-permute-start(bf16[208,128]{1,0:T(8,128)(2,1)S(1)} %first_batch.1.refs_0_), channel_id=1, source_target_pairs={{0,6},{2,0},{4,2},{6,4},{1,7},{3,1},{5,3},{7,5},{8,14},{10,8},{12,... | collective-permute-start | bytes 159752 | tf_op jit(solution)/shard_map/ppermute | solution.py:268
  58.7 7.5 %collective-permute-start.8 = (bf16[208,128]{1,0:T(8,128)(2,1)S(1)}, bf16[208,128]{1,0:T(8,128)(2,1)S(1)}, u32[]{:S(2)}, u32[]{:S(2)}) collective-permute-start(bf16[208,128]{1,0:T(8,128)(2,1)S(1)} %first_batch.1.refs_0_), channel_id=1, source_target_pairs={{0,4},{2,6},{4,0},{6,2},{1,5},{3,7},{5,1},{7,3},{8,12},{10,14},{12... | collective-permute-start | bytes 159752 | tf_op jit(solution)/shard_map/ppermute | solution.py:268
  59.2 10.9 %collective-permute-start.7 = (bf16[208,128]{1,0:T(8,128)(2,1)S(1)}, bf16[208,128]{1,0:T(8,128)(2,1)S(1)}, u32[]{:S(2)}, u32[]{:S(2)}) collective-permute-start(bf16[208,128]{1,0:T(8,128)(2,1)S(1)} %first_batch.1.refs_0_), channel_id=1, source_target_pairs={{0,2},{2,4},{4,6},{6,0},{1,3},{3,5},{5,7},{7,1},{8,10},{10,12},{12... | collective-permute-start | bytes 159752 | tf_op jit(solution)/shard_map/ppermute | solution.py:268
  59.7 11.6 %collective-permute-start.10 = (bf16[208,128]{1,0:T(8,128)(2,1)S(1)}, bf16[208,128]{1,0:T(8,128)(2,1)S(1)}, u32[]{:S(2)}, u32[]{:S(2)}) collective-permute-start(bf16[208,128]{1,0:T(8,128)(2,1)S(1)} %first_batch.1.refs_0_), channel_id=1, source_target_pairs={{0,1},{1,0},{2,3},{3,2},{4,5},{5,4},{6,7},{7,6},{8,9},{9,8},{10,11... | collective-permute-start | bytes 159752 | tf_op jit(solution)/shard_map/ppermute | solution.py:268
  65.3 6.1 %collective-permute-start.13 = (bf16[208,128]{1,0:T(8,128)(2,1)S(1)}, bf16[208,128]{1,0:T(8,128)(2,1)S(1)}, u32[]{:S(2)}, u32[]{:S(2)}) collective-permute-start(bf16[208,128]{1,0:T(8,128)(2,1)S(1)} %collective-permute-done.9.refs_3_), channel_id=1, source_target_pairs={{0,1},{1,0},{2,3},{3,2},{4,5},{5,4},{6,7},{7,6},{8,9},{9,8},{10,11... | collective-permute-start | bytes 159752 | tf_op jit(solution)/shard_map/ppermute | solution.py:268
  66.2 5.2 %collective-permute-start.12 = (bf16[208,128]{1,0:T(8,128)(2,1)S(1)}, bf16[208,128]{1,0:T(8,128)(2,1)S(1)}, u32[]{:S(2)}, u32[]{:S(2)}) collective-permute-start(bf16[208,128]{1,0:T(8,128)(2,1)S(1)} %collective-permute-done.8.refs_2_), channel_id=1, source_target_pairs={{0,1},{1,0},{2,3},{3,2},{4,5},{5,4},{6,7},{7,6},{8,9},{9,8},{10,11... | collective-permute-start | bytes 159752 | tf_op jit(solution)/shard_map/ppermute | solution.py:268
  73.3 3.4 %collective-permute-start.16 = (bf16[208,128]{1,0:T(8,128)(2,1)S(1)}, bf16[208,128]{1,0:T(8,128)(2,1)S(1)}, u32[]{:S(2)}, u32[]{:S(2)}) collective-permute-start(bf16[208,128]{1,0:T(8,128)(2,1)S(1)} %get-tuple-element.55.refs_0_), channel_id=1, source_target_pairs={{0,6},{2,0},{4,2},{6,4},{1,7},{3,1},{5,3},{7,5},{8,14},{10,8},{12,... | collective-permute-start | bytes 159752 | tf_op jit(solution)/shard_map/ppermute | solution.py:268
  74.0 4.5 %collective-permute-start.15 = (bf16[208,128]{1,0:T(8,128)(2,1)S(1)}, bf16[208,128]{1,0:T(8,128)(2,1)S(1)}, u32[]{:S(2)}, u32[]{:S(2)}) collective-permute-start(bf16[208,128]{1,0:T(8,128)(2,1)S(1)} %get-tuple-element.55.refs_0_), channel_id=1, source_target_pairs={{0,4},{2,6},{4,0},{6,2},{1,5},{3,7},{5,1},{7,3},{8,12},{10,14},{12... | collective-permute-start | bytes 159752 | tf_op jit(solution)/shard_map/ppermute | solution.py:268
  75.0 5.4 %collective-permute-start.14 = (bf16[208,128]{1,0:T(8,128)(2,1)S(1)}, bf16[208,128]{1,0:T(8,128)(2,1)S(1)}, u32[]{:S(2)}, u32[]{:S(2)}) collective-permute-start(bf16[208,128]{1,0:T(8,128)(2,1)S(1)} %get-tuple-element.55.refs_0_), channel_id=1, source_target_pairs={{0,2},{2,4},{4,6},{6,0},{1,3},{3,5},{5,7},{7,1},{8,10},{10,12},{12... | collective-permute-start | bytes 159752 | tf_op jit(solution)/shard_map/ppermute | solution.py:268
  75.8 5.9 %collective-permute-start.17 = (bf16[208,128]{1,0:T(8,128)(2,1)S(1)}, bf16[208,128]{1,0:T(8,128)(2,1)S(1)}, u32[]{:S(2)}, u32[]{:S(2)}) collective-permute-start(bf16[208,128]{1,0:T(8,128)(2,1)S(1)} %get-tuple-element.55.refs_0_), channel_id=1, source_target_pairs={{0,1},{1,0},{2,3},{3,2},{4,5},{5,4},{6,7},{7,6},{8,9},{9,8},{10,11... | collective-permute-start | bytes 159752 | tf_op jit(solution)/shard_map/ppermute | solution.py:268
  76.7 5.0 %collective-permute-start.20 = (bf16[208,128]{1,0:T(8,128)(2,1)S(1)}, bf16[208,128]{1,0:T(8,128)(2,1)S(1)}, u32[]{:S(2)}, u32[]{:S(2)}) collective-permute-start(bf16[208,128]{1,0:T(8,128)(2,1)S(1)} %collective-permute-done.16.refs_3_), channel_id=1, source_target_pairs={{0,1},{1,0},{2,3},{3,2},{4,5},{5,4},{6,7},{7,6},{8,9},{9,8},{10,11... | collective-permute-start | bytes 159752 | tf_op jit(solution)/shard_map/ppermute | solution.py:268
  78.5 3.2 %collective-permute-start.19 = (bf16[208,128]{1,0:T(8,128)(2,1)S(1)}, bf16[208,128]{1,0:T(8,128)(2,1)S(1)}, u32[]{:S(2)}, u32[]{:S(2)}) collective-permute-start(bf16[208,128]{1,0:T(8,128)(2,1)S(1)} %collective-permute-done.15.refs_2_), channel_id=1, source_target_pairs={{0,1},{1,0},{2,3},{3,2},{4,5},{5,4},{6,7},{7,6},{8,9},{9,8},{10,11... | collective-permute-start | bytes 159752 | tf_op jit(solution)/shard_map/ppermute | solution.py:268
  83.8 3.1 %collective-permute-start.23 = (bf16[208,128]{1,0:T(8,128)(2,1)S(1)}, bf16[208,128]{1,0:T(8,128)(2,1)S(1)}, u32[]{:S(2)}, u32[]{:S(2)}) collective-permute-start(bf16[208,128]{1,0:T(8,128)(2,1)S(1)} %get-tuple-element.63.refs_0_), channel_id=1, source_target_pairs={{0,6},{2,0},{4,2},{6,4},{1,7},{3,1},{5,3},{7,5},{8,14},{10,8},{12,... | collective-permute-start | bytes 159752 | tf_op jit(solution)/shard_map/ppermute | solution.py:268
  85.2 4.5 %collective-permute-start.22 = (bf16[208,128]{1,0:T(8,128)(2,1)S(1)}, bf16[208,128]{1,0:T(8,128)(2,1)S(1)}, u32[]{:S(2)}, u32[]{:S(2)}) collective-permute-start(bf16[208,128]{1,0:T(8,128)(2,1)S(1)} %get-tuple-element.63.refs_0_), channel_id=1, source_target_pairs={{0,4},{2,6},{4,0},{6,2},{1,5},{3,7},{5,1},{7,3},{8,12},{10,14},{12... | collective-permute-start | bytes 159752 | tf_op jit(solution)/shard_map/ppermute | solution.py:268
  86.2 5.5 %collective-permute-start.21 = (bf16[208,128]{1,0:T(8,128)(2,1)S(1)}, bf16[208,128]{1,0:T(8,128)(2,1)S(1)}, u32[]{:S(2)}, u32[]{:S(2)}) collective-permute-start(bf16[208,128]{1,0:T(8,128)(2,1)S(1)} %get-tuple-element.63.refs_0_), channel_id=1, source_target_pairs={{0,2},{2,4},{4,6},{6,0},{1,3},{3,5},{5,7},{7,1},{8,10},{10,12},{12... | collective-permute-start | bytes 159752 | tf_op jit(solution)/shard_map/ppermute | solution.py:268
  86.2 7.4 %collective-permute-start.24 = (bf16[208,128]{1,0:T(8,128)(2,1)S(1)}, bf16[208,128]{1,0:T(8,128)(2,1)S(1)}, u32[]{:S(2)}, u32[]{:S(2)}) collective-permute-start(bf16[208,128]{1,0:T(8,128)(2,1)S(1)} %get-tuple-element.63.refs_0_), channel_id=1, source_target_pairs={{0,1},{1,0},{2,3},{3,2},{4,5},{5,4},{6,7},{7,6},{8,9},{9,8},{10,11... | collective-permute-start | bytes 159752 | tf_op jit(solution)/shard_map/ppermute | solution.py:268
  86.9 6.7 %collective-permute-start.27 = (bf16[208,128]{1,0:T(8,128)(2,1)S(1)}, bf16[208,128]{1,0:T(8,128)(2,1)S(1)}, u32[]{:S(2)}, u32[]{:S(2)}) collective-permute-start(bf16[208,128]{1,0:T(8,128)(2,1)S(1)} %collective-permute-done.23.refs_3_), channel_id=1, source_target_pairs={{0,1},{1,0},{2,3},{3,2},{4,5},{5,4},{6,7},{7,6},{8,9},{9,8},{10,11... | collective-permute-start | bytes 159752 | tf_op jit(solution)/shard_map/ppermute | solution.py:268
  89.7 3.9 %collective-permute-start.26 = (bf16[208,128]{1,0:T(8,128)(2,1)S(1)}, bf16[208,128]{1,0:T(8,128)(2,1)S(1)}, u32[]{:S(2)}, u32[]{:S(2)}) collective-permute-start(bf16[208,128]{1,0:T(8,128)(2,1)S(1)} %collective-permute-done.22.refs_2_), channel_id=1, source_target_pairs={{0,1},{1,0},{2,3},{3,2},{4,5},{5,4},{6,7},{7,6},{8,9},{9,8},{10,11... | collective-permute-start | bytes 159752 | tf_op jit(solution)/shard_map/ppermute | solution.py:268
  95.6 3.5 %collective-permute-start.30 = (bf16[208,128]{1,0:T(8,128)(2,1)S(1)}, bf16[208,128]{1,0:T(8,128)(2,1)S(1)}, u32[]{:S(2)}, u32[]{:S(2)}) collective-permute-start(bf16[208,128]{1,0:T(8,128)(2,1)S(1)} %get-tuple-element.73.refs_0_), channel_id=1, source_target_pairs={{0,6},{2,0},{4,2},{6,4},{1,7},{3,1},{5,3},{7,5},{8,14},{10,8},{12,... | collective-permute-start | bytes 159752 | tf_op jit(solution)/shard_map/ppermute | solution.py:268
  96.2 4.5 %collective-permute-start.29 = (bf16[208,128]{1,0:T(8,128)(2,1)S(1)}, bf16[208,128]{1,0:T(8,128)(2,1)S(1)}, u32[]{:S(2)}, u32[]{:S(2)}) collective-permute-start(bf16[208,128]{1,0:T(8,128)(2,1)S(1)} %get-tuple-element.73.refs_0_), channel_id=1, source_target_pairs={{0,4},{2,6},{4,0},{6,2},{1,5},{3,7},{5,1},{7,3},{8,12},{10,14},{12... | collective-permute-start | bytes 159752 | tf_op jit(solution)/shard_map/ppermute | solution.py:268
  96.8 5.3 %collective-permute-start.28 = (bf16[208,128]{1,0:T(8,128)(2,1)S(1)}, bf16[208,128]{1,0:T(8,128)(2,1)S(1)}, u32[]{:S(2)}, u32[]{:S(2)}) collective-permute-start(bf16[208,128]{1,0:T(8,128)(2,1)S(1)} %get-tuple-element.73.refs_0_), channel_id=1, source_target_pairs={{0,2},{2,4},{4,6},{6,0},{1,3},{3,5},{5,7},{7,1},{8,10},{10,12},{12... | collective-permute-start | bytes 159752 | tf_op jit(solution)/shard_map/ppermute | solution.py:268
  97.5 7.7 %collective-permute-start.31 = (bf16[208,128]{1,0:T(8,128)(2,1)S(1)}, bf16[208,128]{1,0:T(8,128)(2,1)S(1)}, u32[]{:S(2)}, u32[]{:S(2)}) collective-permute-start(bf16[208,128]{1,0:T(8,128)(2,1)S(1)} %get-tuple-element.73.refs_0_), channel_id=1, source_target_pairs={{0,1},{1,0},{2,3},{3,2},{4,5},{5,4},{6,7},{7,6},{8,9},{9,8},{10,11... | collective-permute-start | bytes 159752 | tf_op jit(solution)/shard_map/ppermute | solution.py:268
  99.1 6.0 %collective-permute-start.34 = (bf16[208,128]{1,0:T(8,128)(2,1)S(1)}, bf16[208,128]{1,0:T(8,128)(2,1)S(1)}, u32[]{:S(2)}, u32[]{:S(2)}) collective-permute-start(bf16[208,128]{1,0:T(8,128)(2,1)S(1)} %collective-permute-done.30.refs_3_), channel_id=1, source_target_pairs={{0,1},{1,0},{2,3},{3,2},{4,5},{5,4},{6,7},{7,6},{8,9},{9,8},{10,11... | collective-permute-start | bytes 159752 | tf_op jit(solution)/shard_map/ppermute | solution.py:268
  100.7 4.5 %collective-permute-start.33 = (bf16[208,128]{1,0:T(8,128)(2,1)S(1)}, bf16[208,128]{1,0:T(8,128)(2,1)S(1)}, u32[]{:S(2)}, u32[]{:S(2)}) collective-permute-start(bf16[208,128]{1,0:T(8,128)(2,1)S(1)} %collective-permute-done.29.refs_2_), channel_id=1, source_target_pairs={{0,1},{1,0},{2,3},{3,2},{4,5},{5,4},{6,7},{7,6},{8,9},{9,8},{10,11... | collective-permute-start | bytes 159752 | tf_op jit(solution)/shard_map/ppermute | solution.py:268
  102.2 3.0 %collective-permute-start.32 = (bf16[208,128]{1,0:T(8,128)(2,1)S(1)}, bf16[208,128]{1,0:T(8,128)(2,1)S(1)}, u32[]{:S(2)}, u32[]{:S(2)}) collective-permute-start(bf16[208,128]{1,0:T(8,128)(2,1)S(1)} %collective-permute-done.28.refs_1_), channel_id=1, source_target_pairs={{0,1},{1,0},{2,3},{3,2},{4,5},{5,4},{6,7},{7,6},{8,9},{9,8},{10,11... | collective-permute-start | bytes 159752 | tf_op jit(solution)/shard_map/ppermute | solution.py:268
  (10 other events, 83.8 us)

commit v2 on v1

--- a/solution.py
+++ b/solution.py
@@ -36,12 +36,12 @@
     return pl.ds(pl.multiple_of(info_ref[1] * 128, 128), 128)
 
 
-def pick(info_ref, shifts, core, index_ref, ext_ref, tile, start_ref, out_refs):
+def pick(info_ref, first_by, core, index_ref, ext_ref, tile, start_ref, out_refs):
     first = info_ref[0]
 
     def group(n, carry):
-        by = shifts + n
-        block = lax.rem(info_ref[3] + by, 4) * 2 + core
+        by = first_by ^ n
+        block = (info_ref[3] ^ by) * 2 + core
         here = pl.ds(pl.multiple_of(block * 128, 128), 128)
         for k in range(4):
             local = [index_ref[b, k : k + 1, here] - first for b in range(4)]
@@ -52,13 +52,13 @@
                 high = wide[b] >> 7
                 top = 0 if b < 4 else 8
                 rows = slice(40 * k + 8 * b, 40 * k + 8 * b + 8)
-                acc = jnp.zeros((8, 128), F32) if start_ref is None else start_ref[lax.rem(by, 4), rows, :]
+                acc = jnp.zeros((8, 128), F32) if start_ref is None else start_ref[by, rows, :]
                 for part in range(32):
                     source = ext_ref[top : top + 8, part * 128 : (part + 1) * 128]
                     got = jnp.take_along_axis(source, low, axis=1)
                     acc = jnp.where(high == part, got, acc)
                 out_refs[n, rows, :] = acc
-        rest = tile if start_ref is None else tile + start_ref[lax.rem(by, 4), 160:168, :]
+        rest = tile if start_ref is None else tile + start_ref[by, 160:168, :]
         out_refs[n, 160:168, :] = rest
         return carry
 
@@ -84,18 +84,18 @@
 
 
 def collect_own(info_ref, index_ref, ext_ref, tile_ref, out_ref):
-    pick(info_ref, 1, info_ref[4], index_ref, ext_ref, tile_ref[...], None, out_ref)
-
-
-def collect_rest(info_ref, index_ref, ext_ref, tile_ref, start_ref, p0_ref, p3_ref, work_ref):
-    pick(info_ref, 3, info_ref[4], index_ref, ext_ref, tile_ref[...], start_ref, work_ref)
-    p3_ref[...] = work_ref[0]
+    pick(info_ref, 2, info_ref[4], index_ref, ext_ref, tile_ref[...], None, out_ref)
+
+
+def collect_rest(info_ref, index_ref, ext_ref, tile_ref, start_ref, p0_ref, p1_ref, work_ref):
+    pick(info_ref, 1, info_ref[4], index_ref, ext_ref, tile_ref[...], start_ref, work_ref)
+    p1_ref[...] = work_ref[0]
     p0_ref[...] = work_ref[1]
 
 
-def add_cores(own_ref, other_ref, p1_ref, p2_ref):
-    p1_ref[...] = own_ref[0] + other_ref[1]
-    p2_ref[...] = own_ref[1] + other_ref[2]
+def add_cores(own_ref, other_ref, p2_ref, p3_ref):
+    p2_ref[...] = own_ref[0] + other_ref[2]
+    p3_ref[...] = own_ref[1] + other_ref[3]
 
 
 def add_columns(p0_ref, p1_ref, p2_ref, p3_ref, out_ref):
@@ -114,7 +114,7 @@
         tail = tail + sum_ref[40 * k + 32 : 40 * k + 34, :] * weight
     classes = [jnp.zeros((8, 128), F32)] * 2
     for s in range(4):
-        upper = lax.rem(info_ref[2] - s + 4, 4) >> 1
+        upper = (info_ref[2] ^ s) >> 1
         for t in range(2):
             classes[t] = classes[t] + jnp.where(upper == t, parts[s][160:168, :], 0.0)
     pair = lax.broadcasted_iota(jnp.int32, (8, 128), 0) >> 1
@@ -205,18 +205,18 @@
 
 def slots(info_ref):
     here, core = info_ref[3], info_ref[4]
-    straight = [lax.rem(here - s + 4, 4) * 2 + core for s in range(4)]
-    return straight + [lax.rem(here - s + 4, 4) * 2 + 1 - core for s in range(4)]
+    straight = [(here ^ s) * 2 + core for s in range(4)]
+    return straight + [(here ^ s) * 2 + 1 - core for s in range(4)]
 
 
 def stack(info_ref, refs, anom_ref, incr_ref, inverse_ref):
     for slot, ref in zip(slots(info_ref), refs):
         at = pl.ds(pl.multiple_of(slot * 128, 128), 128)
-        rows = ref[0:128, :]
-        anom_ref[at, :] = rows
+        anom_ref[at, :] = ref[0:128, :]
         incr_ref[:, at] = ref[128:208, :]
-        wide = rows.astype(F32)
-        inverse_ref[at, :] = jnp.broadcast_to((wide[:, 80:81] + wide[:, 81:82]) + wide[:, 82:83], (128, 128))
+    lane = lax.broadcasted_iota(jnp.int32, (128, 128), 0)
+    parts = jnp.where((lane >= 80) & (lane < 83), 1.0, 0.0).astype(BF16)
+    inverse_ref[...] = jnp.dot(anom_ref[...], parts, preferred_element_type=F32)
 
 
 def moved(x_ref, centered_ref, loc_ref, at, batch, anom_ref, incr_ref, inverse_ref, cov_ref, gain_ref):
@@ -264,13 +264,20 @@
         out_ref[10 * z + 8 : 10 * z + 10, :] = work_ref[64 + 2 * z : 66 + 2 * z, :]
 
 
-def shift(a, axis, by, size):
-    return lax.ppermute(a, axis, [(i, (i + by) % size) for i in range(size)])
-
-
-def spread(g):
-    own = [g] + [shift(g, "x", s, 4) for s in (1, 2, 3)]
-    return own + [shift(v, "c", 1, 2) for v in own]
+def swap(a, axis, by, size):
+    return lax.ppermute(a, axis, [(i, i ^ by) for i in range(size)])
+
+
+def swaps(a, axis):
+    got = {s: swap(a, axis, s, 4) for s in (1, 3, 2)}
+    return [a, got[1], got[2], got[3]]
+
+
+def spread(g, beside=()):
+    own = swaps(g, "x")
+    if beside:
+        own[2], *beside = lax.optimization_barrier((own[2], *beside))
+    return own + [swap(v, "c", 1, 2) for v in own], list(beside)
 
 
 def per_device(ensemble, obs_index, obs_weight, obs_value, obs_error_var, loc_class):
@@ -287,11 +294,11 @@
         [pltpu.VMEM((1, 128), F32)],
         name="collect_other",
     )
-    other = shift(other, "c", 1, 2)
+    other = swap(other, "c", 1, 2)
     (own,) = call(collect_own, [((2, CHUNK, 128), F32)], [obs_index, ext, tile], [info], flops=10**9, name="collect_own")
-    p1, p2 = call(add_cores, rows * 2, [own, other], [], name="add_cores")
-    p1, p2 = shift(p1, "x", 1, 4), shift(p2, "x", 2, 4)
-    p0, p3 = call(
+    p2, p3 = call(add_cores, rows * 2, [own, other], [], name="add_cores")
+    p2, p3 = swap(p2, "x", 2, 4), swap(p3, "x", 3, 4)
+    p0, p1 = call(
         collect_rest,
         rows * 2,
         [obs_index, ext, tile, other],
@@ -300,9 +307,9 @@
         flops=10**9,
         name="collect_rest",
     )
-    sums = [p0, p1, p2, shift(p3, "x", 3, 4)]
+    sums = [p0, swap(p1, "x", 1, 4), p2, p3]
     (part,) = call(add_columns, rows, sums, [], name="add_columns")
-    parts = [part] + [shift(part, "y", s, 4) for s in (1, 2, 3)]
+    parts = swaps(part, "y")
     (pack,) = call(
         add_rows,
         [((8, PACK, 128), F32)],
@@ -335,18 +342,27 @@
         name="unpack",
     )
     held = dict(enumerate(zip(both[:4], both[4:])))
-    for batch in range(3):
+    waiting = {}
+    for batch in range(4):
+        soon = sorted(waiting)[:2]
+        beside = [a for at in soon for a in waiting[at]]
+        got, beside = spread(g, beside)
+        for n, at in enumerate(soon):
+            waiting[at] = beside[2 * n : 2 * n + 2]
+        held.update(waiting)
+        if batch == 3:
+            break
         g, *stacked = call(
             next_batch(batch + 1),
             [sent] + blocks,
-            spread(g) + [*held[batch], loc, obs_weight, obs_value, obs_error_var],
+            got + [*held[batch], loc, obs_weight, obs_value, obs_error_var],
             [info],
             work + [wide],
             flops=flops,
             name="next_batch",
         )
-        for at in range(batch + 1, 4):
-            held[at] = call(
+        waiting = {
+            at: call(
                 advance(at, batch),
                 [tall, centered],
                 stacked + [*held[at], loc],
@@ -355,10 +371,12 @@
                 flops=flops,
                 name="advance",
             )
+            for at in range(batch + 1, 4)
+        }
     (state,) = call(
         finish,
         [tall],
-        spread(g) + [*held[3], loc],
+        got + [*held[3], loc],
         [info],
         [pltpu.VMEM(s, d) for s, d in blocks] + work + [pltpu.VMEM((80, 512), F32)],
         flops=flops,

time: 108 us -> 103 us (0.954)
  starting transfers between devices: 45.5 us -> 42 us
  Pallas kernels: 22.9 us -> 20.8 us
    ppermute x35, starting transfers between devices: 45.5 us -> 42 us  [swap(): return lax.ppermute(a, axis, [(i, i ^ by) for i in range(size)])]
    pallas_call x18, Pallas kernels: 22.9 us -> 20.8 us  [call(): pl.pallas_call(body, out_shape=outs, in_specs=[SMEM] * len(scalars) + [VM...]
where the time goes in v2:
time: 103 us; the launch traced here: 102 us
  starting transfers between devices  42 us (41%)
  blocking collectives  26.6 us (26%)
  Pallas kernels  20.8 us (20%)
  waiting for transfers between devices  10.3 us (10%)
  local copies, waits for them, and re-layouts  2.49 us (2%)
    ppermute x35, starting transfers between devices, swap(): return lax.ppermute(a, axis, [(i, i ^ by) for i in range(size)])  42 us
    all_to_all x1, blocking collectives, per_device(): pack = lax.all_to_all(pack, 'z', 0, 0, tiled=True)  26.6 us
    pallas_call x18, Pallas kernels, call(): pl.pallas_call(body, out_shape=outs, in_specs=[SMEM] * len(scalars) + [VM...  20.8 us
    ppermute x35, waiting for transfers between devices, swap(): return lax.ppermute(a, axis, [(i, i ^ by) for i in range(size)])  10.3 us
    unnamed x14, local copies, waits for them, and re-layouts  2.41 us
  transfers between devices with their start and end apart: 35, of which 11 were waited for; matrix products, arithmetic and copies ran while one was open for 0% of the time, Pallas kernels for 9%

profile of v2, /device:TPU:1, one launch (start us, length us, event | category | flops | bytes accessed | tf_op | source)
XLA Modules:
  0.0 102.4 jit_solution(3722957494104240730)
XLA Ops:
  2.5 4.0 %collect_other.1 = (f32[4,168,128]{2,1,0:T(8,128)S(1)}, f32[16,4096]{1,0:T(8,128)S(1)}, f32[8,128]{1,0:T(8,128)S(1)}) custom-call(s32[6]{0:T(128)S(1)} %stack.27.info_ref, s32[4,4,1024]{2,1,0:T(4,128)S(1)} %copy-done.3, f32[10,4096]{1,0:T(8,128)S(1)} %copy-done.5, s32[4,32]{1,0:T(4,128)S(1)} %copy-done.6), custom_call_target="tpu_custom_call" | custom-call | bytes 840192 | tf_op jit(solution)/shard_map/collect_other/pallas_call | solution.py:22
  6.5 3.3 %collective-permute-start = (f32[4,168,128]{2,1,0:T(8,128)S(1)}, f32[4,168,128]{2,1,0:T(8,128)S(1)}, u32[]{:S(2)}, u32[]{:S(2)}) collective-permute-start(f32[4,168,128]{2,1,0:T(8,128)S(1)} %get-tuple-element.60), channel_id=1, source_target_pairs={{0,1},{1,0},{2,3},{3,2},{4,5},{5,4},{6,7},{7,6},{8,9},{9,8},{10,11... | collective-permute-start | bytes 1032200 | tf_op jit(solution)/shard_map/ppermute | solution.py:268
  9.8 2.2 %collect_own.1.own_ref = f32[2,168,128]{2,1,0:T(8,128)S(1)} custom-call(s32[6]{0:T(128)S(1)} %stack.27.info_ref, s32[4,4,1024]{2,1,0:T(4,128)S(1)} %copy-done.3, f32[16,4096]{1,0:T(8,128)S(1)} %get-tuple-element.58.ext_ref, f32[8,128]{1,0:T(8,128)S(1)} %get-tuple-element.59.tile_ref), custom_call_target="tpu_custom_call" | custom-call | flops 1000000000 | bytes 503808 | tf_op jit(solution)/shard_map/collect_own/pallas_call | solution.py:22
  12.0 1.1 %collective-permute-start.2 = (f32[168,128]{1,0:T(8,128)S(1)}, f32[168,128]{1,0:T(8,128)S(1)}, u32[]{:S(2)}, u32[]{:S(2)}) collective-permute-start(f32[168,128]{1,0:T(8,128)S(1)} %get-tuple-element.63), channel_id=1, source_target_pairs={{0,4},{2,6},{4,0},{6,2},{1,5},{3,7},{5,1},{7,3},{8,12},{10,14},{12... | collective-permute-start | bytes 258056 | tf_op jit(solution)/shard_map/ppermute | solution.py:268
  14.0 2.2 %collect_rest.1 = (f32[168,128]{1,0:T(8,128)S(1)}, f32[168,128]{1,0:T(8,128)S(1)}) custom-call(s32[6]{0:T(128)S(1)} %stack.27.info_ref, s32[4,4,1024]{2,1,0:T(4,128)S(1)} %copy-done.3, f32[16,4096]{1,0:T(8,128)S(1)} %get-tuple-element.58.ext_ref, f32[8,128]{1,0:T(8,128)S(1)} %get-tuple-element.59.tile_ref, ...), custom_call_target="tpu_custom_call" | custom-call | flops 1000000000 | bytes 847872 | tf_op jit(solution)/shard_map/collect_rest/pallas_call | solution.py:22
  17.8 2.2 %collective-permute-done.3.p3_ref = f32[168,128]{1,0:T(8,128)S(1)} collective-permute-done((f32[168,128]{1,0:T(8,128)S(1)}, f32[168,128]{1,0:T(8,128)S(1)}, u32[]{:S(2)}, u32[]{:S(2)}) %collective-permute-start.3) | collective-permute-done | bytes 86048 | tf_op jit(solution)/shard_map/ppermute | solution.py:268
  20.0 2.5 %collective-permute-start.6 = (f32[168,128]{1,0:T(8,128)S(1)}, f32[168,128]{1,0:T(8,128)S(1)}, u32[]{:S(2)}, u32[]{:S(2)}) collective-permute-start(f32[168,128]{1,0:T(8,128)S(1)} %add_columns.1.p0_ref), channel_id=1, source_target_pairs={{0,24},{8,16},{16,8},{24,0},{1,25},{9,17},{17,9},{25,1},{2,26},{10... | collective-permute-start | bytes 258056 | tf_op jit(solution)/shard_map/ppermute | solution.py:268
  23.3 1.5 %collective-permute-done.6.p3_ref = f32[168,128]{1,0:T(8,128)S(1)} collective-permute-done((f32[168,128]{1,0:T(8,128)S(1)}, f32[168,128]{1,0:T(8,128)S(1)}, u32[]{:S(2)}, u32[]{:S(2)}) %collective-permute-start.6) | collective-permute-done | bytes 86048 | tf_op jit(solution)/shard_map/ppermute | solution.py:268
  24.8 2.6 %collective-permute-done.5.p2_ref = f32[168,128]{1,0:T(8,128)S(1)} collective-permute-done((f32[168,128]{1,0:T(8,128)S(1)}, f32[168,128]{1,0:T(8,128)S(1)}, u32[]{:S(2)}, u32[]{:S(2)}) %collective-permute-start.5) | collective-permute-done | bytes 86048 | tf_op jit(solution)/shard_map/ppermute | solution.py:268
  28.0 26.6 %all_to_all.5.pack_ref = f32[8,192,128]{2,1,0:T(8,128)S(1)} all-to-all(f32[8,192,128]{2,1,0:T(8,128)S(1)} %add_rows.1), channel_id=1, replica_groups=mesh['z'=8,'y'=4,'x'=4,'c'=2] {'z'}, dimensions={0} | all-to-all | bytes 1572864 | tf_op jit(solution)/shard_map/all_to_all | solution.py:321
  55.3 1.9 %collective-permute-start.9 = (bf16[208,128]{1,0:T(8,128)(2,1)S(1)}, bf16[208,128]{1,0:T(8,128)(2,1)S(1)}, u32[]{:S(2)}, u32[]{:S(2)}) collective-permute-start(bf16[208,128]{1,0:T(8,128)(2,1)S(1)} %first_batch.1.refs_0_), channel_id=1, source_target_pairs={{0,6},{2,4},{4,2},{6,0},{1,7},{3,5},{5,3},{7,1},{8,14},{10,12},{12... | collective-permute-start | bytes 159752 | tf_op jit(solution)/shard_map/ppermute | solution.py:268
  57.2 1.6 %collective-permute-start.8 = (bf16[208,128]{1,0:T(8,128)(2,1)S(1)}, bf16[208,128]{1,0:T(8,128)(2,1)S(1)}, u32[]{:S(2)}, u32[]{:S(2)}) collective-permute-start(bf16[208,128]{1,0:T(8,128)(2,1)S(1)} %first_batch.1.refs_0_), channel_id=1, source_target_pairs={{0,4},{2,6},{4,0},{6,2},{1,5},{3,7},{5,1},{7,3},{8,12},{10,14},{12... | collective-permute-start | bytes 159752 | tf_op jit(solution)/shard_map/ppermute | solution.py:268
  58.9 6.1 %collective-permute-start.10 = (bf16[208,128]{1,0:T(8,128)(2,1)S(1)}, bf16[208,128]{1,0:T(8,128)(2,1)S(1)}, u32[]{:S(2)}, u32[]{:S(2)}) collective-permute-start(bf16[208,128]{1,0:T(8,128)(2,1)S(1)} %first_batch.1.refs_0_), channel_id=1, source_target_pairs={{0,1},{1,0},{2,3},{3,2},{4,5},{5,4},{6,7},{7,6},{8,9},{9,8},{10,11... | collective-permute-start | bytes 159752 | tf_op jit(solution)/shard_map/ppermute | solution.py:268
  64.9 1.2 %collective-permute-start.13 = (bf16[208,128]{1,0:T(8,128)(2,1)S(1)}, bf16[208,128]{1,0:T(8,128)(2,1)S(1)}, u32[]{:S(2)}, u32[]{:S(2)}) collective-permute-start(bf16[208,128]{1,0:T(8,128)(2,1)S(1)} %collective-permute-done.9.refs_3_), channel_id=1, source_target_pairs={{0,1},{1,0},{2,3},{3,2},{4,5},{5,4},{6,7},{7,6},{8,9},{9,8},{10,11... | collective-permute-start | bytes 159752 | tf_op jit(solution)/shard_map/ppermute | solution.py:268
  66.2 2.4 %collective-permute-start.12 = (bf16[208,128]{1,0:T(8,128)(2,1)S(1)}, bf16[208,128]{1,0:T(8,128)(2,1)S(1)}, u32[]{:S(2)}, u32[]{:S(2)}) collective-permute-start(bf16[208,128]{1,0:T(8,128)(2,1)S(1)} %collective-permute-done.8.refs_2_), channel_id=1, source_target_pairs={{0,1},{1,0},{2,3},{3,2},{4,5},{5,4},{6,7},{7,6},{8,9},{9,8},{10,11... | collective-permute-start | bytes 159752 | tf_op jit(solution)/shard_map/ppermute | solution.py:268
  68.6 1.1 %unpack.1 = (f32[80,512]{1,0:T(8,128)S(1)}, f32[80,512]{1,0:T(8,128)S(1)}, f32[80,512]{1,0:T(8,128)S(1)}, f32[80,512]{1,0:T(8,128)S(1)}, bf16[128,512]{1,0:T(8,1...) custom-call(s32[6]{0:T(128)S(1)} %stack.27.info_ref, ...), custom_call_target="tpu_custom_call" | custom-call | flops 67108864 | bytes 2293760 | tf_op jit(solution)/shard_map/unpack/pallas_call | solution.py:22
  69.8 1.4 %next_batch.3 = (bf16[208,128]{1,0:T(8,128)(2,1)S(1)}, bf16[1024,128]{1,0:T(8,128)(2,1)S(1)}, bf16[80,1024]{1,0:T(8,128)(2,1)S(1)}, f32[1024,128]{1,0:T(8,128)S(1)}) custom-call(s32[6]{0:T(128)S(1)} %stack.27.info_ref, bf16[208,128]{1,0:T(8,128)(2,1)S(1)} %first_batch.1.refs_0_, bf16[208,128]{1,0:T(8,128)(2,1)S(1)} %collective-permute-done.7.refs_1_, ...), custom_call_target="tpu_custom_call" | custom-call | flops 268435456 | bytes 2084864 | tf_op jit(solution)/shard_map/next_batch/pallas_call | solution.py:22
  71.2 1.8 %collective-permute-start.15 = (bf16[208,128]{1,0:T(8,128)(2,1)S(1)}, bf16[208,128]{1,0:T(8,128)(2,1)S(1)}, u32[]{:S(2)}, u32[]{:S(2)}) collective-permute-start(bf16[208,128]{1,0:T(8,128)(2,1)S(1)} %get-tuple-element.68.refs_0_), channel_id=1, source_target_pairs={{0,4},{2,6},{4,0},{6,2},{1,5},{3,7},{5,1},{7,3},{8,12},{10,14},{12... | collective-permute-start | bytes 159752 | tf_op jit(solution)/shard_map/ppermute | solution.py:268
  74.0 1.3 %collective-permute-start.17 = (bf16[208,128]{1,0:T(8,128)(2,1)S(1)}, bf16[208,128]{1,0:T(8,128)(2,1)S(1)}, u32[]{:S(2)}, u32[]{:S(2)}) collective-permute-start(bf16[208,128]{1,0:T(8,128)(2,1)S(1)} %get-tuple-element.68.refs_0_), channel_id=1, source_target_pairs={{0,1},{1,0},{2,3},{3,2},{4,5},{5,4},{6,7},{7,6},{8,9},{9,8},{10,11... | collective-permute-start | bytes 159752 | tf_op jit(solution)/shard_map/ppermute | solution.py:268
  77.4 1.3 %collective-permute-start.20 = (bf16[208,128]{1,0:T(8,128)(2,1)S(1)}, bf16[208,128]{1,0:T(8,128)(2,1)S(1)}, u32[]{:S(2)}, u32[]{:S(2)}) collective-permute-start(bf16[208,128]{1,0:T(8,128)(2,1)S(1)} %collective-permute-done.16.refs_3_), channel_id=1, source_target_pairs={{0,1},{1,0},{2,3},{3,2},{4,5},{5,4},{6,7},{7,6},{8,9},{9,8},{10,11... | collective-permute-start | bytes 159752 | tf_op jit(solution)/shard_map/ppermute | solution.py:268
  79.9 1.4 %next_batch.4 = (bf16[208,128]{1,0:T(8,128)(2,1)S(1)}, bf16[1024,128]{1,0:T(8,128)(2,1)S(1)}, bf16[80,1024]{1,0:T(8,128)(2,1)S(1)}, f32[1024,128]{1,0:T(8,128)S(1)}) custom-call(s32[6]{0:T(128)S(1)} %stack.27.info_ref, bf16[208,128]{1,0:T(8,128)(2,1)S(1)} %get-tuple-element.68.refs_0_, bf16[208,128]{1,0:T(8,128)(2,1)S(1)} %collective-permute-done.14.refs_1_, ...), custom_call_target="tpu_custom_call" | custom-call | flops 268435456 | bytes 2084864 | tf_op jit(solution)/shard_map/next_batch/pallas_call | solution.py:22
  81.3 1.5 %collective-permute-start.23 = (bf16[208,128]{1,0:T(8,128)(2,1)S(1)}, bf16[208,128]{1,0:T(8,128)(2,1)S(1)}, u32[]{:S(2)}, u32[]{:S(2)}) collective-permute-start(bf16[208,128]{1,0:T(8,128)(2,1)S(1)} %get-tuple-element.83.refs_0_), channel_id=1, source_target_pairs={{0,6},{2,4},{4,2},{6,0},{1,7},{3,5},{5,3},{7,1},{8,14},{10,12},{12... | collective-permute-start | bytes 159752 | tf_op jit(solution)/shard_map/ppermute | solution.py:268
  83.3 1.4 %collective-permute-start.21 = (bf16[208,128]{1,0:T(8,128)(2,1)S(1)}, bf16[208,128]{1,0:T(8,128)(2,1)S(1)}, u32[]{:S(2)}, u32[]{:S(2)}) collective-permute-start(bf16[208,128]{1,0:T(8,128)(2,1)S(1)} %get-tuple-element.83.refs_0_), channel_id=1, source_target_pairs={{0,2},{2,0},{4,6},{6,4},{1,3},{3,1},{5,7},{7,5},{8,10},{10,8},{12,... | collective-permute-start | bytes 159752 | tf_op jit(solution)/shard_map/ppermute | solution.py:268
  85.3 1.1 %collective-permute-start.24 = (bf16[208,128]{1,0:T(8,128)(2,1)S(1)}, bf16[208,128]{1,0:T(8,128)(2,1)S(1)}, u32[]{:S(2)}, u32[]{:S(2)}) collective-permute-start(bf16[208,128]{1,0:T(8,128)(2,1)S(1)} %get-tuple-element.83.refs_0_), channel_id=1, source_target_pairs={{0,1},{1,0},{2,3},{3,2},{4,5},{5,4},{6,7},{7,6},{8,9},{9,8},{10,11... | collective-permute-start | bytes 159752 | tf_op jit(solution)/shard_map/ppermute | solution.py:268
  87.7 1.4 %collective-permute-start.26 = (bf16[208,128]{1,0:T(8,128)(2,1)S(1)}, bf16[208,128]{1,0:T(8,128)(2,1)S(1)}, u32[]{:S(2)}, u32[]{:S(2)}) collective-permute-start(bf16[208,128]{1,0:T(8,128)(2,1)S(1)} %collective-permute-done.22.refs_2_), channel_id=1, source_target_pairs={{0,1},{1,0},{2,3},{3,2},{4,5},{5,4},{6,7},{7,6},{8,9},{9,8},{10,11... | collective-permute-start | bytes 159752 | tf_op jit(solution)/shard_map/ppermute | solution.py:268
  90.6 1.4 %next_batch.5 = (bf16[208,128]{1,0:T(8,128)(2,1)S(1)}, bf16[1024,128]{1,0:T(8,128)(2,1)S(1)}, bf16[80,1024]{1,0:T(8,128)(2,1)S(1)}, f32[1024,128]{1,0:T(8,128)S(1)}) custom-call(s32[6]{0:T(128)S(1)} %stack.27.info_ref, bf16[208,128]{1,0:T(8,128)(2,1)S(1)} %get-tuple-element.83.refs_0_, bf16[208,128]{1,0:T(8,128)(2,1)S(1)} %collective-permute-done.21.refs_1_, ...), custom_call_target="tpu_custom_call" | custom-call | flops 268435456 | bytes 2084864 | tf_op jit(solution)/shard_map/next_batch/pallas_call | solution.py:22
  92.0 1.3 %collective-permute-start.29 = (bf16[208,128]{1,0:T(8,128)(2,1)S(1)}, bf16[208,128]{1,0:T(8,128)(2,1)S(1)}, u32[]{:S(2)}, u32[]{:S(2)}) collective-permute-start(bf16[208,128]{1,0:T(8,128)(2,1)S(1)} %get-tuple-element.100.refs_0_), channel_id=1, source_target_pairs={{0,4},{2,6},{4,0},{6,2},{1,5},{3,7},{5,1},{7,3},{8,12},{10,14},{12... | collective-permute-start | bytes 159752 | tf_op jit(solution)/shard_map/ppermute | solution.py:268
  93.2 1.1 %collective-permute-start.30 = (bf16[208,128]{1,0:T(8,128)(2,1)S(1)}, bf16[208,128]{1,0:T(8,128)(2,1)S(1)}, u32[]{:S(2)}, u32[]{:S(2)}) collective-permute-start(bf16[208,128]{1,0:T(8,128)(2,1)S(1)} %get-tuple-element.100.refs_0_), channel_id=1, source_target_pairs={{0,6},{2,4},{4,2},{6,0},{1,7},{3,5},{5,3},{7,1},{8,14},{10,12},{12... | collective-permute-start | bytes 159752 | tf_op jit(solution)/shard_map/ppermute | solution.py:268
  94.7 1.2 %collective-permute-start.31 = (bf16[208,128]{1,0:T(8,128)(2,1)S(1)}, bf16[208,128]{1,0:T(8,128)(2,1)S(1)}, u32[]{:S(2)}, u32[]{:S(2)}) collective-permute-start(bf16[208,128]{1,0:T(8,128)(2,1)S(1)} %get-tuple-element.100.refs_0_), channel_id=1, source_target_pairs={{0,1},{1,0},{2,3},{3,2},{4,5},{5,4},{6,7},{7,6},{8,9},{9,8},{10,11... | collective-permute-start | bytes 159752 | tf_op jit(solution)/shard_map/ppermute | solution.py:268
  96.5 1.5 %collective-permute-start.33 = (bf16[208,128]{1,0:T(8,128)(2,1)S(1)}, bf16[208,128]{1,0:T(8,128)(2,1)S(1)}, u32[]{:S(2)}, u32[]{:S(2)}) collective-permute-start(bf16[208,128]{1,0:T(8,128)(2,1)S(1)} %collective-permute-done.29.refs_2_), channel_id=1, source_target_pairs={{0,1},{1,0},{2,3},{3,2},{4,5},{5,4},{6,7},{7,6},{8,9},{9,8},{10,11... | collective-permute-start | bytes 159752 | tf_op jit(solution)/shard_map/ppermute | solution.py:268
  98.1 1.1 %collective-permute-start.34 = (bf16[208,128]{1,0:T(8,128)(2,1)S(1)}, bf16[208,128]{1,0:T(8,128)(2,1)S(1)}, u32[]{:S(2)}, u32[]{:S(2)}) collective-permute-start(bf16[208,128]{1,0:T(8,128)(2,1)S(1)} %collective-permute-done.30.refs_3_), channel_id=1, source_target_pairs={{0,1},{1,0},{2,3},{3,2},{4,5},{5,4},{6,7},{7,6},{8,9},{9,8},{10,11... | collective-permute-start | bytes 159752 | tf_op jit(solution)/shard_map/ppermute | solution.py:268
  100.4 2.0 %finish.1 = f32[80,512]{1,0:T(8,128)} custom-call(s32[6]{0:T(128)S(1)} %stack.27.info_ref, bf16[208,128]{1,0:T(8,128)(2,1)S(1)} %get-tuple-element.100.refs_0_, bf16[208,128]{1,0:T(8,128)(2,1)S(1)} %collective-permute-done.28.refs_1_, bf16[208,128]{1,0:T(8,128)(2,1)S(1)} %collective-permute-done.29.refs_2_, ...), custom_call_target="tpu_custom_call" | custom-call | flops 268435456 | bytes 1146880 | tf_op jit(solution)/shard_map/finish/pallas_call | solution.py:22
  (72 shorter events, 17.7 us)
Async XLA Ops:
  6.5 5.5 %collective-permute-start = (f32[4,168,128]{2,1,0:T(8,128)S(1)}, f32[4,168,128]{2,1,0:T(8,128)S(1)}, u32[]{:S(2)}, u32[]{:S(2)}) collective-permute-start(f32[4,168,128]{2,1,0:T(8,128)S(1)} %get-tuple-element.60), channel_id=1, source_target_pairs={{0,1},{1,0},{2,3},{3,2},{4,5},{5,4},{6,7},{7,6},{8,9},{9,8},{10,11... | collective-permute-start | bytes 1032200 | tf_op jit(solution)/shard_map/ppermute | solution.py:268
  12.0 5.7 %collective-permute-start.2 = (f32[168,128]{1,0:T(8,128)S(1)}, f32[168,128]{1,0:T(8,128)S(1)}, u32[]{:S(2)}, u32[]{:S(2)}) collective-permute-start(f32[168,128]{1,0:T(8,128)S(1)} %get-tuple-element.63), channel_id=1, source_target_pairs={{0,4},{2,6},{4,0},{6,2},{1,5},{3,7},{5,1},{7,3},{8,12},{10,14},{12... | collective-permute-start | bytes 258056 | tf_op jit(solution)/shard_map/ppermute | solution.py:268
  13.1 6.8 %collective-permute-start.3 = (f32[168,128]{1,0:T(8,128)S(1)}, f32[168,128]{1,0:T(8,128)S(1)}, u32[]{:S(2)}, u32[]{:S(2)}) collective-permute-start(f32[168,128]{1,0:T(8,128)S(1)} %get-tuple-element.64), channel_id=1, source_target_pairs={{0,6},{2,4},{4,2},{6,0},{1,7},{3,5},{5,3},{7,1},{8,14},{10,12},{12... | collective-permute-start | bytes 258056 | tf_op jit(solution)/shard_map/ppermute | solution.py:268
  16.2 3.8 %collective-permute-start.1 = (f32[168,128]{1,0:T(8,128)S(1)}, f32[168,128]{1,0:T(8,128)S(1)}, u32[]{:S(2)}, u32[]{:S(2)}) collective-permute-start(f32[168,128]{1,0:T(8,128)S(1)} %get-tuple-element.62), channel_id=1, source_target_pairs={{0,2},{2,0},{4,6},{6,4},{1,3},{3,1},{5,7},{7,5},{8,10},{10,8},{12,... | collective-permute-start | bytes 258056 | tf_op jit(solution)/shard_map/ppermute | solution.py:268
  20.0 4.8 %collective-permute-start.6 = (f32[168,128]{1,0:T(8,128)S(1)}, f32[168,128]{1,0:T(8,128)S(1)}, u32[]{:S(2)}, u32[]{:S(2)}) collective-permute-start(f32[168,128]{1,0:T(8,128)S(1)} %add_columns.1.p0_ref), channel_id=1, source_target_pairs={{0,24},{8,16},{16,8},{24,0},{1,25},{9,17},{17,9},{25,1},{2,26},{10... | collective-permute-start | bytes 258056 | tf_op jit(solution)/shard_map/ppermute | solution.py:268
  22.4 4.9 %collective-permute-start.5 = (f32[168,128]{1,0:T(8,128)S(1)}, f32[168,128]{1,0:T(8,128)S(1)}, u32[]{:S(2)}, u32[]{:S(2)}) collective-permute-start(f32[168,128]{1,0:T(8,128)S(1)} %add_columns.1.p0_ref), channel_id=1, source_target_pairs={{0,16},{8,24},{16,0},{24,8},{1,17},{9,25},{17,1},{25,9},{2,18},{10... | collective-permute-start | bytes 258056 | tf_op jit(solution)/shard_map/ppermute | solution.py:268
  22.8 4.6 %collective-permute-start.4 = (f32[168,128]{1,0:T(8,128)S(1)}, f32[168,128]{1,0:T(8,128)S(1)}, u32[]{:S(2)}, u32[]{:S(2)}) collective-permute-start(f32[168,128]{1,0:T(8,128)S(1)} %add_columns.1.p0_ref), channel_id=1, source_target_pairs={{0,8},{8,0},{16,24},{24,16},{1,9},{9,1},{17,25},{25,17},{2,10},{10... | collective-permute-start | bytes 258056 | tf_op jit(solution)/shard_map/ppermute | solution.py:268
  55.3 9.6 %collective-permute-start.9 = (bf16[208,128]{1,0:T(8,128)(2,1)S(1)}, bf16[208,128]{1,0:T(8,128)(2,1)S(1)}, u32[]{:S(2)}, u32[]{:S(2)}) collective-permute-start(bf16[208,128]{1,0:T(8,128)(2,1)S(1)} %first_batch.1.refs_0_), channel_id=1, source_target_pairs={{0,6},{2,4},{4,2},{6,0},{1,7},{3,5},{5,3},{7,1},{8,14},{10,12},{12... | collective-permute-start | bytes 159752 | tf_op jit(solution)/shard_map/ppermute | solution.py:268
  57.2 9.0 %collective-permute-start.8 = (bf16[208,128]{1,0:T(8,128)(2,1)S(1)}, bf16[208,128]{1,0:T(8,128)(2,1)S(1)}, u32[]{:S(2)}, u32[]{:S(2)}) collective-permute-start(bf16[208,128]{1,0:T(8,128)(2,1)S(1)} %first_batch.1.refs_0_), channel_id=1, source_target_pairs={{0,4},{2,6},{4,0},{6,2},{1,5},{3,7},{5,1},{7,3},{8,12},{10,14},{12... | collective-permute-start | bytes 159752 | tf_op jit(solution)/shard_map/ppermute | solution.py:268
  58.9 9.7 %collective-permute-start.7 = (bf16[208,128]{1,0:T(8,128)(2,1)S(1)}, bf16[208,128]{1,0:T(8,128)(2,1)S(1)}, u32[]{:S(2)}, u32[]{:S(2)}) collective-permute-start(bf16[208,128]{1,0:T(8,128)(2,1)S(1)} %first_batch.1.refs_0_), channel_id=1, source_target_pairs={{0,2},{2,0},{4,6},{6,4},{1,3},{3,1},{5,7},{7,5},{8,10},{10,8},{12,... | collective-permute-start | bytes 159752 | tf_op jit(solution)/shard_map/ppermute | solution.py:268
  58.9 10.8 %collective-permute-start.10 = (bf16[208,128]{1,0:T(8,128)(2,1)S(1)}, bf16[208,128]{1,0:T(8,128)(2,1)S(1)}, u32[]{:S(2)}, u32[]{:S(2)}) collective-permute-start(bf16[208,128]{1,0:T(8,128)(2,1)S(1)} %first_batch.1.refs_0_), channel_id=1, source_target_pairs={{0,1},{1,0},{2,3},{3,2},{4,5},{5,4},{6,7},{7,6},{8,9},{9,8},{10,11... | collective-permute-start | bytes 159752 | tf_op jit(solution)/shard_map/ppermute | solution.py:268
  64.9 4.7 %collective-permute-start.13 = (bf16[208,128]{1,0:T(8,128)(2,1)S(1)}, bf16[208,128]{1,0:T(8,128)(2,1)S(1)}, u32[]{:S(2)}, u32[]{:S(2)}) collective-permute-start(bf16[208,128]{1,0:T(8,128)(2,1)S(1)} %collective-permute-done.9.refs_3_), channel_id=1, source_target_pairs={{0,1},{1,0},{2,3},{3,2},{4,5},{5,4},{6,7},{7,6},{8,9},{9,8},{10,11... | collective-permute-start | bytes 159752 | tf_op jit(solution)/shard_map/ppermute | solution.py:268
  66.2 3.5 %collective-permute-start.12 = (bf16[208,128]{1,0:T(8,128)(2,1)S(1)}, bf16[208,128]{1,0:T(8,128)(2,1)S(1)}, u32[]{:S(2)}, u32[]{:S(2)}) collective-permute-start(bf16[208,128]{1,0:T(8,128)(2,1)S(1)} %collective-permute-done.8.refs_2_), channel_id=1, source_target_pairs={{0,1},{1,0},{2,3},{3,2},{4,5},{5,4},{6,7},{7,6},{8,9},{9,8},{10,11... | collective-permute-start | bytes 159752 | tf_op jit(solution)/shard_map/ppermute | solution.py:268
  71.2 5.3 %collective-permute-start.15 = (bf16[208,128]{1,0:T(8,128)(2,1)S(1)}, bf16[208,128]{1,0:T(8,128)(2,1)S(1)}, u32[]{:S(2)}, u32[]{:S(2)}) collective-permute-start(bf16[208,128]{1,0:T(8,128)(2,1)S(1)} %get-tuple-element.68.refs_0_), channel_id=1, source_target_pairs={{0,4},{2,6},{4,0},{6,2},{1,5},{3,7},{5,1},{7,3},{8,12},{10,14},{12... | collective-permute-start | bytes 159752 | tf_op jit(solution)/shard_map/ppermute | solution.py:268
  73.0 4.4 %collective-permute-start.16 = (bf16[208,128]{1,0:T(8,128)(2,1)S(1)}, bf16[208,128]{1,0:T(8,128)(2,1)S(1)}, u32[]{:S(2)}, u32[]{:S(2)}) collective-permute-start(bf16[208,128]{1,0:T(8,128)(2,1)S(1)} %get-tuple-element.68.refs_0_), channel_id=1, source_target_pairs={{0,6},{2,4},{4,2},{6,0},{1,7},{3,5},{5,3},{7,1},{8,14},{10,12},{12... | collective-permute-start | bytes 159752 | tf_op jit(solution)/shard_map/ppermute | solution.py:268
  73.8 4.9 %collective-permute-start.14 = (bf16[208,128]{1,0:T(8,128)(2,1)S(1)}, bf16[208,128]{1,0:T(8,128)(2,1)S(1)}, u32[]{:S(2)}, u32[]{:S(2)}) collective-permute-start(bf16[208,128]{1,0:T(8,128)(2,1)S(1)} %get-tuple-element.68.refs_0_), channel_id=1, source_target_pairs={{0,2},{2,0},{4,6},{6,4},{1,3},{3,1},{5,7},{7,5},{8,10},{10,8},{12,... | collective-permute-start | bytes 159752 | tf_op jit(solution)/shard_map/ppermute | solution.py:268
  74.0 4.7 %collective-permute-start.17 = (bf16[208,128]{1,0:T(8,128)(2,1)S(1)}, bf16[208,128]{1,0:T(8,128)(2,1)S(1)}, u32[]{:S(2)}, u32[]{:S(2)}) collective-permute-start(bf16[208,128]{1,0:T(8,128)(2,1)S(1)} %get-tuple-element.68.refs_0_), channel_id=1, source_target_pairs={{0,1},{1,0},{2,3},{3,2},{4,5},{5,4},{6,7},{7,6},{8,9},{9,8},{10,11... | collective-permute-start | bytes 159752 | tf_op jit(solution)/shard_map/ppermute | solution.py:268
  76.5 3.1 %collective-permute-start.19 = (bf16[208,128]{1,0:T(8,128)(2,1)S(1)}, bf16[208,128]{1,0:T(8,128)(2,1)S(1)}, u32[]{:S(2)}, u32[]{:S(2)}) collective-permute-start(bf16[208,128]{1,0:T(8,128)(2,1)S(1)} %collective-permute-done.15.refs_2_), channel_id=1, source_target_pairs={{0,1},{1,0},{2,3},{3,2},{4,5},{5,4},{6,7},{7,6},{8,9},{9,8},{10,11... | collective-permute-start | bytes 159752 | tf_op jit(solution)/shard_map/ppermute | solution.py:268
  77.4 2.2 %collective-permute-start.20 = (bf16[208,128]{1,0:T(8,128)(2,1)S(1)}, bf16[208,128]{1,0:T(8,128)(2,1)S(1)}, u32[]{:S(2)}, u32[]{:S(2)}) collective-permute-start(bf16[208,128]{1,0:T(8,128)(2,1)S(1)} %collective-permute-done.16.refs_3_), channel_id=1, source_target_pairs={{0,1},{1,0},{2,3},{3,2},{4,5},{5,4},{6,7},{7,6},{8,9},{9,8},{10,11... | collective-permute-start | bytes 159752 | tf_op jit(solution)/shard_map/ppermute | solution.py:268
  81.3 7.8 %collective-permute-start.23 = (bf16[208,128]{1,0:T(8,128)(2,1)S(1)}, bf16[208,128]{1,0:T(8,128)(2,1)S(1)}, u32[]{:S(2)}, u32[]{:S(2)}) collective-permute-start(bf16[208,128]{1,0:T(8,128)(2,1)S(1)} %get-tuple-element.83.refs_0_), channel_id=1, source_target_pairs={{0,6},{2,4},{4,2},{6,0},{1,7},{3,5},{5,3},{7,1},{8,14},{10,12},{12... | collective-permute-start | bytes 159752 | tf_op jit(solution)/shard_map/ppermute | solution.py:268
  82.8 4.9 %collective-permute-start.22 = (bf16[208,128]{1,0:T(8,128)(2,1)S(1)}, bf16[208,128]{1,0:T(8,128)(2,1)S(1)}, u32[]{:S(2)}, u32[]{:S(2)}) collective-permute-start(bf16[208,128]{1,0:T(8,128)(2,1)S(1)} %get-tuple-element.83.refs_0_), channel_id=1, source_target_pairs={{0,4},{2,6},{4,0},{6,2},{1,5},{3,7},{5,1},{7,3},{8,12},{10,14},{12... | collective-permute-start | bytes 159752 | tf_op jit(solution)/shard_map/ppermute | solution.py:268
  83.3 5.9 %collective-permute-start.21 = (bf16[208,128]{1,0:T(8,128)(2,1)S(1)}, bf16[208,128]{1,0:T(8,128)(2,1)S(1)}, u32[]{:S(2)}, u32[]{:S(2)}) collective-permute-start(bf16[208,128]{1,0:T(8,128)(2,1)S(1)} %get-tuple-element.83.refs_0_), channel_id=1, source_target_pairs={{0,2},{2,0},{4,6},{6,4},{1,3},{3,1},{5,7},{7,5},{8,10},{10,8},{12,... | collective-permute-start | bytes 159752 | tf_op jit(solution)/shard_map/ppermute | solution.py:268
  85.3 4.3 %collective-permute-start.24 = (bf16[208,128]{1,0:T(8,128)(2,1)S(1)}, bf16[208,128]{1,0:T(8,128)(2,1)S(1)}, u32[]{:S(2)}, u32[]{:S(2)}) collective-permute-start(bf16[208,128]{1,0:T(8,128)(2,1)S(1)} %get-tuple-element.83.refs_0_), channel_id=1, source_target_pairs={{0,1},{1,0},{2,3},{3,2},{4,5},{5,4},{6,7},{7,6},{8,9},{9,8},{10,11... | collective-permute-start | bytes 159752 | tf_op jit(solution)/shard_map/ppermute | solution.py:268
  87.7 2.7 %collective-permute-start.26 = (bf16[208,128]{1,0:T(8,128)(2,1)S(1)}, bf16[208,128]{1,0:T(8,128)(2,1)S(1)}, u32[]{:S(2)}, u32[]{:S(2)}) collective-permute-start(bf16[208,128]{1,0:T(8,128)(2,1)S(1)} %collective-permute-done.22.refs_2_), channel_id=1, source_target_pairs={{0,1},{1,0},{2,3},{3,2},{4,5},{5,4},{6,7},{7,6},{8,9},{9,8},{10,11... | collective-permute-start | bytes 159752 | tf_op jit(solution)/shard_map/ppermute | solution.py:268
  89.2 1.2 %collective-permute-start.27 = (bf16[208,128]{1,0:T(8,128)(2,1)S(1)}, bf16[208,128]{1,0:T(8,128)(2,1)S(1)}, u32[]{:S(2)}, u32[]{:S(2)}) collective-permute-start(bf16[208,128]{1,0:T(8,128)(2,1)S(1)} %collective-permute-done.23.refs_3_), channel_id=1, source_target_pairs={{0,1},{1,0},{2,3},{3,2},{4,5},{5,4},{6,7},{7,6},{8,9},{9,8},{10,11... | collective-permute-start | bytes 159752 | tf_op jit(solution)/shard_map/ppermute | solution.py:268
  89.2 1.4 %collective-permute-start.25 = (bf16[208,128]{1,0:T(8,128)(2,1)S(1)}, bf16[208,128]{1,0:T(8,128)(2,1)S(1)}, u32[]{:S(2)}, u32[]{:S(2)}) collective-permute-start(bf16[208,128]{1,0:T(8,128)(2,1)S(1)} %collective-permute-done.21.refs_1_), channel_id=1, source_target_pairs={{0,1},{1,0},{2,3},{3,2},{4,5},{5,4},{6,7},{7,6},{8,9},{9,8},{10,11... | collective-permute-start | bytes 159752 | tf_op jit(solution)/shard_map/ppermute | solution.py:268
  92.0 4.6 %collective-permute-start.29 = (bf16[208,128]{1,0:T(8,128)(2,1)S(1)}, bf16[208,128]{1,0:T(8,128)(2,1)S(1)}, u32[]{:S(2)}, u32[]{:S(2)}) collective-permute-start(bf16[208,128]{1,0:T(8,128)(2,1)S(1)} %get-tuple-element.100.refs_0_), channel_id=1, source_target_pairs={{0,4},{2,6},{4,0},{6,2},{1,5},{3,7},{5,1},{7,3},{8,12},{10,14},{12... | collective-permute-start | bytes 159752 | tf_op jit(solution)/shard_map/ppermute | solution.py:268
  93.2 4.9 %collective-permute-start.30 = (bf16[208,128]{1,0:T(8,128)(2,1)S(1)}, bf16[208,128]{1,0:T(8,128)(2,1)S(1)}, u32[]{:S(2)}, u32[]{:S(2)}) collective-permute-start(bf16[208,128]{1,0:T(8,128)(2,1)S(1)} %get-tuple-element.100.refs_0_), channel_id=1, source_target_pairs={{0,6},{2,4},{4,2},{6,0},{1,7},{3,5},{5,3},{7,1},{8,14},{10,12},{12... | collective-permute-start | bytes 159752 | tf_op jit(solution)/shard_map/ppermute | solution.py:268
  94.3 4.9 %collective-permute-start.28 = (bf16[208,128]{1,0:T(8,128)(2,1)S(1)}, bf16[208,128]{1,0:T(8,128)(2,1)S(1)}, u32[]{:S(2)}, u32[]{:S(2)}) collective-permute-start(bf16[208,128]{1,0:T(8,128)(2,1)S(1)} %get-tuple-element.100.refs_0_), channel_id=1, source_target_pairs={{0,2},{2,0},{4,6},{6,4},{1,3},{3,1},{5,7},{7,5},{8,10},{10,8},{12,... | collective-permute-start | bytes 159752 | tf_op jit(solution)/shard_map/ppermute | solution.py:268
  94.7 4.7 %collective-permute-start.31 = (bf16[208,128]{1,0:T(8,128)(2,1)S(1)}, bf16[208,128]{1,0:T(8,128)(2,1)S(1)}, u32[]{:S(2)}, u32[]{:S(2)}) collective-permute-start(bf16[208,128]{1,0:T(8,128)(2,1)S(1)} %get-tuple-element.100.refs_0_), channel_id=1, source_target_pairs={{0,1},{1,0},{2,3},{3,2},{4,5},{5,4},{6,7},{7,6},{8,9},{9,8},{10,11... | collective-permute-start | bytes 159752 | tf_op jit(solution)/shard_map/ppermute | solution.py:268
  96.5 3.5 %collective-permute-start.33 = (bf16[208,128]{1,0:T(8,128)(2,1)S(1)}, bf16[208,128]{1,0:T(8,128)(2,1)S(1)}, u32[]{:S(2)}, u32[]{:S(2)}) collective-permute-start(bf16[208,128]{1,0:T(8,128)(2,1)S(1)} %collective-permute-done.29.refs_2_), channel_id=1, source_target_pairs={{0,1},{1,0},{2,3},{3,2},{4,5},{5,4},{6,7},{7,6},{8,9},{9,8},{10,11... | collective-permute-start | bytes 159752 | tf_op jit(solution)/shard_map/ppermute | solution.py:268
  98.1 2.0 %collective-permute-start.34 = (bf16[208,128]{1,0:T(8,128)(2,1)S(1)}, bf16[208,128]{1,0:T(8,128)(2,1)S(1)}, u32[]{:S(2)}, u32[]{:S(2)}) collective-permute-start(bf16[208,128]{1,0:T(8,128)(2,1)S(1)} %collective-permute-done.30.refs_3_), channel_id=1, source_target_pairs={{0,1},{1,0},{2,3},{3,2},{4,5},{5,4},{6,7},{7,6},{8,9},{9,8},{10,11... | collective-permute-start | bytes 159752 | tf_op jit(solution)/shard_map/ppermute | solution.py:268
  (10 other events, 80.8 us)

commit v3 on v2

v3 whole, which is shorter than its diff:
```python
import jax
import jax.numpy as jnp
from jax import lax
from jax.experimental import pallas as pl
from jax.experimental.pallas import tpu as pltpu
from jax.sharding import Mesh, PartitionSpec as P

EPS = 1e-05
LOC_TABLE = (1.0, 0.6848958, 0.2083333, 0.0164931, 0.0)
F32 = jnp.float32
BF16 = jnp.bfloat16
VMEM = pl.BlockSpec(memory_space=pltpu.VMEM)

CHUNK = 168
PACK = 192


def place():
    z, y, x, c = [lax.axis_index(n) for n in ("z", "y", "x", "c")]
    block = x * 2 + c
    return [(y * 8 + block) * 4096, block, y, x, c, (y * 8 + block) * 32 + z * 4]


def call(body, shapes, args, placed=True, scratch=(), flops=0, name=None):
    outs = [jax.ShapeDtypeStruct(s, d) for s, d in shapes]
    moved = sum(a.size * a.dtype.itemsize for a in args) + sum(o.size * o.dtype.itemsize for o in outs)
    made = pl.pallas_call(
        (lambda *refs: body(place(), *refs)) if placed else body,
        out_shape=outs,
        in_specs=[VMEM] * len(args),
        out_specs=[VMEM] * len(outs),
        scratch_shapes=list(scratch),
        compiler_params=pltpu.CompilerParams(vmem_limit_bytes=16 * 2**20),
        cost_estimate=pl.CostEstimate(flops=flops, bytes_accessed=moved, transcendentals=0),
        name=name,
    )(*args)
    return list(made)


def lanes(info):
    return pl.ds(pl.multiple_of(info[1] * 128, 128), 128)


def pick(info, first_by, core, index_ref, ext_ref, tile, start_ref, out_refs):
    first = info[0]

    def group(n, carry):
        by = first_by ^ n
        block = (info[3] ^ by) * 2 + core
        here = pl.ds(pl.multiple_of(block * 128, 128), 128)
        for k in range(4):
            local = [index_ref[b, k : k + 1, here] - first for b in range(4)]
            tail = jnp.concatenate([jnp.broadcast_to(v, (2, 128)) for v in local], axis=0)
            wide = [jnp.broadcast_to(v, (8, 128)) for v in local] + [tail]
            for b in range(5):
                low = wide[b] & 127
                high = wide[b] >> 7
                top = 0 if b < 4 else 8
                rows = slice(40 * k + 8 * b, 40 * k + 8 * b + 8)
                acc = jnp.zeros((8, 128), F32) if start_ref is None else start_ref[by, rows, :]
                for part in range(32):
                    source = ext_ref[top : top + 8, part * 128 : (part + 1) * 128]
                    got = jnp.take_along_axis(source, low, axis=1)
                    acc = jnp.where(high == part, got, acc)
                out_refs[n, rows, :] = acc
        rest = tile if start_ref is None else tile + start_ref[by, 160:168, :]
        out_refs[n, 160:168, :] = rest
        return carry

    lax.fori_loop(0, out_refs.shape[0], group, 0)


def collect_other(info, index_ref, ens_ref, class_ref, out_ref, ext_ref, tile_ref, row_ref):
    ext_ref[0:8, :] = ens_ref[0:8, :]
    for r in range(4):
        ext_ref[8 + 2 * r : 10 + 2 * r, :] = ens_ref[8:10, :]
    even = lax.broadcasted_iota(jnp.int32, (32, 16), 0) == 2 * lax.broadcasted_iota(jnp.int32, (32, 16), 1)
    odd = lax.broadcasted_iota(jnp.int32, (32, 16), 0) == 2 * lax.broadcasted_iota(jnp.int32, (32, 16), 1) + 1
    mix = jnp.where(even, 1.0, jnp.where(odd, 8.0, 0.0)).astype(BF16)
    pairs = jnp.dot(class_ref[...].astype(F32).astype(BF16), mix, preferred_element_type=F32)
    for half in range(2):
        for i in range(4):
            row_ref[0:1, 64 * half + 16 * i : 64 * half + 16 * i + 16] = pairs[i : i + 1, :]
    row = lax.broadcasted_iota(jnp.int32, (8, 128), 0) == (info[2] & 1) * 4 + info[3]
    lane = (lax.broadcasted_iota(jnp.int32, (8, 128), 1) >> 6) == info[4]
    tile = jnp.where(row & lane, jnp.broadcast_to(row_ref[...], (8, 128)), 0.0)
    tile_ref[...] = tile
    pick(info, 0, 1 - info[4], index_ref, ext_ref, tile, None, out_ref)


def collect_own(info, index_ref, ext_ref, tile_ref, out_ref):
    pick(info, 2, info[4], index_ref, ext_ref, tile_ref[...], None, out_ref)


def collect_rest(info, index_ref, ext_ref, tile_ref, start_ref, p0_ref, p1_ref, work_ref):
    pick(info, 1, info[4], index_ref, ext_ref, tile_ref[...], start_ref, work_ref)
    p1_ref[...] = work_ref[0]
    p0_ref[...] = work_ref[1]


def add_cores(own_ref, other_ref, p2_ref, p3_ref):
    p2_ref[...] = own_ref[0] + other_ref[2]
    p3_ref[...] = own_ref[1] + other_ref[3]


def add_columns(p0_ref, p1_ref, p2_ref, p3_ref, out_ref):
    out_ref[...] = (p0_ref[...] + p1_ref[...]) + (p2_ref[...] + p3_ref[...])


def add_rows(info, weight_ref, ext_ref, p0_ref, p1_ref, p2_ref, p3_ref, out_ref, sum_ref):
    parts = [p0_ref, p1_ref, p2_ref, p3_ref]
    sum_ref[...] = (p0_ref[0:160, :] + p1_ref[0:160, :]) + (p2_ref[0:160, :] + p3_ref[0:160, :])
    here = lanes(info)
    head = jnp.zeros((8, 128), F32)
    tail = jnp.zeros((2, 128), F32)
    for k in range(4):
        weight = weight_ref[0, k : k + 1, here]
        head = head + sum_ref[40 * k : 40 * k + 8, :] * weight
        tail = tail + sum_ref[40 * k + 32 : 40 * k + 34, :] * weight
    classes = [jnp.zeros((8, 128), F32)] * 2
    for s in range(4):
        upper = (info[2] ^ s) >> 1
        for t in range(2):
            classes[t] = classes[t] + jnp.where(upper == t, parts[s][160:168, :], 0.0)
    pair = lax.broadcasted_iota(jnp.int32, (8, 128), 0) >> 1
    for z in range(8):
        for k in range(4):
            out_ref[z, 24 * k : 24 * k + 24, :] = sum_ref[40 * k + 8 : 40 * k + 32, :]
            out_ref[z, 104 + 6 * k : 110 + 6 * k, :] = sum_ref[40 * k + 34 : 40 * k + 40, :]
        out_ref[z, 96:104, :] = head
        out_ref[z, 128:136, :] = jnp.zeros((8, 128), F32)
        out_ref[z, 128:130, :] = tail
        last = jnp.zeros((8, 128), F32)
        for i in range(4):
            at = slice(512 * z + 128 * i, 512 * z + 128 * i + 128)
            out_ref[z, 136 + 8 * i : 144 + 8 * i, :] = ext_ref[0:8, at]
            last = jnp.where(pair == i, ext_ref[8:16, at], last)
        out_ref[z, 168:176, :] = last
        for t in range(2):
            out_ref[z, 176 + 8 * t : 184 + 8 * t, :] = classes[t]


def increments(prior, value, errvar, out_ref, wide_ref):
    mean = jnp.mean(prior, axis=0, keepdims=True)
    anom = prior - mean
    var = jnp.sum(anom * anom, axis=0, keepdims=True) / 79.0
    inverse = 1.0 / (var + EPS)
    post_var = 1.0 / (inverse + 1.0 / errvar)
    post_mean = post_var * (mean * inverse + value / errvar)
    shrink = jnp.sqrt(errvar / (errvar + var))
    incr = post_mean - mean + (shrink - 1.0) * anom
    rest = inverse / 79.0
    wide_ref[0:80, :] = anom.astype(BF16).astype(F32)
    wide_ref[80:128, :] = jnp.zeros((48, 128), F32)
    for row in (80, 81, 82):
        part = rest.astype(BF16).astype(F32)
        wide_ref[row : row + 1, :] = part
        rest = rest - part
    out_ref[0:128, :] = jnp.transpose(wide_ref[...]).astype(BF16)
    out_ref[128:208, :] = incr.astype(BF16)


def first_batch(info, pack_ref, value_ref, errvar_ref, out_ref, prior_ref, wide_ref):
    for z in range(8):
        prior_ref[8 * z : 8 * z + 8, :] = pack_ref[z, 96:104, :]
        prior_ref[64 + 2 * z : 66 + 2 * z, :] = pack_ref[z, 128:130, :]
    here = lanes(info)
    increments(prior_ref[...], value_ref[0:1, here], errvar_ref[0:1, here], out_ref, wide_ref)


def center(x, out_ref):
    out_ref[0:80, :] = (x - jnp.mean(x, axis=0, keepdims=True)).astype(BF16)
    out_ref[80:128, :] = jnp.zeros((48, x.shape[1]), BF16)


def unpack(info, pack_ref, index_ref, *refs):
    outs, centered, loc_ref = refs[:4], refs[4:8], refs[8]
    here = lanes(info)
    table = pack_ref[:, 176:192, :].reshape(128, 128).astype(BF16)
    for b in range(4):
        for k in range(4):
            at = slice(128 * k, 128 * k + 128)
            for z in range(8):
                if b < 3:
                    outs[b][8 * z : 8 * z + 8, at] = pack_ref[z, 24 * k + 8 * b : 24 * k + 8 * b + 8, :]
                    outs[b][64 + 2 * z : 66 + 2 * z, at] = pack_ref[z, 104 + 6 * k + 2 * b : 106 + 6 * k + 2 * b, :]
                else:
                    outs[b][8 * z : 8 * z + 8, at] = pack_ref[z, 136 + 8 * k : 144 + 8 * k, :]
                    outs[b][64 + 2 * z : 66 + 2 * z, at] = pack_ref[z, 168 + 2 * k : 170 + 2 * k, :]
            if b < 3:
                block = index_ref[b + 1, k : k + 1, here] >> 7
            else:
                block = jnp.full((1, 128), info[5] + k, jnp.int32)
            holder = ((block >> 2) & 7) * 16 + (block >> 6)
            own = (lax.broadcasted_iota(jnp.int32, (128, 128), 0) == holder).astype(F32).astype(BF16)
            found = lax.dot_general(table, own, (((0,), (0,)), ((), ())), preferred_element_type=F32)
            which = ((block >> 5) & 1) * 4 + (block & 3)
            pairs = jnp.zeros((16, 128), F32)
            for i in range(8):
                pairs = pairs + jnp.where(which == i, found[16 * i : 16 * i + 16, :], 0.0)
            odd = jnp.floor(pairs * 0.125)
            for core, level in ((info[4], pairs - 8.0 * odd), (1 - info[4], odd)):
                weights = jnp.zeros((16, 128), F32)
                for n, w in enumerate(LOC_TABLE):
                    weights = weights + jnp.where(level == n, w, 0.0)
                loc_ref[b, pl.ds(pl.multiple_of(core * 16, 16), 16), at] = weights
    for x_ref, c_ref in zip(outs, centered):
        center(x_ref[...], c_ref)


def stack(info, refs, anom_ref, incr_ref, inverse_ref):
    for s, ref in enumerate(refs):
        at = pl.ds(pl.multiple_of((info[3] ^ s) * 128, 128), 128)
        anom_ref[at, :] = ref[0:128, :]
        incr_ref[:, at] = ref[128:208, :]
    lane = lax.broadcasted_iota(jnp.int32, (128, 128), 0)
    parts = jnp.where((lane >= 80) & (lane < 83), 1.0, 0.0).astype(BF16)
    inverse_ref[...] = jnp.dot(anom_ref[...], parts, preferred_element_type=F32)


def change(other, centered_ref, loc_ref, at, batch, anom_ref, incr_ref, inverse_ref, cov_ref, gain_ref):
    cov_ref[...] = jnp.dot(anom_ref[...], centered_ref[...], preferred_element_type=F32)
    for p in range(4):
        row = 16 * other + 4 * batch + p
        rows = slice(128 * p, 128 * p + 128)
        for k in range(4):
            cols = slice(128 * k, 128 * k + 128)
            gain_ref[rows, cols] = ((cov_ref[rows, cols] * inverse_ref[rows, :]) * loc_ref[at, row : row + 1, cols]).astype(BF16)
    return jnp.dot(incr_ref[...], gain_ref[...], preferred_element_type=F32)


def half(at, batch):
    def body(info, *refs):
        c_ref, loc_ref, part_ref, anom_ref, incr_ref, inverse_ref, cov_ref, gain_ref = refs[4:]
        stack(info, refs[:4], anom_ref, incr_ref, inverse_ref)
        part_ref[...] = change(0, c_ref, loc_ref, at, batch, anom_ref, incr_ref, inverse_ref, cov_ref, gain_ref)

    return body


def next_batch(batch):
    def body(info, *refs):
        x_ref, c_ref, loc_ref, part_ref, weight_ref, value_ref, errvar_ref = refs[4:11]
        out_ref, anom_ref, incr_ref, inverse_ref, cov_ref, gain_ref, wide_ref = refs[11:]
        stack(info, refs[:4], anom_ref, incr_ref, inverse_ref)
        blocks = (anom_ref, incr_ref, inverse_ref, cov_ref, gain_ref)
        x = x_ref[...] + (part_ref[...] + change(1, c_ref, loc_ref, batch - 1, batch - 1, *blocks))
        here = lanes(info)
        prior = x[:, 0:128] * weight_ref[batch, 0:1, here]
        for k in range(1, 4):
            prior = prior + x[:, 128 * k : 128 * k + 128] * weight_ref[batch, k : k + 1, here]
        increments(prior, value_ref[batch : batch + 1, here], errvar_ref[batch : batch + 1, here], out_ref, wide_ref)

    return body


def advance(at, batch):
    def body(*refs):
        own, other = refs[:3], refs[3:6]
        x_ref, c_ref, loc_ref, out_ref, c_out_ref, cov_ref, gain_ref = refs[6:]
        first = change(0, c_ref, loc_ref, at, batch, *own, cov_ref, gain_ref)
        x = x_ref[...] + (first + change(1, c_ref, loc_ref, at, batch, *other, cov_ref, gain_ref))
        out_ref[...] = x
        center(x, c_out_ref)

    return body


def finish(info, *refs):
    x_ref, c_ref, loc_ref, part_ref, out_ref, anom_ref, incr_ref, inverse_ref, cov_ref, gain_ref, work_ref = refs[4:]
    stack(info, refs[:4], anom_ref, incr_ref, inverse_ref)
    blocks = (anom_ref, incr_ref, inverse_ref, cov_ref, gain_ref)
    work_ref[...] = x_ref[...] + (part_ref[...] + change(1, c_ref, loc_ref, 3, 3, *blocks))
    for z in range(8):
        out_ref[10 * z : 10 * z + 8, :] = work_ref[8 * z : 8 * z + 8, :]
        out_ref[10 * z + 8 : 10 * z + 10, :] = work_ref[64 + 2 * z : 66 + 2 * z, :]


def swap(a, axis, by, size):
    return lax.ppermute(a, axis, [(i, i ^ by) for i in range(size)])


def swaps(a, axis):
    got = {s: swap(a, axis, s, 4) for s in (1, 3, 2)}
    return [a, got[1], got[2], got[3]]


def spread(g, beside=()):
    own = swaps(g, "x")
    if beside:
        own[2], *beside = lax.optimization_barrier((own[2], *beside))
    return own, [swap(v, "c", 1, 2) for v in own], list(beside)


def per_device(ensemble, obs_index, obs_weight, obs_value, obs_error_var, loc_class):
    rows = [((CHUNK, 128), F32)]
    other, ext, tile = call(
        collect_other,
        [((4, CHUNK, 128), F32), ((16, 4096), F32), ((8, 128), F32)],
        [obs_index, ensemble, loc_class],
        True,
        [pltpu.VMEM((1, 128), F32)],
        name="collect_other",
    )
    other = swap(other, "c", 1, 2)
    (own,) = call(collect_own, [((2, CHUNK, 128), F32)], [obs_index, ext, tile], True, flops=10**9, name="collect_own")
    p2, p3 = call(add_cores, rows * 2, [own, other], False, name="add_cores")
    p2, p3 = swap(p2, "x", 2, 4), swap(p3, "x", 3, 4)
    p0, p1 = call(
        collect_rest,
        rows * 2,
        [obs_index, ext, tile, other],
        True,
        [pltpu.VMEM((2, CHUNK, 128), F32)],
        flops=10**9,
        name="collect_rest",
    )
    sums = [p0, swap(p1, "x", 1, 4), p2, p3]
    (part,) = call(add_columns, rows, sums, False, name="add_columns")
    parts = swaps(part, "y")
    (pack,) = call(
        add_rows,
        [((8, PACK, 128), F32)],
        [obs_weight, ext] + parts,
        True,
        [pltpu.VMEM((160, 128), F32)],
        name="add_rows",
    )
    pack = lax.all_to_all(pack, "z", 0, 0, tiled=True)

    tall, centered, sent = ((80, 512), F32), ((128, 512), BF16), ((208, 128), BF16)
    blocks = [((512, 128), BF16), ((80, 512), BF16), ((512, 128), F32)]
    wide = pltpu.VMEM((128, 128), F32)
    work = [pltpu.VMEM((512, 512), F32), pltpu.VMEM((512, 512), BF16)]
    flops = 2 * 2 * 1024 * 128 * 512
    (g,) = call(
        first_batch,
        [sent],
        [pack, obs_value, obs_error_var],
        True,
        [pltpu.VMEM((80, 128), F32), wide],
        name="first_batch",
    )
    *both, loc = call(
        unpack,
        [tall] * 4 + [centered] * 4 + [((4, 32, 512), F32)],
        [pack, obs_index],
        True,
        flops=2 * 128 * 128 * 2048,
        name="unpack",
    )
    held = dict(enumerate(zip(both[:4], both[4:])))
    waiting = {}
    for batch in range(4):
        soon = sorted(waiting)[:2]
        own, other, beside = spread(g, [a for at in soon for a in waiting[at]])
        for n, at in enumerate(soon):
            waiting[at] = beside[2 * n : 2 * n + 2]
        held.update(waiting)
        at = min(batch, 3)
        part, *first = call(
            half(at, batch),
            [tall] + blocks * (batch < 3),
            own + [held[at][1], loc],
            True,
            work if batch < 3 else [pltpu.VMEM(s, d) for s, d in blocks] + work,
            flops=flops // 2,
            name="half",
        )
        if batch == 3:
            break
        g, *second = call(
            next_batch(batch + 1),
            [sent] + blocks,
            other + [*held[at], loc, part, obs_weight, obs_value, obs_error_var],
            True,
            work + [wide],
            flops=flops // 2,
            name="next_batch",
        )
        waiting = {
            at: call(
                advance(at, batch),
                [tall, centered],
                first + second + [*held[at], loc],
                False,
                work,
                flops=flops,
                name="advance",
            )
            for at in range(batch + 1, 4)
        }
    (state,) = call(
        finish,
        [tall],
        other + [*held[3], loc, part],
        True,
        [pltpu.VMEM(s, d) for s, d in blocks] + work + [pltpu.VMEM((80, 512), F32)],
        flops=flops // 2,
        name="finish",
    )
    return state


def solution(mesh):
    fine = Mesh(mesh.devices.reshape(8, 4, 4, 2), ("z", "y", "x", "c"))
    tiles = ("y", "x", "c")
    in_specs = (P("z", tiles), P(), P(), P(), P(), P(tiles + ("z",), None))
    out_specs = P(None, tiles + ("z",))
    return jax.shard_map(per_device, mesh=fine, in_specs=in_specs, out_specs=out_specs, check_vma=False)
```

time: 103 us -> 97 us (0.942)
  Pallas kernels: 20.8 us -> 17.3 us
  waiting for transfers between devices: 10.3 us -> 8.66 us
    pallas_call x18 -> x22, Pallas kernels: 20.8 us -> 17.3 us  [call(): pl.pallas_call((lambda *refs: body(place(), *refs)) if placed else body,...]
    ppermute x35, waiting for transfers between devices: 10.3 us -> 8.66 us  [swap(): return lax.ppermute(a, axis, [(i, i ^ by) for i in range(size)])]
  transfers between devices with their start and end apart: 35 -> 35, of which waited for: 11 -> 10; matrix products, arithmetic and copies ran while one was open for 0% -> 0% of each run, Pallas kernels for 9% -> 11%
where the time goes in v3:
time: 97 us; the launch traced here: 96.7 us
  starting transfers between devices  41.4 us (43%)
  blocking collectives  26.6 us (27%)
  Pallas kernels  17.3 us (18%)
  waiting for transfers between devices  8.66 us (9%)
  local copies, waits for them, and re-layouts  2.49 us (3%)
    ppermute x35, starting transfers between devices, swap(): return lax.ppermute(a, axis, [(i, i ^ by) for i in range(size)])  41.4 us
    all_to_all x1, blocking collectives, per_device(): pack = lax.all_to_all(pack, 'z', 0, 0, tiled=True)  26.6 us
    pallas_call x22, Pallas kernels, call(): pl.pallas_call((lambda *refs: body(place(), *refs)) if placed else body,...  17.3 us
    ppermute x35, waiting for transfers between devices, swap(): return lax.ppermute(a, axis, [(i, i ^ by) for i in range(size)])  8.66 us
    unnamed x14, local copies, waits for them, and re-layouts  2.49 us
  transfers between devices with their start and end apart: 35, of which 10 were waited for; matrix products, arithmetic and copies ran while one was open for 0% of the time, Pallas kernels for 11%

profile of v3, /device:TPU:1, one launch (start us, length us, event | category | flops | bytes accessed | tf_op | source)
XLA Modules:
  0.0 96.7 jit_solution(8835304396511140759)
XLA Ops:
  0.0 0.9 copy-done.3
  2.5 3.5 %collect_other.1 = (f32[4,168,128]{2,1,0:T(8,128)S(1)}, f32[16,4096]{1,0:T(8,128)S(1)}, f32[8,128]{1,0:T(8,128)S(1)}) custom-call(s32[4,4,1024]{2,1,0:T(4,128)S(1)} %copy-done.4, f32[10,4096]{1,0:T(8,128)S(1)} %copy-done.3, s32[4,32]{1,0:T(4,128)S(1)} %copy-done.6), custom_call_target="tpu_custom_call" | custom-call | bytes 840192 | tf_op jit(solution)/shard_map/collect_other/pallas_call | solution.py:27
  6.0 3.3 %collective-permute-start = (f32[4,168,128]{2,1,0:T(8,128)S(1)}, f32[4,168,128]{2,1,0:T(8,128)S(1)}, u32[]{:S(2)}, u32[]{:S(2)}) collective-permute-start(f32[4,168,128]{2,1,0:T(8,128)S(1)} %get-tuple-element.72), channel_id=1, source_target_pairs={{0,1},{1,0},{2,3},{3,2},{4,5},{5,4},{6,7},{7,6},{8,9},{9,8},{10,11... | collective-permute-start | bytes 1032200 | tf_op jit(solution)/shard_map/ppermute | solution.py:280
  9.3 1.6 %collect_own.1.own_ref = f32[2,168,128]{2,1,0:T(8,128)S(1)} custom-call(s32[4,4,1024]{2,1,0:T(4,128)S(1)} %copy-done.4, f32[16,4096]{1,0:T(8,128)S(1)} %get-tuple-element.70.refs_1_, f32[8,128]{1,0:T(8,128)S(1)} %get-tuple-element.71.refs_2_), custom_call_target="tpu_custom_call" | custom-call | flops 1000000000 | bytes 503808 | tf_op jit(solution)/shard_map/collect_own/pallas_call | solution.py:27
  11.0 1.1 %collective-permute-start.2 = (f32[168,128]{1,0:T(8,128)S(1)}, f32[168,128]{1,0:T(8,128)S(1)}, u32[]{:S(2)}, u32[]{:S(2)}) collective-permute-start(f32[168,128]{1,0:T(8,128)S(1)} %get-tuple-element.75), channel_id=1, source_target_pairs={{0,4},{2,6},{4,0},{6,2},{1,5},{3,7},{5,1},{7,3},{8,12},{10,14},{12... | collective-permute-start | bytes 258056 | tf_op jit(solution)/shard_map/ppermute | solution.py:280
  12.9 1.6 %collect_rest.1 = (f32[168,128]{1,0:T(8,128)S(1)}, f32[168,128]{1,0:T(8,128)S(1)}) custom-call(s32[4,4,1024]{2,1,0:T(4,128)S(1)} %copy-done.4, f32[16,4096]{1,0:T(8,128)S(1)} %get-tuple-element.70.refs_1_, f32[8,128]{1,0:T(8,128)S(1)} %get-tuple-element.71.refs_2_, f32[4,168,128]{2,1,0:T(8,128)S(1)} %collective-permute-done.refs_3_.other_ref), custom_call_target="tpu_custom_call" | custom-call | flops 1000000000 | bytes 847872 | tf_op jit(solution)/shard_map/collect_rest/pallas_call | solution.py:27
  15.4 1.3 %collective-permute-done.2.p2_ref = f32[168,128]{1,0:T(8,128)S(1)} collective-permute-done((f32[168,128]{1,0:T(8,128)S(1)}, f32[168,128]{1,0:T(8,128)S(1)}, u32[]{:S(2)}, u32[]{:S(2)}) %collective-permute-start.2) | collective-permute-done | bytes 86048 | tf_op jit(solution)/shard_map/ppermute | solution.py:280
  16.7 2.2 %collective-permute-done.3.p3_ref = f32[168,128]{1,0:T(8,128)S(1)} collective-permute-done((f32[168,128]{1,0:T(8,128)S(1)}, f32[168,128]{1,0:T(8,128)S(1)}, u32[]{:S(2)}, u32[]{:S(2)}) %collective-permute-start.3) | collective-permute-done | bytes 86048 | tf_op jit(solution)/shard_map/ppermute | solution.py:280
  18.9 1.9 %collective-permute-start.6 = (f32[168,128]{1,0:T(8,128)S(1)}, f32[168,128]{1,0:T(8,128)S(1)}, u32[]{:S(2)}, u32[]{:S(2)}) collective-permute-start(f32[168,128]{1,0:T(8,128)S(1)} %add_columns.1.refs_2_), channel_id=1, source_target_pairs={{0,24},{8,16},{16,8},{24,0},{1,25},{9,17},{17,9},{25,1},{2,26},{10... | collective-permute-start | bytes 258056 | tf_op jit(solution)/shard_map/ppermute | solution.py:280
  21.2 1.1 %collective-permute-start.4 = (f32[168,128]{1,0:T(8,128)S(1)}, f32[168,128]{1,0:T(8,128)S(1)}, u32[]{:S(2)}, u32[]{:S(2)}) collective-permute-start(f32[168,128]{1,0:T(8,128)S(1)} %add_columns.1.refs_2_), channel_id=1, source_target_pairs={{0,8},{8,0},{16,24},{24,16},{1,9},{9,1},{17,25},{25,17},{2,10},{10... | collective-permute-start | bytes 258056 | tf_op jit(solution)/shard_map/ppermute | solution.py:280
  22.2 1.3 %collective-permute-done.6.refs_5_ = f32[168,128]{1,0:T(8,128)S(1)} collective-permute-done((f32[168,128]{1,0:T(8,128)S(1)}, f32[168,128]{1,0:T(8,128)S(1)}, u32[]{:S(2)}, u32[]{:S(2)}) %collective-permute-start.6) | collective-permute-done | bytes 86048 | tf_op jit(solution)/shard_map/ppermute | solution.py:280
  23.5 2.2 %collective-permute-done.5.refs_4_ = f32[168,128]{1,0:T(8,128)S(1)} collective-permute-done((f32[168,128]{1,0:T(8,128)S(1)}, f32[168,128]{1,0:T(8,128)S(1)}, u32[]{:S(2)}, u32[]{:S(2)}) %collective-permute-start.5) | collective-permute-done | bytes 86048 | tf_op jit(solution)/shard_map/ppermute | solution.py:280
  25.9 26.6 %all_to_all.5.refs_0_ = f32[8,192,128]{2,1,0:T(8,128)S(1)} all-to-all(f32[8,192,128]{2,1,0:T(8,128)S(1)} %add_rows.1), channel_id=1, replica_groups=mesh['z'=8,'y'=4,'x'=4,'c'=2] {'z'}, dimensions={0} | all-to-all | bytes 1572864 | tf_op jit(solution)/shard_map/all_to_all | solution.py:329
  52.7 1.9 %collective-permute-start.12 = (bf16[208,128]{1,0:T(8,128)(2,1)S(1)}, bf16[208,128]{1,0:T(8,128)(2,1)S(1)}, u32[]{:S(2)}, u32[]{:S(2)}) collective-permute-start(bf16[208,128]{1,0:T(8,128)(2,1)S(1)} %first_batch.1.refs_0_), channel_id=1, source_target_pairs={{0,6},{2,4},{4,2},{6,0},{1,7},{3,5},{5,3},{7,1},{8,14},{10,12},{12... | collective-permute-start | bytes 159752 | tf_op jit(solution)/shard_map/ppermute | solution.py:280
  54.6 1.6 %collective-permute-start.10 = (bf16[208,128]{1,0:T(8,128)(2,1)S(1)}, bf16[208,128]{1,0:T(8,128)(2,1)S(1)}, u32[]{:S(2)}, u32[]{:S(2)}) collective-permute-start(bf16[208,128]{1,0:T(8,128)(2,1)S(1)} %first_batch.1.refs_0_), channel_id=1, source_target_pairs={{0,4},{2,6},{4,0},{6,2},{1,5},{3,7},{5,1},{7,3},{8,12},{10,14},{12... | collective-permute-start | bytes 159752 | tf_op jit(solution)/shard_map/ppermute | solution.py:280
  56.1 6.1 %collective-permute-start.7 = (bf16[208,128]{1,0:T(8,128)(2,1)S(1)}, bf16[208,128]{1,0:T(8,128)(2,1)S(1)}, u32[]{:S(2)}, u32[]{:S(2)}) collective-permute-start(bf16[208,128]{1,0:T(8,128)(2,1)S(1)} %first_batch.1.refs_0_), channel_id=1, source_target_pairs={{0,1},{1,0},{2,3},{3,2},{4,5},{5,4},{6,7},{7,6},{8,9},{9,8},{10,11... | collective-permute-start | bytes 159752 | tf_op jit(solution)/shard_map/ppermute | solution.py:280
  62.3 1.2 %collective-permute-start.13 = (bf16[208,128]{1,0:T(8,128)(2,1)S(1)}, bf16[208,128]{1,0:T(8,128)(2,1)S(1)}, u32[]{:S(2)}, u32[]{:S(2)}) collective-permute-start(bf16[208,128]{1,0:T(8,128)(2,1)S(1)} %collective-permute-done.12.refs_3_), channel_id=1, source_target_pairs={{0,1},{1,0},{2,3},{3,2},{4,5},{5,4},{6,7},{7,6},{8,9},{9,8},{10,11... | collective-permute-start | bytes 159752 | tf_op jit(solution)/shard_map/ppermute | solution.py:280
  63.5 2.4 %collective-permute-start.11 = (bf16[208,128]{1,0:T(8,128)(2,1)S(1)}, bf16[208,128]{1,0:T(8,128)(2,1)S(1)}, u32[]{:S(2)}, u32[]{:S(2)}) collective-permute-start(bf16[208,128]{1,0:T(8,128)(2,1)S(1)} %collective-permute-done.10.refs_2_), channel_id=1, source_target_pairs={{0,1},{1,0},{2,3},{3,2},{4,5},{5,4},{6,7},{7,6},{8,9},{9,8},{10,11... | collective-permute-start | bytes 159752 | tf_op jit(solution)/shard_map/ppermute | solution.py:280
  67.8 1.8 %collective-permute-start.17 = (bf16[208,128]{1,0:T(8,128)(2,1)S(1)}, bf16[208,128]{1,0:T(8,128)(2,1)S(1)}, u32[]{:S(2)}, u32[]{:S(2)}) collective-permute-start(bf16[208,128]{1,0:T(8,128)(2,1)S(1)} %get-tuple-element.81.refs_0_), channel_id=1, source_target_pairs={{0,4},{2,6},{4,0},{6,2},{1,5},{3,7},{5,1},{7,3},{8,12},{10,14},{12... | collective-permute-start | bytes 159752 | tf_op jit(solution)/shard_map/ppermute | solution.py:280
  69.6 0.9 collective-permute-start.19
  70.5 1.3 %collective-permute-start.14 = (bf16[208,128]{1,0:T(8,128)(2,1)S(1)}, bf16[208,128]{1,0:T(8,128)(2,1)S(1)}, u32[]{:S(2)}, u32[]{:S(2)}) collective-permute-start(bf16[208,128]{1,0:T(8,128)(2,1)S(1)} %get-tuple-element.81.refs_0_), channel_id=1, source_target_pairs={{0,1},{1,0},{2,3},{3,2},{4,5},{5,4},{6,7},{7,6},{8,9},{9,8},{10,11... | collective-permute-start | bytes 159752 | tf_op jit(solution)/shard_map/ppermute | solution.py:280
  74.0 1.3 %collective-permute-start.20 = (bf16[208,128]{1,0:T(8,128)(2,1)S(1)}, bf16[208,128]{1,0:T(8,128)(2,1)S(1)}, u32[]{:S(2)}, u32[]{:S(2)}) collective-permute-start(bf16[208,128]{1,0:T(8,128)(2,1)S(1)} %collective-permute-done.19.refs_3_), channel_id=1, source_target_pairs={{0,1},{1,0},{2,3},{3,2},{4,5},{5,4},{6,7},{7,6},{8,9},{9,8},{10,11... | collective-permute-start | bytes 159752 | tf_op jit(solution)/shard_map/ppermute | solution.py:280
  77.2 1.5 %collective-permute-start.26 = (bf16[208,128]{1,0:T(8,128)(2,1)S(1)}, bf16[208,128]{1,0:T(8,128)(2,1)S(1)}, u32[]{:S(2)}, u32[]{:S(2)}) collective-permute-start(bf16[208,128]{1,0:T(8,128)(2,1)S(1)} %get-tuple-element.100.refs_0_), channel_id=1, source_target_pairs={{0,6},{2,4},{4,2},{6,0},{1,7},{3,5},{5,3},{7,1},{8,14},{10,12},{12... | collective-permute-start | bytes 159752 | tf_op jit(solution)/shard_map/ppermute | solution.py:280
  79.1 1.4 %collective-permute-start.22 = (bf16[208,128]{1,0:T(8,128)(2,1)S(1)}, bf16[208,128]{1,0:T(8,128)(2,1)S(1)}, u32[]{:S(2)}, u32[]{:S(2)}) collective-permute-start(bf16[208,128]{1,0:T(8,128)(2,1)S(1)} %get-tuple-element.100.refs_0_), channel_id=1, source_target_pairs={{0,2},{2,0},{4,6},{6,4},{1,3},{3,1},{5,7},{7,5},{8,10},{10,8},{12,... | collective-permute-start | bytes 159752 | tf_op jit(solution)/shard_map/ppermute | solution.py:280
  81.2 1.1 %collective-permute-start.21 = (bf16[208,128]{1,0:T(8,128)(2,1)S(1)}, bf16[208,128]{1,0:T(8,128)(2,1)S(1)}, u32[]{:S(2)}, u32[]{:S(2)}) collective-permute-start(bf16[208,128]{1,0:T(8,128)(2,1)S(1)} %get-tuple-element.100.refs_0_), channel_id=1, source_target_pairs={{0,1},{1,0},{2,3},{3,2},{4,5},{5,4},{6,7},{7,6},{8,9},{9,8},{10,11... | collective-permute-start | bytes 159752 | tf_op jit(solution)/shard_map/ppermute | solution.py:280
  83.8 1.1 %collective-permute-start.25 = (bf16[208,128]{1,0:T(8,128)(2,1)S(1)}, bf16[208,128]{1,0:T(8,128)(2,1)S(1)}, u32[]{:S(2)}, u32[]{:S(2)}) collective-permute-start(bf16[208,128]{1,0:T(8,128)(2,1)S(1)} %collective-permute-done.24.refs_2_), channel_id=1, source_target_pairs={{0,1},{1,0},{2,3},{3,2},{4,5},{5,4},{6,7},{7,6},{8,9},{9,8},{10,11... | collective-permute-start | bytes 159752 | tf_op jit(solution)/shard_map/ppermute | solution.py:280
  87.0 1.3 %collective-permute-start.31 = (bf16[208,128]{1,0:T(8,128)(2,1)S(1)}, bf16[208,128]{1,0:T(8,128)(2,1)S(1)}, u32[]{:S(2)}, u32[]{:S(2)}) collective-permute-start(bf16[208,128]{1,0:T(8,128)(2,1)S(1)} %get-tuple-element.121.refs_0_), channel_id=1, source_target_pairs={{0,4},{2,6},{4,0},{6,2},{1,5},{3,7},{5,1},{7,3},{8,12},{10,14},{12... | collective-permute-start | bytes 159752 | tf_op jit(solution)/shard_map/ppermute | solution.py:280
  88.3 1.1 %collective-permute-start.33 = (bf16[208,128]{1,0:T(8,128)(2,1)S(1)}, bf16[208,128]{1,0:T(8,128)(2,1)S(1)}, u32[]{:S(2)}, u32[]{:S(2)}) collective-permute-start(bf16[208,128]{1,0:T(8,128)(2,1)S(1)} %get-tuple-element.121.refs_0_), channel_id=1, source_target_pairs={{0,6},{2,4},{4,2},{6,0},{1,7},{3,5},{5,3},{7,1},{8,14},{10,12},{12... | collective-permute-start | bytes 159752 | tf_op jit(solution)/shard_map/ppermute | solution.py:280
  89.8 1.2 %collective-permute-start.28 = (bf16[208,128]{1,0:T(8,128)(2,1)S(1)}, bf16[208,128]{1,0:T(8,128)(2,1)S(1)}, u32[]{:S(2)}, u32[]{:S(2)}) collective-permute-start(bf16[208,128]{1,0:T(8,128)(2,1)S(1)} %get-tuple-element.121.refs_0_), channel_id=1, source_target_pairs={{0,1},{1,0},{2,3},{3,2},{4,5},{5,4},{6,7},{7,6},{8,9},{9,8},{10,11... | collective-permute-start | bytes 159752 | tf_op jit(solution)/shard_map/ppermute | solution.py:280
  91.7 1.4 %collective-permute-start.32 = (bf16[208,128]{1,0:T(8,128)(2,1)S(1)}, bf16[208,128]{1,0:T(8,128)(2,1)S(1)}, u32[]{:S(2)}, u32[]{:S(2)}) collective-permute-start(bf16[208,128]{1,0:T(8,128)(2,1)S(1)} %collective-permute-done.31.refs_2_), channel_id=1, source_target_pairs={{0,1},{1,0},{2,3},{3,2},{4,5},{5,4},{6,7},{7,6},{8,9},{9,8},{10,11... | collective-permute-start | bytes 159752 | tf_op jit(solution)/shard_map/ppermute | solution.py:280
  93.1 1.1 %collective-permute-start.34 = (bf16[208,128]{1,0:T(8,128)(2,1)S(1)}, bf16[208,128]{1,0:T(8,128)(2,1)S(1)}, u32[]{:S(2)}, u32[]{:S(2)}) collective-permute-start(bf16[208,128]{1,0:T(8,128)(2,1)S(1)} %collective-permute-done.33.refs_3_), channel_id=1, source_target_pairs={{0,1},{1,0},{2,3},{3,2},{4,5},{5,4},{6,7},{7,6},{8,9},{9,8},{10,11... | collective-permute-start | bytes 159752 | tf_op jit(solution)/shard_map/ppermute | solution.py:280
  95.5 1.2 %finish.1 = f32[80,512]{1,0:T(8,128)} custom-call(bf16[208,128]{1,0:T(8,128)(2,1)S(1)} %collective-permute-done.28.refs_0_, bf16[208,128]{1,0:T(8,128)(2,1)S(1)} %collective-permute-done.30.refs_1_, bf16[208,128]{1,0:T(8,128)(2,1)S(1)} %collective-permute-done.32.refs_2_, bf16[208,128]{1,0:T(8,128)(2,1)S(1)} %collective-permute-done.34.refs_3_, ...), custom_call_target="tpu_custom_call" | custom-call | flops 134217728 | bytes 1097728 | tf_op jit(solution)/shard_map/finish/pallas_call | solution.py:27
  (75 shorter events, 16.9 us)
Async XLA Ops:
  6.0 5.0 %collective-permute-start = (f32[4,168,128]{2,1,0:T(8,128)S(1)}, f32[4,168,128]{2,1,0:T(8,128)S(1)}, u32[]{:S(2)}, u32[]{:S(2)}) collective-permute-start(f32[4,168,128]{2,1,0:T(8,128)S(1)} %get-tuple-element.72), channel_id=1, source_target_pairs={{0,1},{1,0},{2,3},{3,2},{4,5},{5,4},{6,7},{7,6},{8,9},{9,8},{10,11... | collective-permute-start | bytes 1032200 | tf_op jit(solution)/shard_map/ppermute | solution.py:280
  11.0 5.7 %collective-permute-start.2 = (f32[168,128]{1,0:T(8,128)S(1)}, f32[168,128]{1,0:T(8,128)S(1)}, u32[]{:S(2)}, u32[]{:S(2)}) collective-permute-start(f32[168,128]{1,0:T(8,128)S(1)} %get-tuple-element.75), channel_id=1, source_target_pairs={{0,4},{2,6},{4,0},{6,2},{1,5},{3,7},{5,1},{7,3},{8,12},{10,14},{12... | collective-permute-start | bytes 258056 | tf_op jit(solution)/shard_map/ppermute | solution.py:280
  12.1 6.8 %collective-permute-start.3 = (f32[168,128]{1,0:T(8,128)S(1)}, f32[168,128]{1,0:T(8,128)S(1)}, u32[]{:S(2)}, u32[]{:S(2)}) collective-permute-start(f32[168,128]{1,0:T(8,128)S(1)} %get-tuple-element.76), channel_id=1, source_target_pairs={{0,6},{2,4},{4,2},{6,0},{1,7},{3,5},{5,3},{7,1},{8,14},{10,12},{12... | collective-permute-start | bytes 258056 | tf_op jit(solution)/shard_map/ppermute | solution.py:280
  14.6 4.3 %collective-permute-start.1 = (f32[168,128]{1,0:T(8,128)S(1)}, f32[168,128]{1,0:T(8,128)S(1)}, u32[]{:S(2)}, u32[]{:S(2)}) collective-permute-start(f32[168,128]{1,0:T(8,128)S(1)} %get-tuple-element.74), channel_id=1, source_target_pairs={{0,2},{2,0},{4,6},{6,4},{1,3},{3,1},{5,7},{7,5},{8,10},{10,8},{12,... | collective-permute-start | bytes 258056 | tf_op jit(solution)/shard_map/ppermute | solution.py:280
  18.9 4.6 %collective-permute-start.6 = (f32[168,128]{1,0:T(8,128)S(1)}, f32[168,128]{1,0:T(8,128)S(1)}, u32[]{:S(2)}, u32[]{:S(2)}) collective-permute-start(f32[168,128]{1,0:T(8,128)S(1)} %add_columns.1.refs_2_), channel_id=1, source_target_pairs={{0,24},{8,16},{16,8},{24,0},{1,25},{9,17},{17,9},{25,1},{2,26},{10... | collective-permute-start | bytes 258056 | tf_op jit(solution)/shard_map/ppermute | solution.py:280
  20.8 4.9 %collective-permute-start.5 = (f32[168,128]{1,0:T(8,128)S(1)}, f32[168,128]{1,0:T(8,128)S(1)}, u32[]{:S(2)}, u32[]{:S(2)}) collective-permute-start(f32[168,128]{1,0:T(8,128)S(1)} %add_columns.1.refs_2_), channel_id=1, source_target_pairs={{0,16},{8,24},{16,0},{24,8},{1,17},{9,25},{17,1},{25,9},{2,18},{10... | collective-permute-start | bytes 258056 | tf_op jit(solution)/shard_map/ppermute | solution.py:280
  21.2 4.6 %collective-permute-start.4 = (f32[168,128]{1,0:T(8,128)S(1)}, f32[168,128]{1,0:T(8,128)S(1)}, u32[]{:S(2)}, u32[]{:S(2)}) collective-permute-start(f32[168,128]{1,0:T(8,128)S(1)} %add_columns.1.refs_2_), channel_id=1, source_target_pairs={{0,8},{8,0},{16,24},{24,16},{1,9},{9,1},{17,25},{25,17},{2,10},{10... | collective-permute-start | bytes 258056 | tf_op jit(solution)/shard_map/ppermute | solution.py:280
  52.7 9.6 %collective-permute-start.12 = (bf16[208,128]{1,0:T(8,128)(2,1)S(1)}, bf16[208,128]{1,0:T(8,128)(2,1)S(1)}, u32[]{:S(2)}, u32[]{:S(2)}) collective-permute-start(bf16[208,128]{1,0:T(8,128)(2,1)S(1)} %first_batch.1.refs_0_), channel_id=1, source_target_pairs={{0,6},{2,4},{4,2},{6,0},{1,7},{3,5},{5,3},{7,1},{8,14},{10,12},{12... | collective-permute-start | bytes 159752 | tf_op jit(solution)/shard_map/ppermute | solution.py:280
  54.6 9.0 %collective-permute-start.10 = (bf16[208,128]{1,0:T(8,128)(2,1)S(1)}, bf16[208,128]{1,0:T(8,128)(2,1)S(1)}, u32[]{:S(2)}, u32[]{:S(2)}) collective-permute-start(bf16[208,128]{1,0:T(8,128)(2,1)S(1)} %first_batch.1.refs_0_), channel_id=1, source_target_pairs={{0,4},{2,6},{4,0},{6,2},{1,5},{3,7},{5,1},{7,3},{8,12},{10,14},{12... | collective-permute-start | bytes 159752 | tf_op jit(solution)/shard_map/ppermute | solution.py:280
  56.1 9.8 %collective-permute-start.8 = (bf16[208,128]{1,0:T(8,128)(2,1)S(1)}, bf16[208,128]{1,0:T(8,128)(2,1)S(1)}, u32[]{:S(2)}, u32[]{:S(2)}) collective-permute-start(bf16[208,128]{1,0:T(8,128)(2,1)S(1)} %first_batch.1.refs_0_), channel_id=1, source_target_pairs={{0,2},{2,0},{4,6},{6,4},{1,3},{3,1},{5,7},{7,5},{8,10},{10,8},{12,... | collective-permute-start | bytes 159752 | tf_op jit(solution)/shard_map/ppermute | solution.py:280
  56.1 10.9 %collective-permute-start.7 = (bf16[208,128]{1,0:T(8,128)(2,1)S(1)}, bf16[208,128]{1,0:T(8,128)(2,1)S(1)}, u32[]{:S(2)}, u32[]{:S(2)}) collective-permute-start(bf16[208,128]{1,0:T(8,128)(2,1)S(1)} %first_batch.1.refs_0_), channel_id=1, source_target_pairs={{0,1},{1,0},{2,3},{3,2},{4,5},{5,4},{6,7},{7,6},{8,9},{9,8},{10,11... | collective-permute-start | bytes 159752 | tf_op jit(solution)/shard_map/ppermute | solution.py:280
  62.3 4.8 %collective-permute-start.13 = (bf16[208,128]{1,0:T(8,128)(2,1)S(1)}, bf16[208,128]{1,0:T(8,128)(2,1)S(1)}, u32[]{:S(2)}, u32[]{:S(2)}) collective-permute-start(bf16[208,128]{1,0:T(8,128)(2,1)S(1)} %collective-permute-done.12.refs_3_), channel_id=1, source_target_pairs={{0,1},{1,0},{2,3},{3,2},{4,5},{5,4},{6,7},{7,6},{8,9},{9,8},{10,11... | collective-permute-start | bytes 159752 | tf_op jit(solution)/shard_map/ppermute | solution.py:280
  63.5 3.6 %collective-permute-start.11 = (bf16[208,128]{1,0:T(8,128)(2,1)S(1)}, bf16[208,128]{1,0:T(8,128)(2,1)S(1)}, u32[]{:S(2)}, u32[]{:S(2)}) collective-permute-start(bf16[208,128]{1,0:T(8,128)(2,1)S(1)} %collective-permute-done.10.refs_2_), channel_id=1, source_target_pairs={{0,1},{1,0},{2,3},{3,2},{4,5},{5,4},{6,7},{7,6},{8,9},{9,8},{10,11... | collective-permute-start | bytes 159752 | tf_op jit(solution)/shard_map/ppermute | solution.py:280
  65.9 1.2 %collective-permute-start.9 = (bf16[208,128]{1,0:T(8,128)(2,1)S(1)}, bf16[208,128]{1,0:T(8,128)(2,1)S(1)}, u32[]{:S(2)}, u32[]{:S(2)}) collective-permute-start(bf16[208,128]{1,0:T(8,128)(2,1)S(1)} %collective-permute-done.8.refs_1_), channel_id=1, source_target_pairs={{0,1},{1,0},{2,3},{3,2},{4,5},{5,4},{6,7},{7,6},{8,9},{9,8},{10,11... | collective-permute-start | bytes 159752 | tf_op jit(solution)/shard_map/ppermute | solution.py:280
  67.8 5.5 %collective-permute-start.17 = (bf16[208,128]{1,0:T(8,128)(2,1)S(1)}, bf16[208,128]{1,0:T(8,128)(2,1)S(1)}, u32[]{:S(2)}, u32[]{:S(2)}) collective-permute-start(bf16[208,128]{1,0:T(8,128)(2,1)S(1)} %get-tuple-element.81.refs_0_), channel_id=1, source_target_pairs={{0,4},{2,6},{4,0},{6,2},{1,5},{3,7},{5,1},{7,3},{8,12},{10,14},{12... | collective-permute-start | bytes 159752 | tf_op jit(solution)/shard_map/ppermute | solution.py:280
  69.6 4.4 %collective-permute-start.19 = (bf16[208,128]{1,0:T(8,128)(2,1)S(1)}, bf16[208,128]{1,0:T(8,128)(2,1)S(1)}, u32[]{:S(2)}, u32[]{:S(2)}) collective-permute-start(bf16[208,128]{1,0:T(8,128)(2,1)S(1)} %get-tuple-element.81.refs_0_), channel_id=1, source_target_pairs={{0,6},{2,4},{4,2},{6,0},{1,7},{3,5},{5,3},{7,1},{8,14},{10,12},{12... | collective-permute-start | bytes 159752 | tf_op jit(solution)/shard_map/ppermute | solution.py:280
  70.5 4.8 %collective-permute-start.15 = (bf16[208,128]{1,0:T(8,128)(2,1)S(1)}, bf16[208,128]{1,0:T(8,128)(2,1)S(1)}, u32[]{:S(2)}, u32[]{:S(2)}) collective-permute-start(bf16[208,128]{1,0:T(8,128)(2,1)S(1)} %get-tuple-element.81.refs_0_), channel_id=1, source_target_pairs={{0,2},{2,0},{4,6},{6,4},{1,3},{3,1},{5,7},{7,5},{8,10},{10,8},{12,... | collective-permute-start | bytes 159752 | tf_op jit(solution)/shard_map/ppermute | solution.py:280
  70.5 5.2 %collective-permute-start.14 = (bf16[208,128]{1,0:T(8,128)(2,1)S(1)}, bf16[208,128]{1,0:T(8,128)(2,1)S(1)}, u32[]{:S(2)}, u32[]{:S(2)}) collective-permute-start(bf16[208,128]{1,0:T(8,128)(2,1)S(1)} %get-tuple-element.81.refs_0_), channel_id=1, source_target_pairs={{0,1},{1,0},{2,3},{3,2},{4,5},{5,4},{6,7},{7,6},{8,9},{9,8},{10,11... | collective-permute-start | bytes 159752 | tf_op jit(solution)/shard_map/ppermute | solution.py:280
  73.3 2.8 %collective-permute-start.18 = (bf16[208,128]{1,0:T(8,128)(2,1)S(1)}, bf16[208,128]{1,0:T(8,128)(2,1)S(1)}, u32[]{:S(2)}, u32[]{:S(2)}) collective-permute-start(bf16[208,128]{1,0:T(8,128)(2,1)S(1)} %collective-permute-done.17.refs_2_), channel_id=1, source_target_pairs={{0,1},{1,0},{2,3},{3,2},{4,5},{5,4},{6,7},{7,6},{8,9},{9,8},{10,11... | collective-permute-start | bytes 159752 | tf_op jit(solution)/shard_map/ppermute | solution.py:280
  74.0 2.1 %collective-permute-start.20 = (bf16[208,128]{1,0:T(8,128)(2,1)S(1)}, bf16[208,128]{1,0:T(8,128)(2,1)S(1)}, u32[]{:S(2)}, u32[]{:S(2)}) collective-permute-start(bf16[208,128]{1,0:T(8,128)(2,1)S(1)} %collective-permute-done.19.refs_3_), channel_id=1, source_target_pairs={{0,1},{1,0},{2,3},{3,2},{4,5},{5,4},{6,7},{7,6},{8,9},{9,8},{10,11... | collective-permute-start | bytes 159752 | tf_op jit(solution)/shard_map/ppermute | solution.py:280
  77.2 7.8 %collective-permute-start.26 = (bf16[208,128]{1,0:T(8,128)(2,1)S(1)}, bf16[208,128]{1,0:T(8,128)(2,1)S(1)}, u32[]{:S(2)}, u32[]{:S(2)}) collective-permute-start(bf16[208,128]{1,0:T(8,128)(2,1)S(1)} %get-tuple-element.100.refs_0_), channel_id=1, source_target_pairs={{0,6},{2,4},{4,2},{6,0},{1,7},{3,5},{5,3},{7,1},{8,14},{10,12},{12... | collective-permute-start | bytes 159752 | tf_op jit(solution)/shard_map/ppermute | solution.py:280
  78.6 5.2 %collective-permute-start.24 = (bf16[208,128]{1,0:T(8,128)(2,1)S(1)}, bf16[208,128]{1,0:T(8,128)(2,1)S(1)}, u32[]{:S(2)}, u32[]{:S(2)}) collective-permute-start(bf16[208,128]{1,0:T(8,128)(2,1)S(1)} %get-tuple-element.100.refs_0_), channel_id=1, source_target_pairs={{0,4},{2,6},{4,0},{6,2},{1,5},{3,7},{5,1},{7,3},{8,12},{10,14},{12... | collective-permute-start | bytes 159752 | tf_op jit(solution)/shard_map/ppermute | solution.py:280
  79.1 5.9 %collective-permute-start.22 = (bf16[208,128]{1,0:T(8,128)(2,1)S(1)}, bf16[208,128]{1,0:T(8,128)(2,1)S(1)}, u32[]{:S(2)}, u32[]{:S(2)}) collective-permute-start(bf16[208,128]{1,0:T(8,128)(2,1)S(1)} %get-tuple-element.100.refs_0_), channel_id=1, source_target_pairs={{0,2},{2,0},{4,6},{6,4},{1,3},{3,1},{5,7},{7,5},{8,10},{10,8},{12,... | collective-permute-start | bytes 159752 | tf_op jit(solution)/shard_map/ppermute | solution.py:280
  81.2 4.8 %collective-permute-start.21 = (bf16[208,128]{1,0:T(8,128)(2,1)S(1)}, bf16[208,128]{1,0:T(8,128)(2,1)S(1)}, u32[]{:S(2)}, u32[]{:S(2)}) collective-permute-start(bf16[208,128]{1,0:T(8,128)(2,1)S(1)} %get-tuple-element.100.refs_0_), channel_id=1, source_target_pairs={{0,1},{1,0},{2,3},{3,2},{4,5},{5,4},{6,7},{7,6},{8,9},{9,8},{10,11... | collective-permute-start | bytes 159752 | tf_op jit(solution)/shard_map/ppermute | solution.py:280
  83.8 2.4 %collective-permute-start.25 = (bf16[208,128]{1,0:T(8,128)(2,1)S(1)}, bf16[208,128]{1,0:T(8,128)(2,1)S(1)}, u32[]{:S(2)}, u32[]{:S(2)}) collective-permute-start(bf16[208,128]{1,0:T(8,128)(2,1)S(1)} %collective-permute-done.24.refs_2_), channel_id=1, source_target_pairs={{0,1},{1,0},{2,3},{3,2},{4,5},{5,4},{6,7},{7,6},{8,9},{9,8},{10,11... | collective-permute-start | bytes 159752 | tf_op jit(solution)/shard_map/ppermute | solution.py:280
  85.0 1.4 %collective-permute-start.23 = (bf16[208,128]{1,0:T(8,128)(2,1)S(1)}, bf16[208,128]{1,0:T(8,128)(2,1)S(1)}, u32[]{:S(2)}, u32[]{:S(2)}) collective-permute-start(bf16[208,128]{1,0:T(8,128)(2,1)S(1)} %collective-permute-done.22.refs_1_), channel_id=1, source_target_pairs={{0,1},{1,0},{2,3},{3,2},{4,5},{5,4},{6,7},{7,6},{8,9},{9,8},{10,11... | collective-permute-start | bytes 159752 | tf_op jit(solution)/shard_map/ppermute | solution.py:280
  87.0 4.7 %collective-permute-start.31 = (bf16[208,128]{1,0:T(8,128)(2,1)S(1)}, bf16[208,128]{1,0:T(8,128)(2,1)S(1)}, u32[]{:S(2)}, u32[]{:S(2)}) collective-permute-start(bf16[208,128]{1,0:T(8,128)(2,1)S(1)} %get-tuple-element.121.refs_0_), channel_id=1, source_target_pairs={{0,4},{2,6},{4,0},{6,2},{1,5},{3,7},{5,1},{7,3},{8,12},{10,14},{12... | collective-permute-start | bytes 159752 | tf_op jit(solution)/shard_map/ppermute | solution.py:280
  88.3 4.9 %collective-permute-start.33 = (bf16[208,128]{1,0:T(8,128)(2,1)S(1)}, bf16[208,128]{1,0:T(8,128)(2,1)S(1)}, u32[]{:S(2)}, u32[]{:S(2)}) collective-permute-start(bf16[208,128]{1,0:T(8,128)(2,1)S(1)} %get-tuple-element.121.refs_0_), channel_id=1, source_target_pairs={{0,6},{2,4},{4,2},{6,0},{1,7},{3,5},{5,3},{7,1},{8,14},{10,12},{12... | collective-permute-start | bytes 159752 | tf_op jit(solution)/shard_map/ppermute | solution.py:280
  89.4 4.9 %collective-permute-start.29 = (bf16[208,128]{1,0:T(8,128)(2,1)S(1)}, bf16[208,128]{1,0:T(8,128)(2,1)S(1)}, u32[]{:S(2)}, u32[]{:S(2)}) collective-permute-start(bf16[208,128]{1,0:T(8,128)(2,1)S(1)} %get-tuple-element.121.refs_0_), channel_id=1, source_target_pairs={{0,2},{2,0},{4,6},{6,4},{1,3},{3,1},{5,7},{7,5},{8,10},{10,8},{12,... | collective-permute-start | bytes 159752 | tf_op jit(solution)/shard_map/ppermute | solution.py:280
  89.8 5.2 %collective-permute-start.28 = (bf16[208,128]{1,0:T(8,128)(2,1)S(1)}, bf16[208,128]{1,0:T(8,128)(2,1)S(1)}, u32[]{:S(2)}, u32[]{:S(2)}) collective-permute-start(bf16[208,128]{1,0:T(8,128)(2,1)S(1)} %get-tuple-element.121.refs_0_), channel_id=1, source_target_pairs={{0,1},{1,0},{2,3},{3,2},{4,5},{5,4},{6,7},{7,6},{8,9},{9,8},{10,11... | collective-permute-start | bytes 159752 | tf_op jit(solution)/shard_map/ppermute | solution.py:280
  91.7 3.5 %collective-permute-start.32 = (bf16[208,128]{1,0:T(8,128)(2,1)S(1)}, bf16[208,128]{1,0:T(8,128)(2,1)S(1)}, u32[]{:S(2)}, u32[]{:S(2)}) collective-permute-start(bf16[208,128]{1,0:T(8,128)(2,1)S(1)} %collective-permute-done.31.refs_2_), channel_id=1, source_target_pairs={{0,1},{1,0},{2,3},{3,2},{4,5},{5,4},{6,7},{7,6},{8,9},{9,8},{10,11... | collective-permute-start | bytes 159752 | tf_op jit(solution)/shard_map/ppermute | solution.py:280
  93.1 2.0 %collective-permute-start.34 = (bf16[208,128]{1,0:T(8,128)(2,1)S(1)}, bf16[208,128]{1,0:T(8,128)(2,1)S(1)}, u32[]{:S(2)}, u32[]{:S(2)}) collective-permute-start(bf16[208,128]{1,0:T(8,128)(2,1)S(1)} %collective-permute-done.33.refs_3_), channel_id=1, source_target_pairs={{0,1},{1,0},{2,3},{3,2},{4,5},{5,4},{6,7},{7,6},{8,9},{9,8},{10,11... | collective-permute-start | bytes 159752 | tf_op jit(solution)/shard_map/ppermute | solution.py:280
  (10 other events, 79.8 us)

commit v4 on v3

--- a/solution.py
+++ b/solution.py
@@ -103,13 +103,8 @@
     p3_ref[...] = own_ref[1] + other_ref[3]
 
 
-def add_columns(p0_ref, p1_ref, p2_ref, p3_ref, out_ref):
-    out_ref[...] = (p0_ref[...] + p1_ref[...]) + (p2_ref[...] + p3_ref[...])
-
-
-def add_rows(info, weight_ref, ext_ref, p0_ref, p1_ref, p2_ref, p3_ref, out_ref, sum_ref):
-    parts = [p0_ref, p1_ref, p2_ref, p3_ref]
-    sum_ref[...] = (p0_ref[0:160, :] + p1_ref[0:160, :]) + (p2_ref[0:160, :] + p3_ref[0:160, :])
+def add_columns(info, weight_ref, p0_ref, p1_ref, p2_ref, p3_ref, out_ref, sum_ref):
+    sum_ref[...] = (p0_ref[...] + p1_ref[...]) + (p2_ref[...] + p3_ref[...])
     here = lanes(info)
     head = jnp.zeros((8, 128), F32)
     tail = jnp.zeros((2, 128), F32)
@@ -117,19 +112,25 @@
         weight = weight_ref[0, k : k + 1, here]
         head = head + sum_ref[40 * k : 40 * k + 8, :] * weight
         tail = tail + sum_ref[40 * k + 32 : 40 * k + 34, :] * weight
+        out_ref[24 * k : 24 * k + 24, :] = sum_ref[40 * k + 8 : 40 * k + 32, :]
+        out_ref[104 + 6 * k : 110 + 6 * k, :] = sum_ref[40 * k + 34 : 40 * k + 40, :]
+    out_ref[96:104, :] = head
+    out_ref[128:136, :] = jnp.zeros((8, 128), F32)
+    out_ref[128:130, :] = tail
+    out_ref[136:144, :] = sum_ref[160:168, :]
+
+
+def add_rows(info, ext_ref, p0_ref, p1_ref, p2_ref, p3_ref, out_ref):
+    parts = [p0_ref, p1_ref, p2_ref, p3_ref]
+    total = (p0_ref[0:136, :] + p1_ref[0:136, :]) + (p2_ref[0:136, :] + p3_ref[0:136, :])
     classes = [jnp.zeros((8, 128), F32)] * 2
     for s in range(4):
         upper = (info[2] ^ s) >> 1
         for t in range(2):
-            classes[t] = classes[t] + jnp.where(upper == t, parts[s][160:168, :], 0.0)
+            classes[t] = classes[t] + jnp.where(upper == t, parts[s][136:144, :], 0.0)
     pair = lax.broadcasted_iota(jnp.int32, (8, 128), 0) >> 1
     for z in range(8):
-        for k in range(4):
-            out_ref[z, 24 * k : 24 * k + 24, :] = sum_ref[40 * k + 8 : 40 * k + 32, :]
-            out_ref[z, 104 + 6 * k : 110 + 6 * k, :] = sum_ref[40 * k + 34 : 40 * k + 40, :]
-        out_ref[z, 96:104, :] = head
-        out_ref[z, 128:136, :] = jnp.zeros((8, 128), F32)
-        out_ref[z, 128:130, :] = tail
+        out_ref[z, 0:136, :] = total
         last = jnp.zeros((8, 128), F32)
         for i in range(4):
             at = slice(512 * z + 128 * i, 512 * z + 128 * i + 128)
@@ -316,14 +317,20 @@
         name="collect_rest",
     )
     sums = [p0, swap(p1, "x", 1, 4), p2, p3]
-    (part,) = call(add_columns, rows, sums, False, name="add_columns")
+    (part,) = call(
+        add_columns,
+        [((144, 128), F32)],
+        [obs_weight] + sums,
+        True,
+        [pltpu.VMEM((CHUNK, 128), F32)],
+        name="add_columns",
+    )
     parts = swaps(part, "y")
     (pack,) = call(
         add_rows,
         [((8, PACK, 128), F32)],
-        [obs_weight, ext] + parts,
-        True,
-        [pltpu.VMEM((160, 128), F32)],
+        [ext] + parts,
+        True,
         name="add_rows",
     )
     pack = lax.all_to_all(pack, "z", 0, 0, tiled=True)
@@ -350,13 +357,23 @@
         name="unpack",
     )
     held = dict(enumerate(zip(both[:4], both[4:])))
-    waiting = {}
+    stacked = []
+    beside = ((), ((1, 0), (2, 0)), ((2, 1), (3, 0)), ((3, 1), (3, 2)))
     for batch in range(4):
-        soon = sorted(waiting)[:2]
-        own, other, beside = spread(g, [a for at in soon for a in waiting[at]])
-        for n, at in enumerate(soon):
-            waiting[at] = beside[2 * n : 2 * n + 2]
-        held.update(waiting)
+        news = {}
+        for at, past in beside[batch]:
+            news[at] = call(
+                advance(at, past),
+                [tall, centered],
+                stacked[past] + [*news.get(at, held[at]), loc],
+                False,
+                work,
+                flops=flops,
+                name="advance",
+            )
+        own, other, flat = spread(g, [a for at in news for a in news[at]])
+        for n, at in enumerate(news):
+            held[at] = flat[2 * n : 2 * n + 2]
         at = min(batch, 3)
         part, *first = call(
             half(at, batch),
@@ -378,18 +395,7 @@
             flops=flops // 2,
             name="next_batch",
         )
-        waiting = {
-            at: call(
-                advance(at, batch),
-                [tall, centered],
-                first + second + [*held[at], loc],
-                False,
-                work,
-                flops=flops,
-                name="advance",
-            )
-            for at in range(batch + 1, 4)
-        }
+        stacked.append(first + second)
     (state,) = call(
         finish,
         [tall],

time: 97 us -> 96.1 us (level)
  no operation moved by 1% of the time
where the time goes in v4:
time: 96.1 us; the launch traced here: 95.9 us
  starting transfers between devices  40.9 us (43%)
  blocking collectives  26.7 us (28%)
  Pallas kernels  17.2 us (18%)
  waiting for transfers between devices  8.36 us (9%)
  local copies, waits for them, and re-layouts  2.49 us (3%)
    ppermute x35, starting transfers between devices, swap(): return lax.ppermute(a, axis, [(i, i ^ by) for i in range(size)])  40.9 us
    all_to_all x1, blocking collectives, per_device(): pack = lax.all_to_all(pack, 'z', 0, 0, tiled=True)  26.7 us
    pallas_call x22, Pallas kernels, call(): pl.pallas_call((lambda *refs: body(place(), *refs)) if placed else body,...  17.2 us
    ppermute x35, waiting for transfers between devices, swap(): return lax.ppermute(a, axis, [(i, i ^ by) for i in range(size)])  8.36 us
    unnamed x14, local copies, waits for them, and re-layouts  2.49 us
  transfers between devices with their start and end apart: 35, of which 10 were waited for; matrix products, arithmetic and copies ran while one was open for 0% of the time, Pallas kernels for 11%

profile of v4, /device:TPU:1, one launch (start us, length us, event | category | flops | bytes accessed | tf_op | source)
XLA Modules:
  0.0 95.9 jit_solution(7747034612579167550)
XLA Ops:
  0.0 0.9 copy-done.3
  2.5 3.5 %collect_other.1 = (f32[4,168,128]{2,1,0:T(8,128)S(1)}, f32[16,4096]{1,0:T(8,128)S(1)}, f32[8,128]{1,0:T(8,128)S(1)}) custom-call(s32[4,4,1024]{2,1,0:T(4,128)S(1)} %copy-done.4, f32[10,4096]{1,0:T(8,128)S(1)} %copy-done.3, s32[4,32]{1,0:T(4,128)S(1)} %copy-done.6), custom_call_target="tpu_custom_call" | custom-call | bytes 840192 | tf_op jit(solution)/shard_map/collect_other/pallas_call | solution.py:27
  6.0 3.3 %collective-permute-start = (f32[4,168,128]{2,1,0:T(8,128)S(1)}, f32[4,168,128]{2,1,0:T(8,128)S(1)}, u32[]{:S(2)}, u32[]{:S(2)}) collective-permute-start(f32[4,168,128]{2,1,0:T(8,128)S(1)} %get-tuple-element.72), channel_id=1, source_target_pairs={{0,1},{1,0},{2,3},{3,2},{4,5},{5,4},{6,7},{7,6},{8,9},{9,8},{10,11... | collective-permute-start | bytes 1032200 | tf_op jit(solution)/shard_map/ppermute | solution.py:281
  9.3 1.6 %collect_own.1.own_ref = f32[2,168,128]{2,1,0:T(8,128)S(1)} custom-call(s32[4,4,1024]{2,1,0:T(4,128)S(1)} %copy-done.4, f32[16,4096]{1,0:T(8,128)S(1)} %get-tuple-element.70.refs_1_.refs_0_, f32[8,128]{1,0:T(8,128)S(1)} %get-tuple-element.71.refs_2_), custom_call_target="tpu_custom_call" | custom-call | flops 1000000000 | bytes 503808 | tf_op jit(solution)/shard_map/collect_own/pallas_call | solution.py:27
  11.0 1.1 %collective-permute-start.2 = (f32[168,128]{1,0:T(8,128)S(1)}, f32[168,128]{1,0:T(8,128)S(1)}, u32[]{:S(2)}, u32[]{:S(2)}) collective-permute-start(f32[168,128]{1,0:T(8,128)S(1)} %get-tuple-element.75), channel_id=1, source_target_pairs={{0,4},{2,6},{4,0},{6,2},{1,5},{3,7},{5,1},{7,3},{8,12},{10,14},{12... | collective-permute-start | bytes 258056 | tf_op jit(solution)/shard_map/ppermute | solution.py:281
  12.9 1.6 %collect_rest.1 = (f32[168,128]{1,0:T(8,128)S(1)}, f32[168,128]{1,0:T(8,128)S(1)}) custom-call(s32[4,4,1024]{2,1,0:T(4,128)S(1)} %copy-done.4, f32[16,4096]{1,0:T(8,128)S(1)} %get-tuple-element.70.refs_1_.refs_0_, f32[8,128]{1,0:T(8,128)S(1)} %get-tuple-element.71.refs_2_, f32[4,168,128]{2,1,0:T(8,128)S(1)} %collective-permute-done.refs_3_.other_ref), custom_call_target="tpu_custom_call" | custom-call | flops 1000000000 | bytes 847872 | tf_op jit(solution)/shard_map/collect_rest/pallas_call | solution.py:27
  14.6 0.9 collective-permute-start.1
  15.4 1.3 %collective-permute-done.2.refs_3_ = f32[168,128]{1,0:T(8,128)S(1)} collective-permute-done((f32[168,128]{1,0:T(8,128)S(1)}, f32[168,128]{1,0:T(8,128)S(1)}, u32[]{:S(2)}, u32[]{:S(2)}) %collective-permute-start.2) | collective-permute-done | bytes 86048 | tf_op jit(solution)/shard_map/ppermute | solution.py:281
  16.7 2.2 %collective-permute-done.3.refs_4_ = f32[168,128]{1,0:T(8,128)S(1)} collective-permute-done((f32[168,128]{1,0:T(8,128)S(1)}, f32[168,128]{1,0:T(8,128)S(1)}, u32[]{:S(2)}, u32[]{:S(2)}) %collective-permute-start.3) | collective-permute-done | bytes 86048 | tf_op jit(solution)/shard_map/ppermute | solution.py:281
  18.9 1.9 %collective-permute-start.6 = (f32[144,128]{1,0:T(8,128)S(1)}, f32[144,128]{1,0:T(8,128)S(1)}, u32[]{:S(2)}, u32[]{:S(2)}) collective-permute-start(f32[144,128]{1,0:T(8,128)S(1)} %add_columns.1.refs_1_), channel_id=1, source_target_pairs={{0,24},{8,16},{16,8},{24,0},{1,25},{9,17},{17,9},{25,1},{2,26},{10... | collective-permute-start | bytes 221192 | tf_op jit(solution)/shard_map/ppermute | solution.py:281
  21.2 1.1 %collective-permute-start.4 = (f32[144,128]{1,0:T(8,128)S(1)}, f32[144,128]{1,0:T(8,128)S(1)}, u32[]{:S(2)}, u32[]{:S(2)}) collective-permute-start(f32[144,128]{1,0:T(8,128)S(1)} %add_columns.1.refs_1_), channel_id=1, source_target_pairs={{0,8},{8,0},{16,24},{24,16},{1,9},{9,1},{17,25},{25,17},{2,10},{10... | collective-permute-start | bytes 221192 | tf_op jit(solution)/shard_map/ppermute | solution.py:281
  22.3 1.2 %collective-permute-done.6.refs_4_ = f32[144,128]{1,0:T(8,128)S(1)} collective-permute-done((f32[144,128]{1,0:T(8,128)S(1)}, f32[144,128]{1,0:T(8,128)S(1)}, u32[]{:S(2)}, u32[]{:S(2)}) %collective-permute-start.6) | collective-permute-done | bytes 73760 | tf_op jit(solution)/shard_map/ppermute | solution.py:281
  23.4 2.1 %collective-permute-done.5.refs_3_ = f32[144,128]{1,0:T(8,128)S(1)} collective-permute-done((f32[144,128]{1,0:T(8,128)S(1)}, f32[144,128]{1,0:T(8,128)S(1)}, u32[]{:S(2)}, u32[]{:S(2)}) %collective-permute-start.5) | collective-permute-done | bytes 73760 | tf_op jit(solution)/shard_map/ppermute | solution.py:281
  25.6 26.7 %all_to_all.5.refs_0_ = f32[8,192,128]{2,1,0:T(8,128)S(1)} all-to-all(f32[8,192,128]{2,1,0:T(8,128)S(1)} %add_rows.1), channel_id=1, replica_groups=mesh['z'=8,'y'=4,'x'=4,'c'=2] {'z'}, dimensions={0} | all-to-all | bytes 1572864 | tf_op jit(solution)/shard_map/all_to_all | solution.py:336
  52.4 1.9 %collective-permute-start.12 = (bf16[208,128]{1,0:T(8,128)(2,1)S(1)}, bf16[208,128]{1,0:T(8,128)(2,1)S(1)}, u32[]{:S(2)}, u32[]{:S(2)}) collective-permute-start(bf16[208,128]{1,0:T(8,128)(2,1)S(1)} %first_batch.1.refs_0_), channel_id=1, source_target_pairs={{0,6},{2,4},{4,2},{6,0},{1,7},{3,5},{5,3},{7,1},{8,14},{10,12},{12... | collective-permute-start | bytes 159752 | tf_op jit(solution)/shard_map/ppermute | solution.py:281
  54.3 1.6 %collective-permute-start.10 = (bf16[208,128]{1,0:T(8,128)(2,1)S(1)}, bf16[208,128]{1,0:T(8,128)(2,1)S(1)}, u32[]{:S(2)}, u32[]{:S(2)}) collective-permute-start(bf16[208,128]{1,0:T(8,128)(2,1)S(1)} %first_batch.1.refs_0_), channel_id=1, source_target_pairs={{0,4},{2,6},{4,0},{6,2},{1,5},{3,7},{5,1},{7,3},{8,12},{10,14},{12... | collective-permute-start | bytes 159752 | tf_op jit(solution)/shard_map/ppermute | solution.py:281
  56.0 6.0 %collective-permute-start.7 = (bf16[208,128]{1,0:T(8,128)(2,1)S(1)}, bf16[208,128]{1,0:T(8,128)(2,1)S(1)}, u32[]{:S(2)}, u32[]{:S(2)}) collective-permute-start(bf16[208,128]{1,0:T(8,128)(2,1)S(1)} %first_batch.1.refs_0_), channel_id=1, source_target_pairs={{0,1},{1,0},{2,3},{3,2},{4,5},{5,4},{6,7},{7,6},{8,9},{9,8},{10,11... | collective-permute-start | bytes 159752 | tf_op jit(solution)/shard_map/ppermute | solution.py:281
  62.0 1.2 %collective-permute-start.13 = (bf16[208,128]{1,0:T(8,128)(2,1)S(1)}, bf16[208,128]{1,0:T(8,128)(2,1)S(1)}, u32[]{:S(2)}, u32[]{:S(2)}) collective-permute-start(bf16[208,128]{1,0:T(8,128)(2,1)S(1)} %collective-permute-done.12.refs_3_), channel_id=1, source_target_pairs={{0,1},{1,0},{2,3},{3,2},{4,5},{5,4},{6,7},{7,6},{8,9},{9,8},{10,11... | collective-permute-start | bytes 159752 | tf_op jit(solution)/shard_map/ppermute | solution.py:281
  63.3 2.4 %collective-permute-start.11 = (bf16[208,128]{1,0:T(8,128)(2,1)S(1)}, bf16[208,128]{1,0:T(8,128)(2,1)S(1)}, u32[]{:S(2)}, u32[]{:S(2)}) collective-permute-start(bf16[208,128]{1,0:T(8,128)(2,1)S(1)} %collective-permute-done.10.refs_2_), channel_id=1, source_target_pairs={{0,1},{1,0},{2,3},{3,2},{4,5},{5,4},{6,7},{7,6},{8,9},{9,8},{10,11... | collective-permute-start | bytes 159752 | tf_op jit(solution)/shard_map/ppermute | solution.py:281
  67.6 1.8 %collective-permute-start.17 = (bf16[208,128]{1,0:T(8,128)(2,1)S(1)}, bf16[208,128]{1,0:T(8,128)(2,1)S(1)}, u32[]{:S(2)}, u32[]{:S(2)}) collective-permute-start(bf16[208,128]{1,0:T(8,128)(2,1)S(1)} %get-tuple-element.81.refs_0_), channel_id=1, source_target_pairs={{0,4},{2,6},{4,0},{6,2},{1,5},{3,7},{5,1},{7,3},{8,12},{10,14},{12... | collective-permute-start | bytes 159752 | tf_op jit(solution)/shard_map/ppermute | solution.py:281
  69.4 0.9 collective-permute-start.19
  70.3 1.3 %collective-permute-start.14 = (bf16[208,128]{1,0:T(8,128)(2,1)S(1)}, bf16[208,128]{1,0:T(8,128)(2,1)S(1)}, u32[]{:S(2)}, u32[]{:S(2)}) collective-permute-start(bf16[208,128]{1,0:T(8,128)(2,1)S(1)} %get-tuple-element.81.refs_0_), channel_id=1, source_target_pairs={{0,1},{1,0},{2,3},{3,2},{4,5},{5,4},{6,7},{7,6},{8,9},{9,8},{10,11... | collective-permute-start | bytes 159752 | tf_op jit(solution)/shard_map/ppermute | solution.py:281
  73.8 1.3 %collective-permute-start.20 = (bf16[208,128]{1,0:T(8,128)(2,1)S(1)}, bf16[208,128]{1,0:T(8,128)(2,1)S(1)}, u32[]{:S(2)}, u32[]{:S(2)}) collective-permute-start(bf16[208,128]{1,0:T(8,128)(2,1)S(1)} %collective-permute-done.19.refs_3_), channel_id=1, source_target_pairs={{0,1},{1,0},{2,3},{3,2},{4,5},{5,4},{6,7},{7,6},{8,9},{9,8},{10,11... | collective-permute-start | bytes 159752 | tf_op jit(solution)/shard_map/ppermute | solution.py:281
  76.9 1.3 %collective-permute-start.24 = (bf16[208,128]{1,0:T(8,128)(2,1)S(1)}, bf16[208,128]{1,0:T(8,128)(2,1)S(1)}, u32[]{:S(2)}, u32[]{:S(2)}) collective-permute-start(bf16[208,128]{1,0:T(8,128)(2,1)S(1)} %get-tuple-element.100.refs_0_), channel_id=1, source_target_pairs={{0,4},{2,6},{4,0},{6,2},{1,5},{3,7},{5,1},{7,3},{8,12},{10,14},{12... | collective-permute-start | bytes 159752 | tf_op jit(solution)/shard_map/ppermute | solution.py:281
  78.2 1.3 %collective-permute-start.26 = (bf16[208,128]{1,0:T(8,128)(2,1)S(1)}, bf16[208,128]{1,0:T(8,128)(2,1)S(1)}, u32[]{:S(2)}, u32[]{:S(2)}) collective-permute-start(bf16[208,128]{1,0:T(8,128)(2,1)S(1)} %get-tuple-element.100.refs_0_), channel_id=1, source_target_pairs={{0,6},{2,4},{4,2},{6,0},{1,7},{3,5},{5,3},{7,1},{8,14},{10,12},{12... | collective-permute-start | bytes 159752 | tf_op jit(solution)/shard_map/ppermute | solution.py:281
  80.4 1.1 %collective-permute-start.21 = (bf16[208,128]{1,0:T(8,128)(2,1)S(1)}, bf16[208,128]{1,0:T(8,128)(2,1)S(1)}, u32[]{:S(2)}, u32[]{:S(2)}) collective-permute-start(bf16[208,128]{1,0:T(8,128)(2,1)S(1)} %get-tuple-element.100.refs_0_), channel_id=1, source_target_pairs={{0,1},{1,0},{2,3},{3,2},{4,5},{5,4},{6,7},{7,6},{8,9},{9,8},{10,11... | collective-permute-start | bytes 159752 | tf_op jit(solution)/shard_map/ppermute | solution.py:281
  82.8 1.1 %collective-permute-start.27 = (bf16[208,128]{1,0:T(8,128)(2,1)S(1)}, bf16[208,128]{1,0:T(8,128)(2,1)S(1)}, u32[]{:S(2)}, u32[]{:S(2)}) collective-permute-start(bf16[208,128]{1,0:T(8,128)(2,1)S(1)} %collective-permute-done.26.refs_3_), channel_id=1, source_target_pairs={{0,1},{1,0},{2,3},{3,2},{4,5},{5,4},{6,7},{7,6},{8,9},{9,8},{10,11... | collective-permute-start | bytes 159752 | tf_op jit(solution)/shard_map/ppermute | solution.py:281
  86.1 1.4 %collective-permute-start.31 = (bf16[208,128]{1,0:T(8,128)(2,1)S(1)}, bf16[208,128]{1,0:T(8,128)(2,1)S(1)}, u32[]{:S(2)}, u32[]{:S(2)}) collective-permute-start(bf16[208,128]{1,0:T(8,128)(2,1)S(1)} %get-tuple-element.119.refs_0_), channel_id=1, source_target_pairs={{0,4},{2,6},{4,0},{6,2},{1,5},{3,7},{5,1},{7,3},{8,12},{10,14},{12... | collective-permute-start | bytes 159752 | tf_op jit(solution)/shard_map/ppermute | solution.py:281
  87.5 1.3 %collective-permute-start.33 = (bf16[208,128]{1,0:T(8,128)(2,1)S(1)}, bf16[208,128]{1,0:T(8,128)(2,1)S(1)}, u32[]{:S(2)}, u32[]{:S(2)}) collective-permute-start(bf16[208,128]{1,0:T(8,128)(2,1)S(1)} %get-tuple-element.119.refs_0_), channel_id=1, source_target_pairs={{0,6},{2,4},{4,2},{6,0},{1,7},{3,5},{5,3},{7,1},{8,14},{10,12},{12... | collective-permute-start | bytes 159752 | tf_op jit(solution)/shard_map/ppermute | solution.py:281
  89.6 1.5 %collective-permute-start.28 = (bf16[208,128]{1,0:T(8,128)(2,1)S(1)}, bf16[208,128]{1,0:T(8,128)(2,1)S(1)}, u32[]{:S(2)}, u32[]{:S(2)}) collective-permute-start(bf16[208,128]{1,0:T(8,128)(2,1)S(1)} %get-tuple-element.119.refs_0_), channel_id=1, source_target_pairs={{0,1},{1,0},{2,3},{3,2},{4,5},{5,4},{6,7},{7,6},{8,9},{9,8},{10,11... | collective-permute-start | bytes 159752 | tf_op jit(solution)/shard_map/ppermute | solution.py:281
  92.2 1.2 %collective-permute-start.34 = (bf16[208,128]{1,0:T(8,128)(2,1)S(1)}, bf16[208,128]{1,0:T(8,128)(2,1)S(1)}, u32[]{:S(2)}, u32[]{:S(2)}) collective-permute-start(bf16[208,128]{1,0:T(8,128)(2,1)S(1)} %collective-permute-done.33.refs_3_), channel_id=1, source_target_pairs={{0,1},{1,0},{2,3},{3,2},{4,5},{5,4},{6,7},{7,6},{8,9},{9,8},{10,11... | collective-permute-start | bytes 159752 | tf_op jit(solution)/shard_map/ppermute | solution.py:281
  94.7 1.2 %finish.1 = f32[80,512]{1,0:T(8,128)} custom-call(bf16[208,128]{1,0:T(8,128)(2,1)S(1)} %collective-permute-done.28.refs_0_, bf16[208,128]{1,0:T(8,128)(2,1)S(1)} %collective-permute-done.30.refs_1_, bf16[208,128]{1,0:T(8,128)(2,1)S(1)} %collective-permute-done.32.refs_2_, bf16[208,128]{1,0:T(8,128)(2,1)S(1)} %collective-permute-done.34.refs_3_, ...), custom_call_target="tpu_custom_call" | custom-call | flops 134217728 | bytes 1097728 | tf_op jit(solution)/shard_map/finish/pallas_call | solution.py:27
  (75 shorter events, 16.5 us)
Async XLA Ops:
  6.0 5.0 %collective-permute-start = (f32[4,168,128]{2,1,0:T(8,128)S(1)}, f32[4,168,128]{2,1,0:T(8,128)S(1)}, u32[]{:S(2)}, u32[]{:S(2)}) collective-permute-start(f32[4,168,128]{2,1,0:T(8,128)S(1)} %get-tuple-element.72), channel_id=1, source_target_pairs={{0,1},{1,0},{2,3},{3,2},{4,5},{5,4},{6,7},{7,6},{8,9},{9,8},{10,11... | collective-permute-start | bytes 1032200 | tf_op jit(solution)/shard_map/ppermute | solution.py:281
  11.0 5.7 %collective-permute-start.2 = (f32[168,128]{1,0:T(8,128)S(1)}, f32[168,128]{1,0:T(8,128)S(1)}, u32[]{:S(2)}, u32[]{:S(2)}) collective-permute-start(f32[168,128]{1,0:T(8,128)S(1)} %get-tuple-element.75), channel_id=1, source_target_pairs={{0,4},{2,6},{4,0},{6,2},{1,5},{3,7},{5,1},{7,3},{8,12},{10,14},{12... | collective-permute-start | bytes 258056 | tf_op jit(solution)/shard_map/ppermute | solution.py:281
  12.1 6.8 %collective-permute-start.3 = (f32[168,128]{1,0:T(8,128)S(1)}, f32[168,128]{1,0:T(8,128)S(1)}, u32[]{:S(2)}, u32[]{:S(2)}) collective-permute-start(f32[168,128]{1,0:T(8,128)S(1)} %get-tuple-element.76), channel_id=1, source_target_pairs={{0,6},{2,4},{4,2},{6,0},{1,7},{3,5},{5,3},{7,1},{8,14},{10,12},{12... | collective-permute-start | bytes 258056 | tf_op jit(solution)/shard_map/ppermute | solution.py:281
  14.6 4.3 %collective-permute-start.1 = (f32[168,128]{1,0:T(8,128)S(1)}, f32[168,128]{1,0:T(8,128)S(1)}, u32[]{:S(2)}, u32[]{:S(2)}) collective-permute-start(f32[168,128]{1,0:T(8,128)S(1)} %get-tuple-element.74), channel_id=1, source_target_pairs={{0,2},{2,0},{4,6},{6,4},{1,3},{3,1},{5,7},{7,5},{8,10},{10,8},{12,... | collective-permute-start | bytes 258056 | tf_op jit(solution)/shard_map/ppermute | solution.py:281
  18.9 4.5 %collective-permute-start.6 = (f32[144,128]{1,0:T(8,128)S(1)}, f32[144,128]{1,0:T(8,128)S(1)}, u32[]{:S(2)}, u32[]{:S(2)}) collective-permute-start(f32[144,128]{1,0:T(8,128)S(1)} %add_columns.1.refs_1_), channel_id=1, source_target_pairs={{0,24},{8,16},{16,8},{24,0},{1,25},{9,17},{17,9},{25,1},{2,26},{10... | collective-permute-start | bytes 221192 | tf_op jit(solution)/shard_map/ppermute | solution.py:281
  20.8 4.7 %collective-permute-start.5 = (f32[144,128]{1,0:T(8,128)S(1)}, f32[144,128]{1,0:T(8,128)S(1)}, u32[]{:S(2)}, u32[]{:S(2)}) collective-permute-start(f32[144,128]{1,0:T(8,128)S(1)} %add_columns.1.refs_1_), channel_id=1, source_target_pairs={{0,16},{8,24},{16,0},{24,8},{1,17},{9,25},{17,1},{25,9},{2,18},{10... | collective-permute-start | bytes 221192 | tf_op jit(solution)/shard_map/ppermute | solution.py:281
  21.2 4.4 %collective-permute-start.4 = (f32[144,128]{1,0:T(8,128)S(1)}, f32[144,128]{1,0:T(8,128)S(1)}, u32[]{:S(2)}, u32[]{:S(2)}) collective-permute-start(f32[144,128]{1,0:T(8,128)S(1)} %add_columns.1.refs_1_), channel_id=1, source_target_pairs={{0,8},{8,0},{16,24},{24,16},{1,9},{9,1},{17,25},{25,17},{2,10},{10... | collective-permute-start | bytes 221192 | tf_op jit(solution)/shard_map/ppermute | solution.py:281
  52.4 9.6 %collective-permute-start.12 = (bf16[208,128]{1,0:T(8,128)(2,1)S(1)}, bf16[208,128]{1,0:T(8,128)(2,1)S(1)}, u32[]{:S(2)}, u32[]{:S(2)}) collective-permute-start(bf16[208,128]{1,0:T(8,128)(2,1)S(1)} %first_batch.1.refs_0_), channel_id=1, source_target_pairs={{0,6},{2,4},{4,2},{6,0},{1,7},{3,5},{5,3},{7,1},{8,14},{10,12},{12... | collective-permute-start | bytes 159752 | tf_op jit(solution)/shard_map/ppermute | solution.py:281
  54.3 8.9 %collective-permute-start.10 = (bf16[208,128]{1,0:T(8,128)(2,1)S(1)}, bf16[208,128]{1,0:T(8,128)(2,1)S(1)}, u32[]{:S(2)}, u32[]{:S(2)}) collective-permute-start(bf16[208,128]{1,0:T(8,128)(2,1)S(1)} %first_batch.1.refs_0_), channel_id=1, source_target_pairs={{0,4},{2,6},{4,0},{6,2},{1,5},{3,7},{5,1},{7,3},{8,12},{10,14},{12... | collective-permute-start | bytes 159752 | tf_op jit(solution)/shard_map/ppermute | solution.py:281
  56.0 9.7 %collective-permute-start.8 = (bf16[208,128]{1,0:T(8,128)(2,1)S(1)}, bf16[208,128]{1,0:T(8,128)(2,1)S(1)}, u32[]{:S(2)}, u32[]{:S(2)}) collective-permute-start(bf16[208,128]{1,0:T(8,128)(2,1)S(1)} %first_batch.1.refs_0_), channel_id=1, source_target_pairs={{0,2},{2,0},{4,6},{6,4},{1,3},{3,1},{5,7},{7,5},{8,10},{10,8},{12,... | collective-permute-start | bytes 159752 | tf_op jit(solution)/shard_map/ppermute | solution.py:281
  56.0 10.8 %collective-permute-start.7 = (bf16[208,128]{1,0:T(8,128)(2,1)S(1)}, bf16[208,128]{1,0:T(8,128)(2,1)S(1)}, u32[]{:S(2)}, u32[]{:S(2)}) collective-permute-start(bf16[208,128]{1,0:T(8,128)(2,1)S(1)} %first_batch.1.refs_0_), channel_id=1, source_target_pairs={{0,1},{1,0},{2,3},{3,2},{4,5},{5,4},{6,7},{7,6},{8,9},{9,8},{10,11... | collective-permute-start | bytes 159752 | tf_op jit(solution)/shard_map/ppermute | solution.py:281
  62.0 4.8 %collective-permute-start.13 = (bf16[208,128]{1,0:T(8,128)(2,1)S(1)}, bf16[208,128]{1,0:T(8,128)(2,1)S(1)}, u32[]{:S(2)}, u32[]{:S(2)}) collective-permute-start(bf16[208,128]{1,0:T(8,128)(2,1)S(1)} %collective-permute-done.12.refs_3_), channel_id=1, source_target_pairs={{0,1},{1,0},{2,3},{3,2},{4,5},{5,4},{6,7},{7,6},{8,9},{9,8},{10,11... | collective-permute-start | bytes 159752 | tf_op jit(solution)/shard_map/ppermute | solution.py:281
  63.3 3.6 %collective-permute-start.11 = (bf16[208,128]{1,0:T(8,128)(2,1)S(1)}, bf16[208,128]{1,0:T(8,128)(2,1)S(1)}, u32[]{:S(2)}, u32[]{:S(2)}) collective-permute-start(bf16[208,128]{1,0:T(8,128)(2,1)S(1)} %collective-permute-done.10.refs_2_), channel_id=1, source_target_pairs={{0,1},{1,0},{2,3},{3,2},{4,5},{5,4},{6,7},{7,6},{8,9},{9,8},{10,11... | collective-permute-start | bytes 159752 | tf_op jit(solution)/shard_map/ppermute | solution.py:281
  67.6 5.5 %collective-permute-start.17 = (bf16[208,128]{1,0:T(8,128)(2,1)S(1)}, bf16[208,128]{1,0:T(8,128)(2,1)S(1)}, u32[]{:S(2)}, u32[]{:S(2)}) collective-permute-start(bf16[208,128]{1,0:T(8,128)(2,1)S(1)} %get-tuple-element.81.refs_0_), channel_id=1, source_target_pairs={{0,4},{2,6},{4,0},{6,2},{1,5},{3,7},{5,1},{7,3},{8,12},{10,14},{12... | collective-permute-start | bytes 159752 | tf_op jit(solution)/shard_map/ppermute | solution.py:281
  69.4 4.4 %collective-permute-start.19 = (bf16[208,128]{1,0:T(8,128)(2,1)S(1)}, bf16[208,128]{1,0:T(8,128)(2,1)S(1)}, u32[]{:S(2)}, u32[]{:S(2)}) collective-permute-start(bf16[208,128]{1,0:T(8,128)(2,1)S(1)} %get-tuple-element.81.refs_0_), channel_id=1, source_target_pairs={{0,6},{2,4},{4,2},{6,0},{1,7},{3,5},{5,3},{7,1},{8,14},{10,12},{12... | collective-permute-start | bytes 159752 | tf_op jit(solution)/shard_map/ppermute | solution.py:281
  70.2 4.8 %collective-permute-start.15 = (bf16[208,128]{1,0:T(8,128)(2,1)S(1)}, bf16[208,128]{1,0:T(8,128)(2,1)S(1)}, u32[]{:S(2)}, u32[]{:S(2)}) collective-permute-start(bf16[208,128]{1,0:T(8,128)(2,1)S(1)} %get-tuple-element.81.refs_0_), channel_id=1, source_target_pairs={{0,2},{2,0},{4,6},{6,4},{1,3},{3,1},{5,7},{7,5},{8,10},{10,8},{12,... | collective-permute-start | bytes 159752 | tf_op jit(solution)/shard_map/ppermute | solution.py:281
  70.3 5.3 %collective-permute-start.14 = (bf16[208,128]{1,0:T(8,128)(2,1)S(1)}, bf16[208,128]{1,0:T(8,128)(2,1)S(1)}, u32[]{:S(2)}, u32[]{:S(2)}) collective-permute-start(bf16[208,128]{1,0:T(8,128)(2,1)S(1)} %get-tuple-element.81.refs_0_), channel_id=1, source_target_pairs={{0,1},{1,0},{2,3},{3,2},{4,5},{5,4},{6,7},{7,6},{8,9},{9,8},{10,11... | collective-permute-start | bytes 159752 | tf_op jit(solution)/shard_map/ppermute | solution.py:281
  73.1 2.8 %collective-permute-start.18 = (bf16[208,128]{1,0:T(8,128)(2,1)S(1)}, bf16[208,128]{1,0:T(8,128)(2,1)S(1)}, u32[]{:S(2)}, u32[]{:S(2)}) collective-permute-start(bf16[208,128]{1,0:T(8,128)(2,1)S(1)} %collective-permute-done.17.refs_2_), channel_id=1, source_target_pairs={{0,1},{1,0},{2,3},{3,2},{4,5},{5,4},{6,7},{7,6},{8,9},{9,8},{10,11... | collective-permute-start | bytes 159752 | tf_op jit(solution)/shard_map/ppermute | solution.py:281
  73.8 2.1 %collective-permute-start.20 = (bf16[208,128]{1,0:T(8,128)(2,1)S(1)}, bf16[208,128]{1,0:T(8,128)(2,1)S(1)}, u32[]{:S(2)}, u32[]{:S(2)}) collective-permute-start(bf16[208,128]{1,0:T(8,128)(2,1)S(1)} %collective-permute-done.19.refs_3_), channel_id=1, source_target_pairs={{0,1},{1,0},{2,3},{3,2},{4,5},{5,4},{6,7},{7,6},{8,9},{9,8},{10,11... | collective-permute-start | bytes 159752 | tf_op jit(solution)/shard_map/ppermute | solution.py:281
  76.9 5.3 %collective-permute-start.24 = (bf16[208,128]{1,0:T(8,128)(2,1)S(1)}, bf16[208,128]{1,0:T(8,128)(2,1)S(1)}, u32[]{:S(2)}, u32[]{:S(2)}) collective-permute-start(bf16[208,128]{1,0:T(8,128)(2,1)S(1)} %get-tuple-element.100.refs_0_), channel_id=1, source_target_pairs={{0,4},{2,6},{4,0},{6,2},{1,5},{3,7},{5,1},{7,3},{8,12},{10,14},{12... | collective-permute-start | bytes 159752 | tf_op jit(solution)/shard_map/ppermute | solution.py:281
  78.2 4.7 %collective-permute-start.26 = (bf16[208,128]{1,0:T(8,128)(2,1)S(1)}, bf16[208,128]{1,0:T(8,128)(2,1)S(1)}, u32[]{:S(2)}, u32[]{:S(2)}) collective-permute-start(bf16[208,128]{1,0:T(8,128)(2,1)S(1)} %get-tuple-element.100.refs_0_), channel_id=1, source_target_pairs={{0,6},{2,4},{4,2},{6,0},{1,7},{3,5},{5,3},{7,1},{8,14},{10,12},{12... | collective-permute-start | bytes 159752 | tf_op jit(solution)/shard_map/ppermute | solution.py:281
  79.5 4.5 %collective-permute-start.22 = (bf16[208,128]{1,0:T(8,128)(2,1)S(1)}, bf16[208,128]{1,0:T(8,128)(2,1)S(1)}, u32[]{:S(2)}, u32[]{:S(2)}) collective-permute-start(bf16[208,128]{1,0:T(8,128)(2,1)S(1)} %get-tuple-element.100.refs_0_), channel_id=1, source_target_pairs={{0,2},{2,0},{4,6},{6,4},{1,3},{3,1},{5,7},{7,5},{8,10},{10,8},{12,... | collective-permute-start | bytes 159752 | tf_op jit(solution)/shard_map/ppermute | solution.py:281
  80.4 4.7 %collective-permute-start.21 = (bf16[208,128]{1,0:T(8,128)(2,1)S(1)}, bf16[208,128]{1,0:T(8,128)(2,1)S(1)}, u32[]{:S(2)}, u32[]{:S(2)}) collective-permute-start(bf16[208,128]{1,0:T(8,128)(2,1)S(1)} %get-tuple-element.100.refs_0_), channel_id=1, source_target_pairs={{0,1},{1,0},{2,3},{3,2},{4,5},{5,4},{6,7},{7,6},{8,9},{9,8},{10,11... | collective-permute-start | bytes 159752 | tf_op jit(solution)/shard_map/ppermute | solution.py:281
  82.2 2.9 %collective-permute-start.25 = (bf16[208,128]{1,0:T(8,128)(2,1)S(1)}, bf16[208,128]{1,0:T(8,128)(2,1)S(1)}, u32[]{:S(2)}, u32[]{:S(2)}) collective-permute-start(bf16[208,128]{1,0:T(8,128)(2,1)S(1)} %collective-permute-done.24.refs_2_), channel_id=1, source_target_pairs={{0,1},{1,0},{2,3},{3,2},{4,5},{5,4},{6,7},{7,6},{8,9},{9,8},{10,11... | collective-permute-start | bytes 159752 | tf_op jit(solution)/shard_map/ppermute | solution.py:281
  82.8 2.2 %collective-permute-start.27 = (bf16[208,128]{1,0:T(8,128)(2,1)S(1)}, bf16[208,128]{1,0:T(8,128)(2,1)S(1)}, u32[]{:S(2)}, u32[]{:S(2)}) collective-permute-start(bf16[208,128]{1,0:T(8,128)(2,1)S(1)} %collective-permute-done.26.refs_3_), channel_id=1, source_target_pairs={{0,1},{1,0},{2,3},{3,2},{4,5},{5,4},{6,7},{7,6},{8,9},{9,8},{10,11... | collective-permute-start | bytes 159752 | tf_op jit(solution)/shard_map/ppermute | solution.py:281
  84.0 1.5 %collective-permute-start.23 = (bf16[208,128]{1,0:T(8,128)(2,1)S(1)}, bf16[208,128]{1,0:T(8,128)(2,1)S(1)}, u32[]{:S(2)}, u32[]{:S(2)}) collective-permute-start(bf16[208,128]{1,0:T(8,128)(2,1)S(1)} %collective-permute-done.22.refs_1_), channel_id=1, source_target_pairs={{0,1},{1,0},{2,3},{3,2},{4,5},{5,4},{6,7},{7,6},{8,9},{9,8},{10,11... | collective-permute-start | bytes 159752 | tf_op jit(solution)/shard_map/ppermute | solution.py:281
  86.1 5.7 %collective-permute-start.31 = (bf16[208,128]{1,0:T(8,128)(2,1)S(1)}, bf16[208,128]{1,0:T(8,128)(2,1)S(1)}, u32[]{:S(2)}, u32[]{:S(2)}) collective-permute-start(bf16[208,128]{1,0:T(8,128)(2,1)S(1)} %get-tuple-element.119.refs_0_), channel_id=1, source_target_pairs={{0,4},{2,6},{4,0},{6,2},{1,5},{3,7},{5,1},{7,3},{8,12},{10,14},{12... | collective-permute-start | bytes 159752 | tf_op jit(solution)/shard_map/ppermute | solution.py:281
  87.5 4.8 %collective-permute-start.33 = (bf16[208,128]{1,0:T(8,128)(2,1)S(1)}, bf16[208,128]{1,0:T(8,128)(2,1)S(1)}, u32[]{:S(2)}, u32[]{:S(2)}) collective-permute-start(bf16[208,128]{1,0:T(8,128)(2,1)S(1)} %get-tuple-element.119.refs_0_), channel_id=1, source_target_pairs={{0,6},{2,4},{4,2},{6,0},{1,7},{3,5},{5,3},{7,1},{8,14},{10,12},{12... | collective-permute-start | bytes 159752 | tf_op jit(solution)/shard_map/ppermute | solution.py:281
  88.7 4.7 %collective-permute-start.29 = (bf16[208,128]{1,0:T(8,128)(2,1)S(1)}, bf16[208,128]{1,0:T(8,128)(2,1)S(1)}, u32[]{:S(2)}, u32[]{:S(2)}) collective-permute-start(bf16[208,128]{1,0:T(8,128)(2,1)S(1)} %get-tuple-element.119.refs_0_), channel_id=1, source_target_pairs={{0,2},{2,0},{4,6},{6,4},{1,3},{3,1},{5,7},{7,5},{8,10},{10,8},{12,... | collective-permute-start | bytes 159752 | tf_op jit(solution)/shard_map/ppermute | solution.py:281
  89.6 4.6 %collective-permute-start.28 = (bf16[208,128]{1,0:T(8,128)(2,1)S(1)}, bf16[208,128]{1,0:T(8,128)(2,1)S(1)}, u32[]{:S(2)}, u32[]{:S(2)}) collective-permute-start(bf16[208,128]{1,0:T(8,128)(2,1)S(1)} %get-tuple-element.119.refs_0_), channel_id=1, source_target_pairs={{0,1},{1,0},{2,3},{3,2},{4,5},{5,4},{6,7},{7,6},{8,9},{9,8},{10,11... | collective-permute-start | bytes 159752 | tf_op jit(solution)/shard_map/ppermute | solution.py:281
  91.8 2.5 %collective-permute-start.32 = (bf16[208,128]{1,0:T(8,128)(2,1)S(1)}, bf16[208,128]{1,0:T(8,128)(2,1)S(1)}, u32[]{:S(2)}, u32[]{:S(2)}) collective-permute-start(bf16[208,128]{1,0:T(8,128)(2,1)S(1)} %collective-permute-done.31.refs_2_), channel_id=1, source_target_pairs={{0,1},{1,0},{2,3},{3,2},{4,5},{5,4},{6,7},{7,6},{8,9},{9,8},{10,11... | collective-permute-start | bytes 159752 | tf_op jit(solution)/shard_map/ppermute | solution.py:281
  92.2 2.1 %collective-permute-start.34 = (bf16[208,128]{1,0:T(8,128)(2,1)S(1)}, bf16[208,128]{1,0:T(8,128)(2,1)S(1)}, u32[]{:S(2)}, u32[]{:S(2)}) collective-permute-start(bf16[208,128]{1,0:T(8,128)(2,1)S(1)} %collective-permute-done.33.refs_3_), channel_id=1, source_target_pairs={{0,1},{1,0},{2,3},{3,2},{4,5},{5,4},{6,7},{7,6},{8,9},{9,8},{10,11... | collective-permute-start | bytes 159752 | tf_op jit(solution)/shard_map/ppermute | solution.py:281
  (10 other events, 79.7 us)

commit v5 on v4

--- a/solution.py
+++ b/solution.py
@@ -356,7 +356,6 @@
         flops=2 * 128 * 128 * 2048,
         name="unpack",
     )
-    held = dict(enumerate(zip(both[:4], both[4:])))
     stacked = []
     beside = ((), ((1, 0), (2, 0)), ((2, 1), (3, 0)), ((3, 1), (3, 2)))
     for batch in range(4):
@@ -371,7 +370,11 @@
                 flops=flops,
                 name="advance",
             )
-        own, other, flat = spread(g, [a for at in news for a in news[at]])
+        if batch == 0:
+            own, other, (*both, loc) = spread(g, [*both, loc])
+            held = dict(enumerate(zip(both[:4], both[4:])))
+        else:
+            own, other, flat = spread(g, [a for at in news for a in news[at]])
         for n, at in enumerate(news):
             held[at] = flat[2 * n : 2 * n + 2]
         at = min(batch, 3)

time: 96.1 us -> 96 us (level)
  starting transfers between devices: 40.9 us -> 39.9 us
  transfers between devices with their start and end apart: 35 -> 35, of which waited for: 10 -> 13; matrix products, arithmetic and copies ran while one was open for 0% -> 0% of each run, Pallas kernels for 11% -> 11%
where the time goes in v5:
time: 96 us; the launch traced here: 95.7 us
  starting transfers between devices  39.9 us (42%)
  blocking collectives  26.7 us (28%)
  Pallas kernels  17.2 us (18%)
  waiting for transfers between devices  9.12 us (9%)
  local copies, waits for them, and re-layouts  2.49 us (3%)
    ppermute x35, starting transfers between devices, swap(): return lax.ppermute(a, axis, [(i, i ^ by) for i in range(size)])  39.9 us
    all_to_all x1, blocking collectives, per_device(): pack = lax.all_to_all(pack, 'z', 0, 0, tiled=True)  26.7 us
    pallas_call x22, Pallas kernels, call(): pl.pallas_call((lambda *refs: body(place(), *refs)) if placed else body,...  17.2 us
    ppermute x35, waiting for transfers between devices, swap(): return lax.ppermute(a, axis, [(i, i ^ by) for i in range(size)])  9.12 us
    unnamed x14, local copies, waits for them, and re-layouts  2.49 us
  transfers between devices with their start and end apart: 35, of which 13 were waited for; matrix products, arithmetic and copies ran while one was open for 0% of the time, Pallas kernels for 11%

profile of v5, /device:TPU:1, one launch (start us, length us, event | category | flops | bytes accessed | tf_op | source)
XLA Modules:
  0.0 95.7 jit_solution(1672569869756996744)
XLA Ops:
  0.0 0.9 copy-done.3
  1.0 0.8 copy-done.4
  2.5 3.5 %collect_other.1 = (f32[4,168,128]{2,1,0:T(8,128)S(1)}, f32[16,4096]{1,0:T(8,128)S(1)}, f32[8,128]{1,0:T(8,128)S(1)}) custom-call(s32[4,4,1024]{2,1,0:T(4,128)S(1)} %copy-done.4, f32[10,4096]{1,0:T(8,128)S(1)} %copy-done.3, s32[4,32]{1,0:T(4,128)S(1)} %copy-done.6), custom_call_target="tpu_custom_call" | custom-call | bytes 840192 | tf_op jit(solution)/shard_map/collect_other/pallas_call | solution.py:27
  6.0 3.3 %collective-permute-start = (f32[4,168,128]{2,1,0:T(8,128)S(1)}, f32[4,168,128]{2,1,0:T(8,128)S(1)}, u32[]{:S(2)}, u32[]{:S(2)}) collective-permute-start(f32[4,168,128]{2,1,0:T(8,128)S(1)} %get-tuple-element.82), channel_id=1, source_target_pairs={{0,1},{1,0},{2,3},{3,2},{4,5},{5,4},{6,7},{7,6},{8,9},{9,8},{10,11... | collective-permute-start | bytes 1032200 | tf_op jit(solution)/shard_map/ppermute | solution.py:281
  9.3 1.6 %collect_own.1.own_ref = f32[2,168,128]{2,1,0:T(8,128)S(1)} custom-call(s32[4,4,1024]{2,1,0:T(4,128)S(1)} %copy-done.4, f32[16,4096]{1,0:T(8,128)S(1)} %get-tuple-element.80.refs_1_.refs_0_, f32[8,128]{1,0:T(8,128)S(1)} %get-tuple-element.81.refs_2_), custom_call_target="tpu_custom_call" | custom-call | flops 1000000000 | bytes 503808 | tf_op jit(solution)/shard_map/collect_own/pallas_call | solution.py:27
  11.0 1.1 %collective-permute-start.2 = (f32[168,128]{1,0:T(8,128)S(1)}, f32[168,128]{1,0:T(8,128)S(1)}, u32[]{:S(2)}, u32[]{:S(2)}) collective-permute-start(f32[168,128]{1,0:T(8,128)S(1)} %get-tuple-element.85), channel_id=1, source_target_pairs={{0,4},{2,6},{4,0},{6,2},{1,5},{3,7},{5,1},{7,3},{8,12},{10,14},{12... | collective-permute-start | bytes 258056 | tf_op jit(solution)/shard_map/ppermute | solution.py:281
  12.1 0.9 collective-permute-start.3
  12.9 1.6 %collect_rest.1 = (f32[168,128]{1,0:T(8,128)S(1)}, f32[168,128]{1,0:T(8,128)S(1)}) custom-call(s32[4,4,1024]{2,1,0:T(4,128)S(1)} %copy-done.4, f32[16,4096]{1,0:T(8,128)S(1)} %get-tuple-element.80.refs_1_.refs_0_, f32[8,128]{1,0:T(8,128)S(1)} %get-tuple-element.81.refs_2_, f32[4,168,128]{2,1,0:T(8,128)S(1)} %collective-permute-done.refs_3_.other_ref), custom_call_target="tpu_custom_call" | custom-call | flops 1000000000 | bytes 847872 | tf_op jit(solution)/shard_map/collect_rest/pallas_call | solution.py:27
  14.6 0.9 collective-permute-start.1
  15.4 1.3 %collective-permute-done.2.refs_3_ = f32[168,128]{1,0:T(8,128)S(1)} collective-permute-done((f32[168,128]{1,0:T(8,128)S(1)}, f32[168,128]{1,0:T(8,128)S(1)}, u32[]{:S(2)}, u32[]{:S(2)}) %collective-permute-start.2) | collective-permute-done | bytes 86048 | tf_op jit(solution)/shard_map/ppermute | solution.py:281
  16.7 2.2 %collective-permute-done.3.refs_4_ = f32[168,128]{1,0:T(8,128)S(1)} collective-permute-done((f32[168,128]{1,0:T(8,128)S(1)}, f32[168,128]{1,0:T(8,128)S(1)}, u32[]{:S(2)}, u32[]{:S(2)}) %collective-permute-start.3) | collective-permute-done | bytes 86048 | tf_op jit(solution)/shard_map/ppermute | solution.py:281
  18.9 1.9 %collective-permute-start.6 = (f32[144,128]{1,0:T(8,128)S(1)}, f32[144,128]{1,0:T(8,128)S(1)}, u32[]{:S(2)}, u32[]{:S(2)}) collective-permute-start(f32[144,128]{1,0:T(8,128)S(1)} %add_columns.1.refs_1_), channel_id=1, source_target_pairs={{0,24},{8,16},{16,8},{24,0},{1,25},{9,17},{17,9},{25,1},{2,26},{10... | collective-permute-start | bytes 221192 | tf_op jit(solution)/shard_map/ppermute | solution.py:281
  21.2 1.1 %collective-permute-start.4 = (f32[144,128]{1,0:T(8,128)S(1)}, f32[144,128]{1,0:T(8,128)S(1)}, u32[]{:S(2)}, u32[]{:S(2)}) collective-permute-start(f32[144,128]{1,0:T(8,128)S(1)} %add_columns.1.refs_1_), channel_id=1, source_target_pairs={{0,8},{8,0},{16,24},{24,16},{1,9},{9,1},{17,25},{25,17},{2,10},{10... | collective-permute-start | bytes 221192 | tf_op jit(solution)/shard_map/ppermute | solution.py:281
  22.3 1.2 %collective-permute-done.6.refs_4_ = f32[144,128]{1,0:T(8,128)S(1)} collective-permute-done((f32[144,128]{1,0:T(8,128)S(1)}, f32[144,128]{1,0:T(8,128)S(1)}, u32[]{:S(2)}, u32[]{:S(2)}) %collective-permute-start.6) | collective-permute-done | bytes 73760 | tf_op jit(solution)/shard_map/ppermute | solution.py:281
  23.4 2.1 %collective-permute-done.5.refs_3_ = f32[144,128]{1,0:T(8,128)S(1)} collective-permute-done((f32[144,128]{1,0:T(8,128)S(1)}, f32[144,128]{1,0:T(8,128)S(1)}, u32[]{:S(2)}, u32[]{:S(2)}) %collective-permute-start.5) | collective-permute-done | bytes 73760 | tf_op jit(solution)/shard_map/ppermute | solution.py:281
  25.6 26.7 %all_to_all.5.refs_0_ = f32[8,192,128]{2,1,0:T(8,128)S(1)} all-to-all(f32[8,192,128]{2,1,0:T(8,128)S(1)} %add_rows.1), channel_id=1, replica_groups=mesh['z'=8,'y'=4,'x'=4,'c'=2] {'z'}, dimensions={0} | all-to-all | bytes 1572864 | tf_op jit(solution)/shard_map/all_to_all | solution.py:336
  52.4 3.3 %collective-permute-start.10 = (bf16[208,128]{1,0:T(8,128)(2,1)S(1)}, bf16[208,128]{1,0:T(8,128)(2,1)S(1)}, u32[]{:S(2)}, u32[]{:S(2)}) collective-permute-start(bf16[208,128]{1,0:T(8,128)(2,1)S(1)} %first_batch.1.refs_0_), channel_id=1, source_target_pairs={{0,4},{2,6},{4,0},{6,2},{1,5},{3,7},{5,1},{7,3},{8,12},{10,14},{12... | collective-permute-start | bytes 159752 | tf_op jit(solution)/shard_map/ppermute | solution.py:281
  55.7 0.9 collective-permute-start.12
  56.6 4.8 %collective-permute-start.7 = (bf16[208,128]{1,0:T(8,128)(2,1)S(1)}, bf16[208,128]{1,0:T(8,128)(2,1)S(1)}, u32[]{:S(2)}, u32[]{:S(2)}) collective-permute-start(bf16[208,128]{1,0:T(8,128)(2,1)S(1)} %first_batch.1.refs_0_), channel_id=1, source_target_pairs={{0,1},{1,0},{2,3},{3,2},{4,5},{5,4},{6,7},{7,6},{8,9},{9,8},{10,11... | collective-permute-start | bytes 159752 | tf_op jit(solution)/shard_map/ppermute | solution.py:281
  62.1 3.5 %collective-permute-start.13 = (bf16[208,128]{1,0:T(8,128)(2,1)S(1)}, bf16[208,128]{1,0:T(8,128)(2,1)S(1)}, u32[]{:S(2)}, u32[]{:S(2)}) collective-permute-start(bf16[208,128]{1,0:T(8,128)(2,1)S(1)} %collective-permute-done.12.refs_3_), channel_id=1, source_target_pairs={{0,1},{1,0},{2,3},{3,2},{4,5},{5,4},{6,7},{7,6},{8,9},{9,8},{10,11... | collective-permute-start | bytes 159752 | tf_op jit(solution)/shard_map/ppermute | solution.py:281
  67.6 1.2 %collective-permute-start.17 = (bf16[208,128]{1,0:T(8,128)(2,1)S(1)}, bf16[208,128]{1,0:T(8,128)(2,1)S(1)}, u32[]{:S(2)}, u32[]{:S(2)}) collective-permute-start(bf16[208,128]{1,0:T(8,128)(2,1)S(1)} %get-tuple-element.101.refs_0_), channel_id=1, source_target_pairs={{0,4},{2,6},{4,0},{6,2},{1,5},{3,7},{5,1},{7,3},{8,12},{10,14},{12... | collective-permute-start | bytes 159752 | tf_op jit(solution)/shard_map/ppermute | solution.py:281
  68.8 0.9 collective-permute-start.19
  70.4 1.2 %collective-permute-start.14 = (bf16[208,128]{1,0:T(8,128)(2,1)S(1)}, bf16[208,128]{1,0:T(8,128)(2,1)S(1)}, u32[]{:S(2)}, u32[]{:S(2)}) collective-permute-start(bf16[208,128]{1,0:T(8,128)(2,1)S(1)} %get-tuple-element.101.refs_0_), channel_id=1, source_target_pairs={{0,1},{1,0},{2,3},{3,2},{4,5},{5,4},{6,7},{7,6},{8,9},{9,8},{10,11... | collective-permute-start | bytes 159752 | tf_op jit(solution)/shard_map/ppermute | solution.py:281
  76.7 1.4 %collective-permute-start.24 = (bf16[208,128]{1,0:T(8,128)(2,1)S(1)}, bf16[208,128]{1,0:T(8,128)(2,1)S(1)}, u32[]{:S(2)}, u32[]{:S(2)}) collective-permute-start(bf16[208,128]{1,0:T(8,128)(2,1)S(1)} %get-tuple-element.120.refs_0_), channel_id=1, source_target_pairs={{0,4},{2,6},{4,0},{6,2},{1,5},{3,7},{5,1},{7,3},{8,12},{10,14},{12... | collective-permute-start | bytes 159752 | tf_op jit(solution)/shard_map/ppermute | solution.py:281
  78.2 1.3 %collective-permute-start.26 = (bf16[208,128]{1,0:T(8,128)(2,1)S(1)}, bf16[208,128]{1,0:T(8,128)(2,1)S(1)}, u32[]{:S(2)}, u32[]{:S(2)}) collective-permute-start(bf16[208,128]{1,0:T(8,128)(2,1)S(1)} %get-tuple-element.120.refs_0_), channel_id=1, source_target_pairs={{0,6},{2,4},{4,2},{6,0},{1,7},{3,5},{5,3},{7,1},{8,14},{10,12},{12... | collective-permute-start | bytes 159752 | tf_op jit(solution)/shard_map/ppermute | solution.py:281
  80.2 1.1 %collective-permute-start.21 = (bf16[208,128]{1,0:T(8,128)(2,1)S(1)}, bf16[208,128]{1,0:T(8,128)(2,1)S(1)}, u32[]{:S(2)}, u32[]{:S(2)}) collective-permute-start(bf16[208,128]{1,0:T(8,128)(2,1)S(1)} %get-tuple-element.120.refs_0_), channel_id=1, source_target_pairs={{0,1},{1,0},{2,3},{3,2},{4,5},{5,4},{6,7},{7,6},{8,9},{9,8},{10,11... | collective-permute-start | bytes 159752 | tf_op jit(solution)/shard_map/ppermute | solution.py:281
  82.6 1.5 %collective-permute-start.27 = (bf16[208,128]{1,0:T(8,128)(2,1)S(1)}, bf16[208,128]{1,0:T(8,128)(2,1)S(1)}, u32[]{:S(2)}, u32[]{:S(2)}) collective-permute-start(bf16[208,128]{1,0:T(8,128)(2,1)S(1)} %collective-permute-done.26.refs_3_), channel_id=1, source_target_pairs={{0,1},{1,0},{2,3},{3,2},{4,5},{5,4},{6,7},{7,6},{8,9},{9,8},{10,11... | collective-permute-start | bytes 159752 | tf_op jit(solution)/shard_map/ppermute | solution.py:281
  86.0 1.3 %collective-permute-start.31 = (bf16[208,128]{1,0:T(8,128)(2,1)S(1)}, bf16[208,128]{1,0:T(8,128)(2,1)S(1)}, u32[]{:S(2)}, u32[]{:S(2)}) collective-permute-start(bf16[208,128]{1,0:T(8,128)(2,1)S(1)} %get-tuple-element.139.refs_0_), channel_id=1, source_target_pairs={{0,4},{2,6},{4,0},{6,2},{1,5},{3,7},{5,1},{7,3},{8,12},{10,14},{12... | collective-permute-start | bytes 159752 | tf_op jit(solution)/shard_map/ppermute | solution.py:281
  87.4 1.3 %collective-permute-start.33 = (bf16[208,128]{1,0:T(8,128)(2,1)S(1)}, bf16[208,128]{1,0:T(8,128)(2,1)S(1)}, u32[]{:S(2)}, u32[]{:S(2)}) collective-permute-start(bf16[208,128]{1,0:T(8,128)(2,1)S(1)} %get-tuple-element.139.refs_0_), channel_id=1, source_target_pairs={{0,6},{2,4},{4,2},{6,0},{1,7},{3,5},{5,3},{7,1},{8,14},{10,12},{12... | collective-permute-start | bytes 159752 | tf_op jit(solution)/shard_map/ppermute | solution.py:281
  89.5 1.5 %collective-permute-start.28 = (bf16[208,128]{1,0:T(8,128)(2,1)S(1)}, bf16[208,128]{1,0:T(8,128)(2,1)S(1)}, u32[]{:S(2)}, u32[]{:S(2)}) collective-permute-start(bf16[208,128]{1,0:T(8,128)(2,1)S(1)} %get-tuple-element.139.refs_0_), channel_id=1, source_target_pairs={{0,1},{1,0},{2,3},{3,2},{4,5},{5,4},{6,7},{7,6},{8,9},{9,8},{10,11... | collective-permute-start | bytes 159752 | tf_op jit(solution)/shard_map/ppermute | solution.py:281
  92.4 0.9 collective-permute-start.34
  94.5 1.2 %finish.1 = f32[80,512]{1,0:T(8,128)} custom-call(bf16[208,128]{1,0:T(8,128)(2,1)S(1)} %collective-permute-done.28.refs_0_, bf16[208,128]{1,0:T(8,128)(2,1)S(1)} %collective-permute-done.30.refs_1_, bf16[208,128]{1,0:T(8,128)(2,1)S(1)} %collective-permute-done.32.refs_2_, bf16[208,128]{1,0:T(8,128)(2,1)S(1)} %collective-permute-done.34.refs_3_, ...), custom_call_target="tpu_custom_call" | custom-call | flops 134217728 | bytes 1097728 | tf_op jit(solution)/shard_map/finish/pallas_call | solution.py:27
  (75 shorter events, 17.2 us)
Async XLA Ops:
  6.0 5.0 %collective-permute-start = (f32[4,168,128]{2,1,0:T(8,128)S(1)}, f32[4,168,128]{2,1,0:T(8,128)S(1)}, u32[]{:S(2)}, u32[]{:S(2)}) collective-permute-start(f32[4,168,128]{2,1,0:T(8,128)S(1)} %get-tuple-element.82), channel_id=1, source_target_pairs={{0,1},{1,0},{2,3},{3,2},{4,5},{5,4},{6,7},{7,6},{8,9},{9,8},{10,11... | collective-permute-start | bytes 1032200 | tf_op jit(solution)/shard_map/ppermute | solution.py:281
  11.0 5.7 %collective-permute-start.2 = (f32[168,128]{1,0:T(8,128)S(1)}, f32[168,128]{1,0:T(8,128)S(1)}, u32[]{:S(2)}, u32[]{:S(2)}) collective-permute-start(f32[168,128]{1,0:T(8,128)S(1)} %get-tuple-element.85), channel_id=1, source_target_pairs={{0,4},{2,6},{4,0},{6,2},{1,5},{3,7},{5,1},{7,3},{8,12},{10,14},{12... | collective-permute-start | bytes 258056 | tf_op jit(solution)/shard_map/ppermute | solution.py:281
  12.1 6.8 %collective-permute-start.3 = (f32[168,128]{1,0:T(8,128)S(1)}, f32[168,128]{1,0:T(8,128)S(1)}, u32[]{:S(2)}, u32[]{:S(2)}) collective-permute-start(f32[168,128]{1,0:T(8,128)S(1)} %get-tuple-element.86), channel_id=1, source_target_pairs={{0,6},{2,4},{4,2},{6,0},{1,7},{3,5},{5,3},{7,1},{8,14},{10,12},{12... | collective-permute-start | bytes 258056 | tf_op jit(solution)/shard_map/ppermute | solution.py:281
  14.6 4.3 %collective-permute-start.1 = (f32[168,128]{1,0:T(8,128)S(1)}, f32[168,128]{1,0:T(8,128)S(1)}, u32[]{:S(2)}, u32[]{:S(2)}) collective-permute-start(f32[168,128]{1,0:T(8,128)S(1)} %get-tuple-element.84), channel_id=1, source_target_pairs={{0,2},{2,0},{4,6},{6,4},{1,3},{3,1},{5,7},{7,5},{8,10},{10,8},{12,... | collective-permute-start | bytes 258056 | tf_op jit(solution)/shard_map/ppermute | solution.py:281
  18.9 4.5 %collective-permute-start.6 = (f32[144,128]{1,0:T(8,128)S(1)}, f32[144,128]{1,0:T(8,128)S(1)}, u32[]{:S(2)}, u32[]{:S(2)}) collective-permute-start(f32[144,128]{1,0:T(8,128)S(1)} %add_columns.1.refs_1_), channel_id=1, source_target_pairs={{0,24},{8,16},{16,8},{24,0},{1,25},{9,17},{17,9},{25,1},{2,26},{10... | collective-permute-start | bytes 221192 | tf_op jit(solution)/shard_map/ppermute | solution.py:281
  20.8 4.7 %collective-permute-start.5 = (f32[144,128]{1,0:T(8,128)S(1)}, f32[144,128]{1,0:T(8,128)S(1)}, u32[]{:S(2)}, u32[]{:S(2)}) collective-permute-start(f32[144,128]{1,0:T(8,128)S(1)} %add_columns.1.refs_1_), channel_id=1, source_target_pairs={{0,16},{8,24},{16,0},{24,8},{1,17},{9,25},{17,1},{25,9},{2,18},{10... | collective-permute-start | bytes 221192 | tf_op jit(solution)/shard_map/ppermute | solution.py:281
  21.2 4.4 %collective-permute-start.4 = (f32[144,128]{1,0:T(8,128)S(1)}, f32[144,128]{1,0:T(8,128)S(1)}, u32[]{:S(2)}, u32[]{:S(2)}) collective-permute-start(f32[144,128]{1,0:T(8,128)S(1)} %add_columns.1.refs_1_), channel_id=1, source_target_pairs={{0,8},{8,0},{16,24},{24,16},{1,9},{9,1},{17,25},{25,17},{2,10},{10... | collective-permute-start | bytes 221192 | tf_op jit(solution)/shard_map/ppermute | solution.py:281
  52.4 9.6 %collective-permute-start.10 = (bf16[208,128]{1,0:T(8,128)(2,1)S(1)}, bf16[208,128]{1,0:T(8,128)(2,1)S(1)}, u32[]{:S(2)}, u32[]{:S(2)}) collective-permute-start(bf16[208,128]{1,0:T(8,128)(2,1)S(1)} %first_batch.1.refs_0_), channel_id=1, source_target_pairs={{0,4},{2,6},{4,0},{6,2},{1,5},{3,7},{5,1},{7,3},{8,12},{10,14},{12... | collective-permute-start | bytes 159752 | tf_op jit(solution)/shard_map/ppermute | solution.py:281
  55.7 6.3 %collective-permute-start.12 = (bf16[208,128]{1,0:T(8,128)(2,1)S(1)}, bf16[208,128]{1,0:T(8,128)(2,1)S(1)}, u32[]{:S(2)}, u32[]{:S(2)}) collective-permute-start(bf16[208,128]{1,0:T(8,128)(2,1)S(1)} %first_batch.1.refs_0_), channel_id=1, source_target_pairs={{0,6},{2,4},{4,2},{6,0},{1,7},{3,5},{5,3},{7,1},{8,14},{10,12},{12... | collective-permute-start | bytes 159752 | tf_op jit(solution)/shard_map/ppermute | solution.py:281
  56.6 9.0 %collective-permute-start.8 = (bf16[208,128]{1,0:T(8,128)(2,1)S(1)}, bf16[208,128]{1,0:T(8,128)(2,1)S(1)}, u32[]{:S(2)}, u32[]{:S(2)}) collective-permute-start(bf16[208,128]{1,0:T(8,128)(2,1)S(1)} %first_batch.1.refs_0_), channel_id=1, source_target_pairs={{0,2},{2,0},{4,6},{6,4},{1,3},{3,1},{5,7},{7,5},{8,10},{10,8},{12,... | collective-permute-start | bytes 159752 | tf_op jit(solution)/shard_map/ppermute | solution.py:281
  56.6 10.0 %collective-permute-start.7 = (bf16[208,128]{1,0:T(8,128)(2,1)S(1)}, bf16[208,128]{1,0:T(8,128)(2,1)S(1)}, u32[]{:S(2)}, u32[]{:S(2)}) collective-permute-start(bf16[208,128]{1,0:T(8,128)(2,1)S(1)} %first_batch.1.refs_0_), channel_id=1, source_target_pairs={{0,1},{1,0},{2,3},{3,2},{4,5},{5,4},{6,7},{7,6},{8,9},{9,8},{10,11... | collective-permute-start | bytes 159752 | tf_op jit(solution)/shard_map/ppermute | solution.py:281
  62.1 4.6 %collective-permute-start.13 = (bf16[208,128]{1,0:T(8,128)(2,1)S(1)}, bf16[208,128]{1,0:T(8,128)(2,1)S(1)}, u32[]{:S(2)}, u32[]{:S(2)}) collective-permute-start(bf16[208,128]{1,0:T(8,128)(2,1)S(1)} %collective-permute-done.12.refs_3_), channel_id=1, source_target_pairs={{0,1},{1,0},{2,3},{3,2},{4,5},{5,4},{6,7},{7,6},{8,9},{9,8},{10,11... | collective-permute-start | bytes 159752 | tf_op jit(solution)/shard_map/ppermute | solution.py:281
  65.6 1.4 %collective-permute-start.11 = (bf16[208,128]{1,0:T(8,128)(2,1)S(1)}, bf16[208,128]{1,0:T(8,128)(2,1)S(1)}, u32[]{:S(2)}, u32[]{:S(2)}) collective-permute-start(bf16[208,128]{1,0:T(8,128)(2,1)S(1)} %collective-permute-done.10.refs_2_), channel_id=1, source_target_pairs={{0,1},{1,0},{2,3},{3,2},{4,5},{5,4},{6,7},{7,6},{8,9},{9,8},{10,11... | collective-permute-start | bytes 159752 | tf_op jit(solution)/shard_map/ppermute | solution.py:281
  67.6 5.4 %collective-permute-start.17 = (bf16[208,128]{1,0:T(8,128)(2,1)S(1)}, bf16[208,128]{1,0:T(8,128)(2,1)S(1)}, u32[]{:S(2)}, u32[]{:S(2)}) collective-permute-start(bf16[208,128]{1,0:T(8,128)(2,1)S(1)} %get-tuple-element.101.refs_0_), channel_id=1, source_target_pairs={{0,4},{2,6},{4,0},{6,2},{1,5},{3,7},{5,1},{7,3},{8,12},{10,14},{12... | collective-permute-start | bytes 159752 | tf_op jit(solution)/shard_map/ppermute | solution.py:281
  68.8 5.3 %collective-permute-start.19 = (bf16[208,128]{1,0:T(8,128)(2,1)S(1)}, bf16[208,128]{1,0:T(8,128)(2,1)S(1)}, u32[]{:S(2)}, u32[]{:S(2)}) collective-permute-start(bf16[208,128]{1,0:T(8,128)(2,1)S(1)} %get-tuple-element.101.refs_0_), channel_id=1, source_target_pairs={{0,6},{2,4},{4,2},{6,0},{1,7},{3,5},{5,3},{7,1},{8,14},{10,12},{12... | collective-permute-start | bytes 159752 | tf_op jit(solution)/shard_map/ppermute | solution.py:281
  69.7 5.2 %collective-permute-start.15 = (bf16[208,128]{1,0:T(8,128)(2,1)S(1)}, bf16[208,128]{1,0:T(8,128)(2,1)S(1)}, u32[]{:S(2)}, u32[]{:S(2)}) collective-permute-start(bf16[208,128]{1,0:T(8,128)(2,1)S(1)} %get-tuple-element.101.refs_0_), channel_id=1, source_target_pairs={{0,2},{2,0},{4,6},{6,4},{1,3},{3,1},{5,7},{7,5},{8,10},{10,8},{12,... | collective-permute-start | bytes 159752 | tf_op jit(solution)/shard_map/ppermute | solution.py:281
  70.4 5.0 %collective-permute-start.14 = (bf16[208,128]{1,0:T(8,128)(2,1)S(1)}, bf16[208,128]{1,0:T(8,128)(2,1)S(1)}, u32[]{:S(2)}, u32[]{:S(2)}) collective-permute-start(bf16[208,128]{1,0:T(8,128)(2,1)S(1)} %get-tuple-element.101.refs_0_), channel_id=1, source_target_pairs={{0,1},{1,0},{2,3},{3,2},{4,5},{5,4},{6,7},{7,6},{8,9},{9,8},{10,11... | collective-permute-start | bytes 159752 | tf_op jit(solution)/shard_map/ppermute | solution.py:281
  73.0 2.7 %collective-permute-start.18 = (bf16[208,128]{1,0:T(8,128)(2,1)S(1)}, bf16[208,128]{1,0:T(8,128)(2,1)S(1)}, u32[]{:S(2)}, u32[]{:S(2)}) collective-permute-start(bf16[208,128]{1,0:T(8,128)(2,1)S(1)} %collective-permute-done.17.refs_2_), channel_id=1, source_target_pairs={{0,1},{1,0},{2,3},{3,2},{4,5},{5,4},{6,7},{7,6},{8,9},{9,8},{10,11... | collective-permute-start | bytes 159752 | tf_op jit(solution)/shard_map/ppermute | solution.py:281
  74.1 1.6 %collective-permute-start.20 = (bf16[208,128]{1,0:T(8,128)(2,1)S(1)}, bf16[208,128]{1,0:T(8,128)(2,1)S(1)}, u32[]{:S(2)}, u32[]{:S(2)}) collective-permute-start(bf16[208,128]{1,0:T(8,128)(2,1)S(1)} %collective-permute-done.19.refs_3_), channel_id=1, source_target_pairs={{0,1},{1,0},{2,3},{3,2},{4,5},{5,4},{6,7},{7,6},{8,9},{9,8},{10,11... | collective-permute-start | bytes 159752 | tf_op jit(solution)/shard_map/ppermute | solution.py:281
  76.7 5.3 %collective-permute-start.24 = (bf16[208,128]{1,0:T(8,128)(2,1)S(1)}, bf16[208,128]{1,0:T(8,128)(2,1)S(1)}, u32[]{:S(2)}, u32[]{:S(2)}) collective-permute-start(bf16[208,128]{1,0:T(8,128)(2,1)S(1)} %get-tuple-element.120.refs_0_), channel_id=1, source_target_pairs={{0,4},{2,6},{4,0},{6,2},{1,5},{3,7},{5,1},{7,3},{8,12},{10,14},{12... | collective-permute-start | bytes 159752 | tf_op jit(solution)/shard_map/ppermute | solution.py:281
  78.2 4.5 %collective-permute-start.26 = (bf16[208,128]{1,0:T(8,128)(2,1)S(1)}, bf16[208,128]{1,0:T(8,128)(2,1)S(1)}, u32[]{:S(2)}, u32[]{:S(2)}) collective-permute-start(bf16[208,128]{1,0:T(8,128)(2,1)S(1)} %get-tuple-element.120.refs_0_), channel_id=1, source_target_pairs={{0,6},{2,4},{4,2},{6,0},{1,7},{3,5},{5,3},{7,1},{8,14},{10,12},{12... | collective-permute-start | bytes 159752 | tf_op jit(solution)/shard_map/ppermute | solution.py:281
  79.4 4.7 %collective-permute-start.22 = (bf16[208,128]{1,0:T(8,128)(2,1)S(1)}, bf16[208,128]{1,0:T(8,128)(2,1)S(1)}, u32[]{:S(2)}, u32[]{:S(2)}) collective-permute-start(bf16[208,128]{1,0:T(8,128)(2,1)S(1)} %get-tuple-element.120.refs_0_), channel_id=1, source_target_pairs={{0,2},{2,0},{4,6},{6,4},{1,3},{3,1},{5,7},{7,5},{8,10},{10,8},{12,... | collective-permute-start | bytes 159752 | tf_op jit(solution)/shard_map/ppermute | solution.py:281
  80.2 4.8 %collective-permute-start.21 = (bf16[208,128]{1,0:T(8,128)(2,1)S(1)}, bf16[208,128]{1,0:T(8,128)(2,1)S(1)}, u32[]{:S(2)}, u32[]{:S(2)}) collective-permute-start(bf16[208,128]{1,0:T(8,128)(2,1)S(1)} %get-tuple-element.120.refs_0_), channel_id=1, source_target_pairs={{0,1},{1,0},{2,3},{3,2},{4,5},{5,4},{6,7},{7,6},{8,9},{9,8},{10,11... | collective-permute-start | bytes 159752 | tf_op jit(solution)/shard_map/ppermute | solution.py:281
  82.0 3.0 %collective-permute-start.25 = (bf16[208,128]{1,0:T(8,128)(2,1)S(1)}, bf16[208,128]{1,0:T(8,128)(2,1)S(1)}, u32[]{:S(2)}, u32[]{:S(2)}) collective-permute-start(bf16[208,128]{1,0:T(8,128)(2,1)S(1)} %collective-permute-done.24.refs_2_), channel_id=1, source_target_pairs={{0,1},{1,0},{2,3},{3,2},{4,5},{5,4},{6,7},{7,6},{8,9},{9,8},{10,11... | collective-permute-start | bytes 159752 | tf_op jit(solution)/shard_map/ppermute | solution.py:281
  82.6 2.4 %collective-permute-start.27 = (bf16[208,128]{1,0:T(8,128)(2,1)S(1)}, bf16[208,128]{1,0:T(8,128)(2,1)S(1)}, u32[]{:S(2)}, u32[]{:S(2)}) collective-permute-start(bf16[208,128]{1,0:T(8,128)(2,1)S(1)} %collective-permute-done.26.refs_3_), channel_id=1, source_target_pairs={{0,1},{1,0},{2,3},{3,2},{4,5},{5,4},{6,7},{7,6},{8,9},{9,8},{10,11... | collective-permute-start | bytes 159752 | tf_op jit(solution)/shard_map/ppermute | solution.py:281
  84.1 1.2 %collective-permute-start.23 = (bf16[208,128]{1,0:T(8,128)(2,1)S(1)}, bf16[208,128]{1,0:T(8,128)(2,1)S(1)}, u32[]{:S(2)}, u32[]{:S(2)}) collective-permute-start(bf16[208,128]{1,0:T(8,128)(2,1)S(1)} %collective-permute-done.22.refs_1_), channel_id=1, source_target_pairs={{0,1},{1,0},{2,3},{3,2},{4,5},{5,4},{6,7},{7,6},{8,9},{9,8},{10,11... | collective-permute-start | bytes 159752 | tf_op jit(solution)/shard_map/ppermute | solution.py:281
  86.0 5.7 %collective-permute-start.31 = (bf16[208,128]{1,0:T(8,128)(2,1)S(1)}, bf16[208,128]{1,0:T(8,128)(2,1)S(1)}, u32[]{:S(2)}, u32[]{:S(2)}) collective-permute-start(bf16[208,128]{1,0:T(8,128)(2,1)S(1)} %get-tuple-element.139.refs_0_), channel_id=1, source_target_pairs={{0,4},{2,6},{4,0},{6,2},{1,5},{3,7},{5,1},{7,3},{8,12},{10,14},{12... | collective-permute-start | bytes 159752 | tf_op jit(solution)/shard_map/ppermute | solution.py:281
  87.4 5.0 %collective-permute-start.33 = (bf16[208,128]{1,0:T(8,128)(2,1)S(1)}, bf16[208,128]{1,0:T(8,128)(2,1)S(1)}, u32[]{:S(2)}, u32[]{:S(2)}) collective-permute-start(bf16[208,128]{1,0:T(8,128)(2,1)S(1)} %get-tuple-element.139.refs_0_), channel_id=1, source_target_pairs={{0,6},{2,4},{4,2},{6,0},{1,7},{3,5},{5,3},{7,1},{8,14},{10,12},{12... | collective-permute-start | bytes 159752 | tf_op jit(solution)/shard_map/ppermute | solution.py:281
  88.7 4.6 %collective-permute-start.29 = (bf16[208,128]{1,0:T(8,128)(2,1)S(1)}, bf16[208,128]{1,0:T(8,128)(2,1)S(1)}, u32[]{:S(2)}, u32[]{:S(2)}) collective-permute-start(bf16[208,128]{1,0:T(8,128)(2,1)S(1)} %get-tuple-element.139.refs_0_), channel_id=1, source_target_pairs={{0,2},{2,0},{4,6},{6,4},{1,3},{3,1},{5,7},{7,5},{8,10},{10,8},{12,... | collective-permute-start | bytes 159752 | tf_op jit(solution)/shard_map/ppermute | solution.py:281
  89.5 4.5 %collective-permute-start.28 = (bf16[208,128]{1,0:T(8,128)(2,1)S(1)}, bf16[208,128]{1,0:T(8,128)(2,1)S(1)}, u32[]{:S(2)}, u32[]{:S(2)}) collective-permute-start(bf16[208,128]{1,0:T(8,128)(2,1)S(1)} %get-tuple-element.139.refs_0_), channel_id=1, source_target_pairs={{0,1},{1,0},{2,3},{3,2},{4,5},{5,4},{6,7},{7,6},{8,9},{9,8},{10,11... | collective-permute-start | bytes 159752 | tf_op jit(solution)/shard_map/ppermute | solution.py:281
  91.8 2.4 %collective-permute-start.32 = (bf16[208,128]{1,0:T(8,128)(2,1)S(1)}, bf16[208,128]{1,0:T(8,128)(2,1)S(1)}, u32[]{:S(2)}, u32[]{:S(2)}) collective-permute-start(bf16[208,128]{1,0:T(8,128)(2,1)S(1)} %collective-permute-done.31.refs_2_), channel_id=1, source_target_pairs={{0,1},{1,0},{2,3},{3,2},{4,5},{5,4},{6,7},{7,6},{8,9},{9,8},{10,11... | collective-permute-start | bytes 159752 | tf_op jit(solution)/shard_map/ppermute | solution.py:281
  92.4 1.7 %collective-permute-start.34 = (bf16[208,128]{1,0:T(8,128)(2,1)S(1)}, bf16[208,128]{1,0:T(8,128)(2,1)S(1)}, u32[]{:S(2)}, u32[]{:S(2)}) collective-permute-start(bf16[208,128]{1,0:T(8,128)(2,1)S(1)} %collective-permute-done.33.refs_3_), channel_id=1, source_target_pairs={{0,1},{1,0},{2,3},{3,2},{4,5},{5,4},{6,7},{7,6},{8,9},{9,8},{10,11... | collective-permute-start | bytes 159752 | tf_op jit(solution)/shard_map/ppermute | solution.py:281
  (10 other events, 75.5 us)
